TPU v7x, 32 devices: a whole 2x2x4 slice. The times are simulated.
32 devices in a mesh: section: 2 (over core), seq: 8 (over z, x), fsdp: 2 (over y).
Axes of the slice: x: 2, y: 2, z: 4, core: 2. Of those that a mesh axis runs over, the one named last changes fastest.
Arguments:
- tokens: bfloat16 [2, 2, 4096, 768], P(None, 'fsdp', 'seq'), may hold values from -6 to 6
- cotangent: bfloat16 [2, 2, 4096, 768], P(None, 'fsdp', 'seq'), may hold values from -6 to 6
- lengths: int32 [2, 2, 4], P(None, 'fsdp'), may hold values from 1 to 3840, 4096 in all within a row
- doc_order: int32 [2, 2, 4], P(None, 'fsdp'), may hold values from 0 to 3, each once within a row
- norm_gain: float32 [2, 768], P('section'), may hold values from 0.1 to 1.9
- w_in: bfloat16 [2, 768, 3352], P('section', 'fsdp'), may hold values from -0.21875 to 0.21875
- conv_w: float32 [2, 4, 1792], P('section'), may hold values from -3 to 3
- conv_b: float32 [2, 1792], P('section'), may hold values from -3 to 3
- dt_bias: float32 [2, 24], P('section'), may hold values from -4 to 0
- a_log: float32 [2, 24], P('section'), may hold values from -8 to 1
- skip_scale: float32 [2, 24], P('section'), may hold values from 0 to 2
- gate_gain: float32 [2, 1536], P('section'), may hold values from 0.1 to 1.9
- w_out: bfloat16 [2, 1536, 768], P('section', 'fsdp'), may hold values from -0.15625 to 0.15625
Outputs:
- activations: bfloat16 [2, 2, 2, 4096, 768], P('section', None, 'fsdp', 'seq')
- input_grads: bfloat16 [2, 2, 2, 4096, 768], P('section', None, 'fsdp', 'seq')
- grad_norm_gain: float32 [2, 768], P('section')
- grad_w_in: float32 [2, 768, 3352], P('section', 'fsdp')
- grad_conv_w: float32 [2, 4, 1792], P('section')
- grad_conv_b: float32 [2, 1792], P('section')
- grad_dt_bias: float32 [2, 24], P('section')
- grad_a_log: float32 [2, 24], P('section')
- grad_skip_scale: float32 [2, 24], P('section')
- grad_gate_gain: float32 [2, 1536], P('section')
- grad_w_out: float32 [2, 1536, 768], P('section', 'fsdp')
Inputs may be any that keep to these rules, and one draw needn't show every extreme that they name: Each row of 4 lengths sums to 4096; its largest is exactly 3840. `doc_order`: each row holds 0 to 3 once each.
All inputs are finite; a program needn't handle non-finite values.
Results may differ from a plain program's by a relative error of at most 0.022.
The roundings to bfloat16 on the way count: a program that leaves them out, or rounds other values in their place, can miss the bound.
Values may be sent and summed in bfloat16 or wider, within the bound.
No kernel may reach another device: no remote copies, remote signals or barrier semaphores. Data moves between devices by JAX's collectives and lax.ppermute only.
A program may use at most 320 MiB of HBM per device.

v0:
```python
from functools import partial

import jax
import jax.numpy as jnp
from jax import lax
from jax.sharding import PartitionSpec as P

DI = 1536
H = 24
P_SIZE = 64
STATE = 128
CONV = 4
GROUP = 256
CONVCH = 1792


epsilon = 1e-05
highest = lax.Precision.HIGHEST


def passed_along(block, axis, distance):
    devices = range(lax.axis_size(axis))
    route = [(i - distance, i) for i in devices if i - distance in devices]
    return lax.ppermute(block, axis, route)


def carried_in(value, axis, combine, identity):
    size, here = (lax.axis_size(axis), lax.axis_index(axis))
    everything = jax.tree.map(lambda part: lax.all_gather(part, axis), value)
    start = jax.tree.map(
        lambda part, zero: jnp.broadcast_to(jnp.asarray(zero, part.dtype), part.shape),
        value,
        identity,
    )

    def carried_lap(k, before):
        reached = k < here
        new = combine(before, jax.tree.map(lambda part: part[k], everything))
        return jax.tree.map(lambda a, b: jnp.where(reached, a, b), new, before)

    return lax.fori_loop(0, size, carried_lap, start)


def prefix_2(value, axis, combine, identity):
    size, here = (lax.axis_size(axis), lax.axis_index(axis))
    everything = jax.tree.map(
        lambda part, kind: lax.all_gather(part.astype(kind), axis),
        value,
        jax.tree.map(lambda a: jnp.bfloat16 if a.dtype == jnp.float32 else a.dtype, value),
    )
    start = jax.tree.map(
        lambda part, zero: jnp.broadcast_to(jnp.asarray(zero, part.dtype), part.shape),
        value,
        identity,
    )

    def prefix_lap(k, before):
        at = size - 1 - k
        reached = at > here
        new = combine(
            before, jax.tree.map(lambda part, own: part[at].astype(own.dtype), everything, value)
        )
        return jax.tree.map(lambda a, b: jnp.where(reached, a, b), new, before)

    return lax.fori_loop(0, size, prefix_lap, start)


def segment_ids(doc_lengths, doc_order, positions):
    labels = jnp.arange(doc_lengths.shape[0], dtype=jnp.int32)
    picked = (doc_order[:, None] == labels[None, :]).astype(jnp.int32)
    ordered = jnp.sum(picked * doc_lengths[None, :], axis=1)
    bounds = jnp.cumsum(ordered)
    return jnp.sum((positions[:, None] >= bounds[None, :]).astype(jnp.int32), axis=1)


def rms_scale(values, gain_vector):
    return (
        values
        * lax.rsqrt(jnp.mean(values * values, axis=-1, keepdims=True) + epsilon)
        * gain_vector
    )


def convolve(padded, padded_labels, conv_weight, conv_bias):
    row_count = padded.shape[0] - CONV + 1
    summed = jnp.zeros((row_count, padded.shape[1]), jnp.float32) + conv_bias[None, :]
    for offset in range(CONV):
        same_doc = (padded_labels[offset : offset + row_count] == padded_labels[CONV - 1 :]).astype(
            jnp.float32
        )
        summed = (
            summed
            + conv_weight[offset][None, :] * padded[offset : offset + row_count] * same_doc[:, None]
        )
    return jax.nn.silu(summed)


def conv_section(padded, raw_steps, conv_weight, conv_bias, step_bias, log_rates, padded_labels):
    mixed_rows = convolve(padded, padded_labels, conv_weight, conv_bias)
    step_sizes = jax.nn.softplus(raw_steps + step_bias[None, :])
    return (mixed_rows, step_sizes, -jnp.exp(log_rates))


def group_terms(values, b_rows, c_rows, step_sizes, decay_rates, labels, before):
    cumulated = jnp.cumsum(step_sizes * decay_rates[None, :], axis=0).T
    previous = jnp.concatenate([before[None], labels[:-1]])
    starts = (labels != previous).astype(jnp.int32)
    opened = (jnp.cumsum(starts) == 0).astype(jnp.float32)
    places = jnp.arange(labels.shape[0], dtype=jnp.int32)
    inside = ((places[:, None] >= places[None, :]) & (labels[:, None] == labels[None, :])).astype(
        jnp.float32
    )
    log_gaps = jnp.where(inside[None] > 0, cumulated[:, :, None] - cumulated[:, None, :], 0.0)
    kernel = jnp.exp(log_gaps) * inside[None]
    scores = jnp.dot(c_rows, b_rows.T, precision=highest)
    mixing = kernel * scores[None] * step_sizes.T[:, None, :]
    intra_out = jnp.einsum("hts,shp->thp", mixing, values, precision=highest)
    same_end = (labels == labels[-1]).astype(jnp.float32)
    weights = jnp.exp(cumulated[:, -1:] - cumulated) * step_sizes.T * same_end[None, :]
    scaled = values * weights.T[:, :, None]
    group_state = jnp.einsum("shp,sn->hpn", scaled, b_rows, precision=highest)
    group_decay = jnp.exp(cumulated[:, -1]) * opened[-1]
    reach_rows = jnp.exp(cumulated).T * opened[:, None]
    return (intra_out, group_state, group_decay, reach_rows)


def group_prepare(values, b_rows, c_rows, step_sizes, decay_rates, labels, before):
    blocks = values.shape[0] // GROUP
    label_blocks = labels.reshape(blocks, GROUP)
    befores = jnp.concatenate([before[None], label_blocks[:-1, -1]])
    mapped = jax.vmap(group_terms, in_axes=(0, 0, 0, 0, None, 0, 0))
    return mapped(
        values.reshape(blocks, GROUP, H, P_SIZE),
        b_rows.reshape(blocks, GROUP, STATE),
        c_rows.reshape(blocks, GROUP, STATE),
        step_sizes.reshape(blocks, GROUP, H),
        decay_rates,
        label_blocks,
        befores,
    )


def device_summary(prepared):
    intra_out, states, decays, reach_rows = prepared
    total_decay = jnp.ones_like(decays[0])
    total_state = jnp.zeros_like(states[0])
    for block_index in range(decays.shape[0]):
        total_state = decays[block_index][:, None, None] * total_state + states[block_index]
        total_decay = total_decay * decays[block_index]
    return (total_decay, total_state)


def mixer_output(prepared, incoming, values, c_rows, skip_scale, gate_part, gate_gain):
    intra_out, states, decays, reach_rows = prepared
    carry_state = incoming
    pieces = []
    for block_index in range(intra_out.shape[0]):
        c_block = c_rows[block_index * GROUP : (block_index + 1) * GROUP]
        outside = jnp.einsum(
            "tn,th,hpn->thp", c_block, reach_rows[block_index], carry_state, precision=highest
        )
        pieces.append(intra_out[block_index] + outside)
        carry_state = decays[block_index][:, None, None] * carry_state + states[block_index]
    scanned = jnp.concatenate(pieces) + skip_scale[None, :, None] * values
    gated_rows = scanned.reshape(values.shape[0], -1) * jax.nn.silu(gate_part)
    return rms_scale(gated_rows, gate_gain)


def combine(earlier, later):
    return (earlier[0] * later[0], later[0][:, None, None] * earlier[1] + later[1])


def local(
    tokens,
    cotangent,
    lengths,
    doc_order,
    norm_gain,
    w_in,
    conv_w,
    conv_b,
    dt_bias,
    a_log,
    skip_scale,
    gate_gain,
    w_out,
):
    micro_count = tokens.shape[0]
    rows_here = tokens.shape[2]
    model_width = tokens.shape[3]
    section_zero = lax.axis_index("section") == 0
    seq_index = lax.axis_index("seq")
    gathered_in, gathered_out = (
        lax.all_gather(w_in, "fsdp", axis=1, tiled=True),
        lax.all_gather(w_out, "fsdp", axis=1, tiled=True),
    )
    full_in = gathered_in[0]
    full_out = gathered_out[0]
    layer_gain = norm_gain[0]
    conv_weight = conv_w[0]
    conv_bias = conv_b[0]
    step_bias = dt_bias[0]
    log_rates = a_log[0]
    skip_vector = skip_scale[0]
    gate_vector = gate_gain[0]
    identity = (jnp.ones((H,), jnp.float32), jnp.zeros((H, P_SIZE, STATE), jnp.float32))
    places = seq_index * rows_here - (CONV - 1) + jnp.arange(rows_here + CONV - 1, dtype=jnp.int32)
    kept_state = []
    outputs = []
    received = jnp.zeros((rows_here, model_width), jnp.bfloat16)
    for tick_index in range(micro_count + 1):
        first_micro = min(tick_index, micro_count - 1)
        second_micro = max(tick_index - 1, 0)
        hidden = jnp.where(section_zero, tokens[first_micro, 0], received).astype(jnp.float32)
        stream_lengths = jnp.where(section_zero, lengths[first_micro, 0], lengths[second_micro, 0])
        stream_order = jnp.where(
            section_zero, doc_order[first_micro, 0], doc_order[second_micro, 0]
        )
        padded_labels = segment_ids(stream_lengths, stream_order, places)
        labels = padded_labels[CONV - 1 :]
        before = jnp.where(seq_index == 0, -1, padded_labels[CONV - 2])
        normed, norm_back = jax.vjp(rms_scale, hidden, layer_gain)
        normed_low = normed.astype(jnp.bfloat16)
        projected = jnp.dot(normed_low, full_in, preferred_element_type=jnp.float32)
        gate_part = projected[:, :DI]
        conv_input = projected[:, DI : DI + CONVCH].astype(jnp.bfloat16)
        halo_rows = passed_along(conv_input[rows_here - (CONV - 1) :], "seq", 1)
        padded = jnp.concatenate([halo_rows, conv_input]).astype(jnp.float32)
        conv_outputs, conv_back = jax.vjp(
            partial(conv_section, padded_labels=padded_labels),
            padded,
            projected[:, DI + CONVCH :],
            conv_weight,
            conv_bias,
            step_bias,
            log_rates,
        )
        mixed_rows = conv_outputs[0]
        values = mixed_rows[:, :DI].reshape(rows_here, H, P_SIZE)
        b_rows = mixed_rows[:, DI : DI + STATE]
        c_rows = mixed_rows[:, DI + STATE :]
        prepared, prepare_back = jax.vjp(
            partial(group_prepare, labels=labels, before=before),
            values,
            b_rows,
            c_rows,
            conv_outputs[1],
            conv_outputs[2],
        )
        summary, summary_back = jax.vjp(device_summary, prepared)
        prefix = carried_in((summary[0], summary[1]), "seq", combine, identity)
        incoming = prefix[1]
        gated_norm, output_back = jax.vjp(
            mixer_output, prepared, incoming, values, c_rows, skip_vector, gate_part, gate_vector
        )
        gated_low = gated_norm.astype(jnp.bfloat16)
        branch = jnp.dot(gated_low, full_out, preferred_element_type=jnp.float32)
        result = (hidden + branch).astype(jnp.bfloat16)
        received = passed_along(result, "section", 1)
        outputs.append(result)
        kept_state.append(
            (
                norm_back,
                normed_low,
                conv_back,
                prepare_back,
                summary_back,
                output_back,
                gated_low,
                summary[0],
                incoming,
            )
        )
    grad_in = jnp.zeros(full_in.shape, jnp.float32)
    grad_out = jnp.zeros(full_out.shape, jnp.float32)
    sum_norm = jnp.zeros_like(layer_gain)
    sum_conv_w = jnp.zeros_like(conv_weight)
    sum_conv_b = jnp.zeros_like(conv_bias)
    sum_step = jnp.zeros_like(step_bias)
    sum_rates = jnp.zeros_like(log_rates)
    sum_skip = jnp.zeros_like(skip_vector)
    sum_gate = jnp.zeros_like(gate_vector)
    back_received = jnp.zeros((rows_here, model_width), jnp.bfloat16)
    input_list = []
    for tick_index in range(micro_count + 1):
        (
            norm_back,
            normed_low,
            conv_back,
            prepare_back,
            summary_back,
            output_back,
            gated_low,
            device_decay,
            incoming,
        ) = kept_state[micro_count - tick_index]
        if tick_index < micro_count:
            given_grad = cotangent[micro_count - 1 - tick_index, 0]
        else:
            given_grad = jnp.zeros_like(back_received)
        upstream = jnp.where(section_zero, back_received, given_grad)
        grad_out = grad_out + jnp.dot(gated_low.T, upstream, preferred_element_type=jnp.float32)
        grad_gated = jnp.dot(upstream, full_out.T, preferred_element_type=jnp.float32)
        back_prep, back_incoming, back_values, back_c_rows, back_skip, back_gate, back_gate_gain = (
            output_back(grad_gated)
        )
        suffix = prefix_2((device_decay, back_incoming), "seq", combine, identity)
        outgoing = suffix[1]
        back_decay = jnp.sum(outgoing * incoming, axis=(1, 2))
        summary_grads = summary_back((back_decay, outgoing))
        total_prep = jax.tree.map(jnp.add, back_prep, summary_grads[0])
        grad_values, grad_b_rows, grad_c_rows, grad_steps, grad_rates = prepare_back(total_prep)
        grad_mixed = jnp.concatenate(
            [
                (grad_values + back_values).reshape(rows_here, DI),
                grad_b_rows,
                grad_c_rows + back_c_rows,
            ],
            axis=1,
        )
        grad_padded, grad_raw_steps, grad_conv_w, grad_conv_b, grad_step_bias, grad_log_rates = (
            conv_back((grad_mixed, grad_steps, grad_rates))
        )
        returned = passed_along(grad_padded[: CONV - 1], "seq", -1)
        grad_conv_in = grad_padded[CONV - 1 :] + jnp.concatenate(
            [jnp.zeros((rows_here - (CONV - 1), CONVCH), jnp.float32), returned]
        )
        grad_projected = jnp.concatenate([back_gate, grad_conv_in, grad_raw_steps], axis=1).astype(
            jnp.bfloat16
        )
        grad_in = grad_in + jnp.dot(
            normed_low.T, grad_projected, preferred_element_type=jnp.float32
        )
        grad_normed = jnp.dot(grad_projected, full_in.T, preferred_element_type=jnp.float32)
        grad_hidden, grad_norm_gain = norm_back(grad_normed)
        sent_grad = (upstream.astype(jnp.float32) + grad_hidden).astype(jnp.bfloat16)
        back_received = passed_along(sent_grad, "section", -1)
        input_list.append(sent_grad)
        sum_norm = sum_norm + grad_norm_gain
        sum_conv_w = sum_conv_w + grad_conv_w
        sum_conv_b = sum_conv_b + grad_conv_b
        sum_step = sum_step + grad_step_bias
        sum_rates = sum_rates + grad_log_rates
        sum_skip = sum_skip + back_skip
        sum_gate = sum_gate + back_gate_gain
    quarter = (
        lax.psum_scatter(
            grad_in.astype(jnp.bfloat16), "fsdp", scatter_dimension=0, tiled=True
        ).astype(jnp.float32),
        lax.psum_scatter(
            grad_out.astype(jnp.bfloat16), "fsdp", scatter_dimension=0, tiled=True
        ).astype(jnp.float32),
    )
    shard_in, shard_out = (
        lax.psum(quarter[0].astype(jnp.bfloat16), "seq").astype(jnp.float32),
        lax.psum(quarter[1].astype(jnp.bfloat16), "seq").astype(jnp.float32),
    )
    small = lax.psum(
        (sum_norm, sum_conv_w, sum_conv_b, sum_step, sum_rates, sum_skip, sum_gate), ("seq", "fsdp")
    )
    section_acts = [
        jnp.where(section_zero, outputs[micro_index], outputs[micro_index + 1])
        for micro_index in range(micro_count)
    ]
    section_grads = [
        jnp.where(
            section_zero,
            input_list[micro_count - micro_index],
            input_list[micro_count - 1 - micro_index],
        )
        for micro_index in range(micro_count)
    ]
    activations = jnp.stack(section_acts)[None, :, None]
    input_grads = jnp.stack(section_grads)[None, :, None]
    return (
        activations,
        input_grads,
        small[0][None],
        shard_in[None],
        small[1][None],
        small[2][None],
        small[3][None],
        small[4][None],
        small[5][None],
        small[6][None],
        shard_out[None],
    )


def solution(mesh):
    in_specs = (
        P(None, "fsdp", "seq", None),
        P(None, "fsdp", "seq", None),
        P(None, "fsdp", None),
        P(None, "fsdp", None),
        P("section", None),
        P("section", "fsdp", None),
        P("section", None, None),
        P("section", None),
        P("section", None),
        P("section", None),
        P("section", None),
        P("section", None),
        P("section", "fsdp", None),
    )
    out_specs = (
        P("section", None, "fsdp", "seq", None),
        P("section", None, "fsdp", "seq", None),
        P("section", None),
        P("section", "fsdp", None),
        P("section", None, None),
        P("section", None),
        P("section", None),
        P("section", None),
        P("section", None),
        P("section", None),
        P("section", "fsdp", None),
    )
    return jax.shard_map(local, mesh=mesh, in_specs=in_specs, out_specs=out_specs, check_vma=False)
```

profile of v0, /device:TPU:0, one launch (start us, length us, event | category | flops | bytes accessed | tf_op | source)
XLA Modules:
  0.0 1425.1 jit_solution(18372099170479699670)
XLA Ops:
  18.9 61.0 %all-gather.18.cloned.1.call-done = bf16[1,768,3352]{1,2,0:T(8,128)(2,1)} async-done(((bf16[1,384,3352]{1,2,0:T(8,128)(2,1)}), bf16[1,768,3352]{1,2,0:T(8,128)(2,1)}) %all-gather.18.cloned.1.call-update) | async-done | bytes 5148688 | tf_op jit(solution)/shard_map/all_gather | solution.py:194
  127.7 22.3 %all-gather.3 = f32[8,1,24]{2,1,0:T(1,128)S(1)} all-gather(f32[1,1,24]{2,1,0:T(1,128)} %get-tuple-element.1111), channel_id=1, replica_groups=mesh['section'=2,'seq'=8,'fsdp'=2] {'seq'}, dimensions={0}, use_global_device_ids=true | all-gather | bytes 864 | tf_op jit(solution)/shard_map/all_gather | solution.py:29
  153.0 17.2 %fusion.161 = f32[2,256,24,64]{1,3,2,0:T(8,128)} fusion(f32[2,24,256]{2,1,0:T(8,128)S(1)} %bitcast.1197, f32[2,256,256]{2,1,0:T(8,128)S(1)} %fusion.510, f32[2,256,256]{2,1,0:T(8,128)S(1)} %get-tuple-element.1074, f32[2,24,256]{2,1,0:T(8,128)S(1)} %copy_bitcast_fusion.2, pred[2,256,256]{2,1,0:T(8,128)(4,1)S(1)} %get-tuple-element.1075, ...), kind=kOutput, calls=%fused_computation.280 | convolution fusion | flops 2431647744 | bytes 7569408 | tf_op jit(solution)/shard_map/jvp(vmap(hts,shp->thp))/dot_general | solution.py:117
  170.2 51.3 %all-gather.20.cloned.1.call-done = f32[8,24,64,128]{3,2,1,0:T(8,128)} async-done(((f32[1,24,64,128]{3,2,1,0:T(8,128)}), f32[8,24,64,128]{3,2,1,0:T(8,128)}) %all-gather.20.cloned.1.call-update) | async-done | bytes 6291472 | tf_op jit(solution)/shard_map/all_gather | solution.py:29
  221.5 11.1 while.90
  243.6 13.8 all-gather.22.cloned.1.call-done
  291.4 6.0 fusion.97
  315.1 20.7 %all-gather.4 = f32[8,1,24]{2,1,0:T(1,128)S(1)} all-gather(f32[1,1,24]{2,1,0:T(1,128)} %get-tuple-element.1115), channel_id=1, replica_groups=mesh['section'=2,'seq'=8,'fsdp'=2] {'seq'}, dimensions={0}, use_global_device_ids=true | all-gather | bytes 864 | tf_op jit(solution)/shard_map/all_gather | solution.py:29
  338.7 17.4 %fusion.166 = f32[2,256,24,64]{1,3,2,0:T(8,128)} fusion(f32[2,24,256]{2,1,0:T(8,128)S(1)} %bitcast.1200, f32[2,256,256]{2,1,0:T(8,128)S(1)} %fusion.511, f32[2,256,256]{2,1,0:T(8,128)} %get-tuple-element.1072, f32[2,24,256]{2,1,0:T(8,128)} %copy-done.202, pred[2,256,256]{2,1,0:T(8,128)(4,1)} %get-tuple-element.1073, f32[2,256,24,64]{1,0,3,2:T(2,128)} %copy-done.18), kind=kOutput, calls=%fused_computation.281 | convolution fusion | flops 2431647744 | bytes 7569408 | tf_op jit(solution)/shard_map/jvp(vmap(hts,shp->thp))/dot_general | solution.py:117
  356.2 54.4 %all-gather.24.cloned.1.call-done = f32[8,24,64,128]{3,2,1,0:T(8,128)} async-done(((f32[1,24,64,128]{3,2,1,0:T(8,128)}), f32[8,24,64,128]{3,2,1,0:T(8,128)}) %all-gather.24.cloned.1.call-update) | async-done | bytes 6291472 | tf_op jit(solution)/shard_map/all_gather | solution.py:29
  410.6 10.8 while.91
  481.5 20.8 %all-gather.5 = f32[8,1,24]{2,1,0:T(1,128)S(1)} all-gather(f32[1,1,24]{2,1,0:T(1,128)} %get-tuple-element.1119), channel_id=1, replica_groups=mesh['section'=2,'seq'=8,'fsdp'=2] {'seq'}, dimensions={0}, use_global_device_ids=true | all-gather | bytes 864 | tf_op jit(solution)/shard_map/all_gather | solution.py:29
  506.0 17.4 %fusion.171 = f32[2,256,24,64]{1,3,2,0:T(8,128)} fusion(f32[2,24,256]{2,1,0:T(8,128)S(1)} %bitcast.1203, f32[2,256,256]{2,1,0:T(8,128)S(1)} %fusion.512, f32[2,256,256]{2,1,0:T(8,128)} %get-tuple-element.1067, f32[2,24,256]{2,1,0:T(8,128)} %copy-done.204, pred[2,256,256]{2,1,0:T(8,128)(4,1)} %get-tuple-element.1066, f32[2,256,24,64]{1,0,3,2:T(2,128)} %copy-done.20), kind=kOutput, calls=%fused_computation.282 | convolution fusion | flops 2431647744 | bytes 7569408 | tf_op jit(solution)/shard_map/jvp(vmap(hts,shp->thp))/dot_general | solution.py:117
  523.4 58.7 %all-gather.26.cloned.1.call-done = f32[8,24,64,128]{3,2,1,0:T(8,128)} async-done(((f32[1,24,64,128]{3,2,1,0:T(8,128)}), f32[8,24,64,128]{3,2,1,0:T(8,128)}) %all-gather.26.cloned.1.call-update) | async-done | bytes 6291472 | tf_op jit(solution)/shard_map/all_gather | solution.py:29
  582.1 10.9 while.92
  605.2 6.0 multiply_reduce_fusion.23
  617.7 17.9 %all-gather.6 = bf16[8,1,24]{2,1,0:T(2,128)(2,1)S(1)} all-gather(bf16[1,1,24]{2,1,0:T(2,128)(2,1)} %get-tuple-element.1117), channel_id=1, replica_groups=mesh['section'=2,'seq'=8,'fsdp'=2] {'seq'}, dimensions={0}, use_global_device_ids=true | all-gather | bytes 432 | tf_op jit(solution)/shard_map/all_gather | solution.py:47
  636.2 23.4 %fusion.28 = (f32[2,24,256]{2,1,0:T(8,128)}, f32[2,24,256]{2,1,0:T(8,128)}, f32[2,24,256]{2,1,0:T(8,128)}, f32[2,256,256]{2,1,0:T(8,128)S(1)}) fusion(f32[2,24,256]{2,1,0:T(8,128)} %bitcast.1204, f32[2,256,256]{2,1,0:T(8,128)} %copy-done.155, f32[2,256,256]{2,1,0:T(8,128)} %get-tuple-element.1067, f32[2,24,256]{2,1,0:T(8,128)} %copy-done.204, ...), kind=kOutput, calls=%fused_computation.47 | convolution fusion | flops 2463723520 | bytes 8241152 | tf_op jit(solution)/shard_map/transpose(jvp(vmap(hts,shp->thp)))/dot_general | solution.py:117
  676.4 19.3 %while.93 = (s32[]{:T(128)}, f32[24,64,128]{2,1,0:T(8,128)S(1)}, s32[]{:T(128)}, bf16[8,24]{1,0:T(8,128)(2,1)}, bf16[8,24,64,128]{3,2,1,0:T(8,128)(2,1)}, /*index=5*/s32[]{:T(128)}, s32[]{:T(128)}, s32[]{:T(128)}, s32[]{:T(128)}) while((s32[]{:T(128)}, f32[24,64,128]{2,1,0:T(8,128)S(1)}, s32[]{:T(128)}, ...), condition=%wide.region_35.37_spmd.clone, body=%wide.region_34.36_spmd.clone.sunk | while | flops 983072 | bytes 1966495 | solution.py:65
  709.9 13.9 bitcast_add_fusion.5
  730.9 7.3 multiply_reduce_fusion.17
  743.7 7.8 pad_add_fusion.2
  770.6 7.1 fusion.195
  786.1 6.0 multiply_reduce_fusion.22
  799.6 17.6 %all-gather.7 = bf16[8,1,24]{2,1,0:T(2,128)(2,1)S(1)} all-gather(bf16[1,1,24]{2,1,0:T(2,128)(2,1)S(1)} %copy-done.353), channel_id=1, replica_groups=mesh['section'=2,'seq'=8,'fsdp'=2] {'seq'}, dimensions={0}, use_global_device_ids=true | all-gather | bytes 432 | tf_op jit(solution)/shard_map/all_gather | solution.py:47
  817.8 23.3 %fusion.30 = (f32[2,24,256]{2,1,0:T(8,128)}, f32[2,24,256]{2,1,0:T(8,128)}, f32[2,24,256]{2,1,0:T(8,128)}, f32[2,256,256]{2,1,0:T(8,128)S(1)}) fusion(f32[2,24,256]{2,1,0:T(8,128)} %bitcast.1201, f32[2,256,256]{2,1,0:T(8,128)} %copy-done.153, f32[2,256,256]{2,1,0:T(8,128)} %get-tuple-element.1072, f32[2,24,256]{2,1,0:T(8,128)S(1)} %copy-done.203, ...), kind=kOutput, calls=%fused_computation.49 | convolution fusion | flops 2463723520 | bytes 8241152 | tf_op jit(solution)/shard_map/transpose(jvp(vmap(hts,shp->thp)))/dot_general | solution.py:117
  850.8 8.9 all-gather.30.cloned.1.call-done
  859.7 15.3 %while.94 = (s32[]{:T(128)}, f32[24,64,128]{2,1,0:T(8,128)S(1)}, s32[]{:T(128)}, bf16[8,24]{1,0:T(8,128)(2,1)}, bf16[8,24,64,128]{3,2,1,0:T(8,128)(2,1)}, /*index=5*/s32[]{:T(128)}, s32[]{:T(128)}, s32[]{:T(128)}, s32[]{:T(128)}) while((s32[]{:T(128)}, f32[24,64,128]{2,1,0:T(8,128)S(1)}, s32[]{:T(128)}, ...), condition=%wide.region_51.53_spmd.clone, body=%wide.region_50.52_spmd.clone.sunk | while | flops 983072 | bytes 1966495 | solution.py:65
  888.7 13.7 bitcast_add_fusion.4
  909.4 7.3 multiply_reduce_fusion.13
  922.5 7.8 pad_add_fusion.1
  949.4 7.1 fusion.197
  965.2 6.0 multiply_reduce_fusion.21
  978.7 17.6 %all-gather.8 = bf16[8,1,24]{2,1,0:T(2,128)(2,1)S(1)} all-gather(bf16[1,1,24]{2,1,0:T(2,128)(2,1)S(1)} %copy-done.352), channel_id=1, replica_groups=mesh['section'=2,'seq'=8,'fsdp'=2] {'seq'}, dimensions={0}, use_global_device_ids=true | all-gather | bytes 432 | tf_op jit(solution)/shard_map/all_gather | solution.py:47
  996.9 9.0 fusion.281
  1006.0 10.2 fusion.280
  1016.3 22.7 %fusion.32 = (f32[2,24,256]{2,1,0:T(8,128)}, f32[2,24,256]{2,1,0:T(8,128)}, f32[2,24,256]{2,1,0:T(8,128)}, f32[2,256,256]{2,1,0:T(8,128)S(1)}) fusion(f32[2,24,256]{2,1,0:T(8,128)S(1)} %bitcast.1199, f32[2,256,256]{2,1,0:T(8,128)S(1)} %copy-done.151, f32[2,256,256]{2,1,0:T(8,128)S(1)} %copy-done.158, f32[2,24,256]{2,1,0:T(8,128)S(1)} %copy-done.201, ...), kind=kOutput, calls=%fused_computation.51 | convolution fusion | flops 2463723520 | bytes 8241152 | tf_op jit(solution)/shard_map/transpose(jvp(vmap(hts,shp->thp)))/dot_general | solution.py:117
  1048.6 15.5 %while.95 = (s32[]{:T(128)}, f32[24,64,128]{2,1,0:T(8,128)S(1)}, s32[]{:T(128)}, bf16[8,24]{1,0:T(8,128)(2,1)}, bf16[8,24,64,128]{3,2,1,0:T(8,128)(2,1)}, /*index=5*/s32[]{:T(128)}, s32[]{:T(128)}, s32[]{:T(128)}, s32[]{:T(128)}) while((s32[]{:T(128)}, f32[24,64,128]{2,1,0:T(8,128)S(1)}, s32[]{:T(128)}, ...), condition=%wide.region_67.69_spmd.clone, body=%wide.region_66.68_spmd.clone.sunk | while | flops 983072 | bytes 1966495 | solution.py:65
  1077.8 13.6 bitcast_add_fusion.3
  1098.4 7.3 multiply_reduce_fusion.9
  1111.4 7.8 pad_add_fusion
  1139.4 11.5 add_convert_fusion
  1150.9 7.9 copy.631
  1171.6 51.9 %reduce-scatter.7.cloned.1.call-done = bf16[384,3352]{1,0:T(8,128)(2,1)} async-done(((bf16[768,3352]{1,0:T(8,128)(2,1)}), bf16[384,3352]{1,0:T(8,128)(2,1)}) %reduce-scatter.7.cloned.1.call-update) | async-done | bytes 2574352
  1227.9 33.0 %reduce-scatter.5.cloned.1.call-done = bf16[768,768]{1,0:T(8,128)(2,1)} async-done(((bf16[1536,768]{1,0:T(8,128)(2,1)}), bf16[768,768]{1,0:T(8,128)(2,1)}) %reduce-scatter.5.cloned.1.call-update) | async-done | bytes 1179664 | tf_op jit(solution)/shard_map/reduce_scatter | solution.py:350
  1276.6 7.4 fusion.198
  1284.0 78.9 %all-reduce.75 = (f32[1,768]{1,0:T(1,128)}, f32[1,4,1792]{2,1,0:T(4,128)}, f32[1,1792]{1,0:T(1,128)}, f32[1,24]{1,0:T(1,128)}, f32[1,24]{1,0:T(1,128)}, /*index=5*/f32[1,24]{1,0:T(1,128)}, f32[1,1536]{1,0:T(1,128)}) all-reduce(f32[1,768]{1,0:T(1,128)S(1)} %broadcast_in_dim.355, ...), channel_id=1, replica_groups=mesh['section'=2,'seq'=8,'fsdp'=2] {'seq','fsdp'}, use_global_device_ids=true, to_apply=%region_84.86 | all-reduce | flops 11336 | bytes 90688 | tf_op jit(solution)/shard_map/psum | solution.py:358
  1366.6 45.5 %all-reduce.79.cloned.1.call-done = (bf16[1,384,3352]{1,2,0:T(8,128)(2,1)}, bf16[1,768,768]{2,1,0:T(8,128)(2,1)}) async-done(((bf16[1,384,3352]{1,2,0:T(8,128)(2,1)}, bf16[1,768,768]{2,1,0:T(8,128)(2,1)}), (bf16[1,384,3352]{1,2,0:T(8,128)(2,1)}, bf16[1,768,768]{2,1,0:T(8,128)(2,1)})) %all-reduce.79.cloned.1.call-update) | async-done | bytes 3754000 | tf_op jit(solution)/shard_map/psum | solution.py:355
  (1233 shorter events, 535.4 us)
Async XLA Ops:
  7.2 72.6 %all-gather.18.cloned.1.call-start = ((), (), s32[]{:S(2)}) async-start(), calls=%async_computation.2 | async-start | bytes 7723008 | tf_op jit(solution)/shard_map/all_gather | solution.py:194
  7.9 213.6 %all-gather.20.cloned.1.call-start = ((), (), s32[]{:S(2)}) async-start(), calls=%async_computation.3 | async-start | bytes 7077888 | tf_op jit(solution)/shard_map/all_gather | solution.py:29
  11.1 111.6 %copy-start.232 = (s32[515]{0:T(1024)}, s32[515]{0:T(1024)S(1)}, u32[]{:S(2)}) copy-start(s32[515]{0:T(1024)S(1)} %get-tuple-element.925) | copy-start | bytes 6184
  13.2 86.1 %copy-start.193 = (f32[1792]{0:T(1024)}, f32[1792]{0:T(1024)S(1)}, u32[]{:S(2)}) copy-start(f32[1792]{0:T(1024)S(1)} %reduce.12) | copy-start | bytes 21508
  16.5 74.8 %copy-start.282 = (f32[1,2,2,128]{3,1,2,0:T(2,128)}, f32[1,2,2,128]{3,1,2,0:T(2,128)S(1)}, u32[]{:S(2)}) copy-start(f32[1,2,2,128]{3,1,2,0:T(2,128)S(1)} %copy.815) | copy-start | bytes 6148
  16.6 74.7 %copy-start.348 = (f32[2,1]{0,1:T(1,128)}, f32[2,1]{0,1:T(1,128)S(1)}, u32[]{:S(2)}) copy-start(f32[2,1]{0,1:T(1,128)S(1)} %copy.639) | copy-start | bytes 28
  17.8 81.5 %copy-start.164 = (f32[1792]{0:T(1024)}, f32[1792]{0:T(1024)S(1)}, u32[]{:S(2)}) copy-start(f32[1792]{0:T(1024)S(1)} %get-tuple-element.921) | copy-start | bytes 21508
  17.8 81.5 %copy-start.167 = (f32[1792]{0:T(1024)}, f32[1792]{0:T(1024)S(1)}, u32[]{:S(2)}) copy-start(f32[1792]{0:T(1024)S(1)} %get-tuple-element.922) | copy-start | bytes 21508
  17.8 81.5 %copy-start.170 = (f32[1792]{0:T(1024)}, f32[1792]{0:T(1024)S(1)}, u32[]{:S(2)}) copy-start(f32[1792]{0:T(1024)S(1)} %get-tuple-element.923) | copy-start | bytes 21508
  17.8 81.5 %copy-start.173 = (f32[1792]{0:T(1024)}, f32[1792]{0:T(1024)S(1)}, u32[]{:S(2)}) copy-start(f32[1792]{0:T(1024)S(1)} %get-tuple-element.924) | copy-start | bytes 21508
  18.1 66.7 %copy-start.299 = (f32[512]{0:T(512)}, f32[512]{0:T(512)S(1)}, u32[]{:S(2)}) copy-start(f32[512]{0:T(512)S(1)} %fusion.200) | copy-start | bytes 6148
  18.7 66.2 %copy-start.198 = (f32[512]{0:T(512)}, f32[512]{0:T(512)S(1)}, u32[]{:S(2)}) copy-start(f32[512]{0:T(512)S(1)} %fusion.449) | copy-start | bytes 6148
  18.7 72.5 %copy-start.215 = (f32[2,256]{1,0:T(2,128)}, f32[2,256]{1,0:T(2,128)S(1)}, u32[]{:S(2)}) copy-start(f32[2,256]{1,0:T(2,128)S(1)} %compare_convert_fusion.6) | copy-start | bytes 6148
  18.8 80.5 %copy-start.264 = (f32[512]{0:T(512)}, f32[512]{0:T(512)S(1)}, u32[]{:S(2)}) copy-start(f32[512]{0:T(512)S(1)} %get-tuple-element.1100) | copy-start | bytes 6148
  18.8 80.5 %copy-start.266 = (f32[512]{0:T(512)}, f32[512]{0:T(512)S(1)}, u32[]{:S(2)}) copy-start(f32[512]{0:T(512)S(1)} %get-tuple-element.1101) | copy-start | bytes 6148
  18.8 80.5 %copy-start.268 = (f32[512]{0:T(512)}, f32[512]{0:T(512)S(1)}, u32[]{:S(2)}) copy-start(f32[512]{0:T(512)S(1)} %get-tuple-element.1102) | copy-start | bytes 6148
  18.8 69.6 %copy-start.291 = (f32[1,24]{1,0:T(1,128)S(1)}, f32[1,24]{1,0:T(1,128)}, u32[]{:S(2)}) copy-start(f32[1,24]{1,0:T(1,128)} %param.34) | copy-start | bytes 292
  85.1 13.1 collective-permute-start
  91.1 61.9 %copy-start.200 = (f32[2,24,256]{2,1,0:T(8,128)}, f32[2,24,256]{2,1,0:T(8,128)S(1)}, u32[]{:S(2)}) copy-start(f32[2,24,256]{2,1,0:T(8,128)S(1)} %copy_bitcast_fusion.2) | copy-start | bytes 147460
  92.0 140.7 %copy-start.317 = (f32[24]{0:T(128)}, f32[24]{0:T(128)S(1)}, u32[]{:S(2)}) copy-start(f32[24]{0:T(128)S(1)} %get-tuple-element.1112) | copy-start | bytes 292
  121.0 136.3 %all-gather.22.cloned.1.call-start = ((), (), s32[]{:S(2)}) async-start(), calls=%async_computation.4 | async-start | bytes 3538944 | tf_op jit(solution)/shard_map/all_gather | solution.py:195
  121.8 288.8 %all-gather.24.cloned.1.call-start = ((), (), s32[]{:S(2)}) async-start(), calls=%async_computation.5 | async-start | bytes 7077888 | tf_op jit(solution)/shard_map/all_gather | solution.py:29
  123.4 46.8 %copy-start.224 = (s32[2,256]{1,0:T(2,128)}, s32[2,256]{1,0:T(2,128)S(1)}, u32[]{:S(2)}) copy-start(s32[2,256]{1,0:T(2,128)S(1)} %eq.254) | copy-start | bytes 6148
  127.7 107.6 %copy-start.179 = (f32[256,24]{0,1:T(8,128)}, f32[256,24]{0,1:T(8,128)S(1)}, u32[]{:S(2)}) copy-start(f32[256,24]{0,1:T(8,128)S(1)} %get-tuple-element.1091) | copy-start | bytes 73732
  127.7 107.6 %copy-start.181 = (f32[256,24]{0,1:T(8,128)}, f32[256,24]{0,1:T(8,128)S(1)}, u32[]{:S(2)}) copy-start(f32[256,24]{0,1:T(8,128)S(1)} %get-tuple-element.1090) | copy-start | bytes 73732
  261.7 5.1 collective-permute-start.1
  274.8 14.3 %collective-permute-start.2 = (bf16[3,1792]{0,1:T(8,128)(2,1)}, bf16[3,1792]{0,1:T(8,128)(2,1)}, u32[]{:S(2)}, u32[]{:S(2)}) collective-permute-start(bf16[3,1792]{0,1:T(8,128)(2,1)} %slice.612), channel_id=1, source_target_pairs={{0,2},{2,4},{4,6},{6,8},{8,10},{10,12},{12,14},{1,3},{3,5},{5,7},{... | collective-permute-start | bytes 32264 | tf_op jit(solution)/shard_map/ppermute | solution.py:24
  288.4 133.1 %copy-start.320 = (f32[24]{0:T(128)}, f32[24]{0:T(128)S(1)}, u32[]{:S(2)}) copy-start(f32[24]{0:T(128)S(1)} %get-tuple-element.1116) | copy-start | bytes 292
  311.6 270.4 %all-gather.26.cloned.1.call-start = ((), (), s32[]{:S(2)}) async-start(), calls=%async_computation.6 | async-start | bytes 7077888 | tf_op jit(solution)/shard_map/all_gather | solution.py:29
  335.8 88.4 %copy-start.183 = (f32[256,24]{0,1:T(8,128)}, f32[256,24]{0,1:T(8,128)S(1)}, u32[]{:S(2)}) copy-start(f32[256,24]{0,1:T(8,128)S(1)} %get-tuple-element.1087) | copy-start | bytes 73732
  335.8 88.4 %copy-start.185 = (f32[256,24]{0,1:T(8,128)}, f32[256,24]{0,1:T(8,128)S(1)}, u32[]{:S(2)}) copy-start(f32[256,24]{0,1:T(8,128)S(1)} %get-tuple-element.1086) | copy-start | bytes 73732
  434.2 4.2 collective-permute-start.3
  445.7 12.1 collective-permute-start.4
  481.4 195.1 %all-gather.28.cloned.1.call-start = ((), (), s32[]{:S(2)}) async-start(), calls=%async_computation.8 | async-start | bytes 3538944 | tf_op jit(solution)/shard_map/all_gather | solution.py:47
  503.1 92.4 %copy-start.187 = (f32[256,24]{0,1:T(8,128)}, f32[256,24]{0,1:T(8,128)S(1)}, u32[]{:S(2)}) copy-start(f32[256,24]{0,1:T(8,128)S(1)} %get-tuple-element.1083) | copy-start | bytes 73732
  503.1 92.4 %copy-start.190 = (f32[256,24]{0,1:T(8,128)}, f32[256,24]{0,1:T(8,128)S(1)}, u32[]{:S(2)}) copy-start(f32[256,24]{0,1:T(8,128)S(1)} %get-tuple-element.1082) | copy-start | bytes 73732
  617.6 242.1 %all-gather.30.cloned.1.call-start = ((), (), s32[]{:S(2)}) async-start(), calls=%async_computation.9 | async-start | bytes 3538944 | tf_op jit(solution)/shard_map/all_gather | solution.py:47
  761.0 5.8 collective-permute-start.5
  778.3 4.4 collective-permute-start.6
  799.6 249.1 %all-gather.32.cloned.1.call-start = ((), (), s32[]{:S(2)}) async-start(), calls=%async_computation.10 | async-start | bytes 3538944 | tf_op jit(solution)/shard_map/all_gather | solution.py:47
  939.8 5.8 collective-permute-start.7
  958.1 4.4 collective-permute-start.8
  978.6 244.9 %reduce-scatter.7.cloned.1.call-start = ((), (), s32[]{:S(2)}) async-start(), calls=%async_computation.11 | async-start | bytes 7962624
  1128.7 5.8 collective-permute-start.9
  1158.8 102.1 %reduce-scatter.5.cloned.1.call-start = ((), (), s32[]{:S(2)}) async-start(), calls=%async_computation.7 | async-start | bytes 3538944 | tf_op jit(solution)/shard_map/reduce_scatter | solution.py:350
  1168.7 243.4 %all-reduce.79.cloned.1.call-start = ((), (), s32[]{:S(2)}) async-start(), calls=%async_computation.12 | async-start | bytes 7507968 | tf_op jit(solution)/shard_map/psum | solution.py:355
  1276.6 86.4 %copy-start.300 = (f32[512]{0:T(512)S(1)}, f32[512]{0:T(512)}, u32[]{:S(2)}) copy-start(f32[512]{0:T(512)} %copy-done.299) | copy-start | bytes 6148
  1284.0 81.3 %copy-start.100 = (bf16[1,512,768]{2,1,0:T(8,128)(2,1)S(1)}, bf16[1,512,768]{2,1,0:T(8,128)(2,1)}, u32[]{:S(2)}) copy-start(bf16[1,512,768]{2,1,0:T(8,128)(2,1)} %get-tuple-element.1012) | copy-start | bytes 2359300
  (343 other events, 2276.6 us)
Sparse Core Ops, SparseCore 0:
  9.6 70.1 all-gather.17
  121.2 100.3 all-gather.19
  223.1 34.2 all-gather.21
  311.8 98.7 all-gather.23
  481.5 100.5 all-gather.25
  617.8 58.6 all-gather.27
  799.7 59.9 all-gather.29
  978.7 59.9 all-gather.31
  1158.9 64.5 reduce-scatter.6
  1226.1 34.7 reduce-scatter.4
  1265.7 146.3 all-reduce.78
where the time goes:
time: 1440 us; the launch traced here: 1430 us
  waiting for transfers between devices  404 us (28%)
  matrix products  346 us (24%)
  other arithmetic  317 us (22%)
  blocking collectives  196 us (14%)
  local copies, waits for them, and re-layouts  116 us (8%)
  starting transfers between devices  23.6 us (2%)
  between operations  21.1 us (1%)
    all_gather x3, waiting for transfers between devices, carried_in(): everything = jax.tree.map(lambda part: lax.all_gather(part, axis), value)  164 us
    dot_general x9, matrix products, group_terms(): intra_out = jnp.einsum('hts,shp->thp', mixing, values, precision=highest)  163 us
    psum x1, blocking collectives, local(): lax.psum((sum_norm, sum_conv_w, sum_conv_b, sum_step, sum_rates, sum_skip...  78.9 us
    all_gather x3, blocking collectives, carried_in(): everything = jax.tree.map(lambda part: lax.all_gather(part, axis), value)  63.9 us
    all_gather x1, waiting for transfers between devices, local(): lax.all_gather(w_in, 'fsdp', axis=1, tiled=True)  61 us
    unnamed x12, waiting for transfers between devices  53.4 us
    all_gather x3, blocking collectives, prefix_2(): lax.all_gather(part.astype(kind), axis)  53.1 us
    psum x1, waiting for transfers between devices, local(): lax.psum(quarter[0].astype(jnp.bfloat16), 'seq').astype(jnp.float32)  45.5 us
  transfers between devices with their start and end apart: 21, of which 16 were waited for; matrix products, arithmetic and copies ran while one was open for 21% of the time, Pallas kernels for 0%

commit v1 on v0

v1 whole, which is shorter than its diff:
```python
import jax
import jax.numpy as jnp
from jax import lax
from jax.experimental import pallas as pl
from jax.experimental.pallas import tpu as pltpu
from jax.sharding import PartitionSpec as P

D = 768
DI = 1536
H = 24
P_SIZE = 64
STATE = 128
CONV = 4
CONVCH = 1792
Q = 128
HALF = DI // 2
PACK = STATE + 16
PACK_WIDE = STATE + 8
TAP_BIAS, NORM, GAIN, STEP_BIAS, BASE_RATE, SKIP = 4, 5, 6, 7, 8, 9
TABLE = (16, CONVCH)
SWAP = ((0, 1), (1, 0))

f32 = jnp.float32
bf16 = jnp.bfloat16
epsilon = 1e-05
masked = -1e30


def nn(a, b):
    return lax.dot_general(a, b, (((1,), (0,)), ((), ())), preferred_element_type=f32)


def nt(a, b):
    return lax.dot_general(a, b, (((1,), (1,)), ((), ())), preferred_element_type=f32)


def tn(a, b):
    return nn(a.astype(f32).T.astype(bf16), b)


def split(v):
    high = v.astype(bf16)
    return high, (v - high.astype(f32)).astype(bf16)


def expand(v, spread):
    high, low = split(v)
    return nn(high, spread) + nn(low, spread)


def expand_row(v, spread):
    return expand(jnp.broadcast_to(v, (8, v.shape[1])), spread)[0:1]


def head_sum(v, spread):
    high, low = split(v)
    return nt(high, spread) + nt(low, spread)


def tri_sum(tri, v):
    high, rest = split(v)
    middle, low = split(v - high.astype(f32))
    return nn(tri, high) + nn(tri, middle) + nn(tri, low)


def iota(shape, dim):
    return lax.broadcasted_iota(jnp.int32, shape, dim)


def spread_matrix():
    return (iota((128, DI), 1) // P_SIZE == iota((128, DI), 0)).astype(bf16)


def two_heads(tile):
    left = iota(tile.shape, 1) < P_SIZE
    zero = jnp.zeros_like(tile)
    return jnp.concatenate([jnp.where(left, tile, zero), jnp.where(left, zero, tile)], axis=0)


def product(a, a_low, b, b_low):
    both = jnp.concatenate([b, b_low], axis=0)
    return nn(jnp.concatenate([a, a], axis=1), both) + nn(a_low, b)


def decay_rows(decay):
    high, low = split(decay)
    row = iota((16, decay.shape[1]), 0)
    both = jnp.where(row == 0, high.astype(f32), jnp.where(row == 1, low.astype(f32), 0.0))
    return both.astype(bf16)


def label_kernel(doc_ref, table_ref, col_ref, lab_ref):
    rows = col_ref.shape[0]
    base = doc_ref[8]
    ends = []
    end = 0
    for k in range(4):
        end = end + doc_ref[doc_ref[4 + k]]
        ends.append(end)

    def label(position):
        found = jnp.zeros(position.shape, jnp.int32)
        for bound in ends:
            found = found + (position >= bound).astype(jnp.int32)
        return jnp.where(position < 0, -1, found)

    def columns(row, lane):
        here = label(base + row)
        block = (row // Q) * Q
        other = jnp.where(
            lane < 3,
            row - 1 - lane,
            jnp.where(lane == 3, block - 1, jnp.where(lane == 4, block + Q - 1, jnp.where(lane == 5, -1, rows - 1))),
        )
        same = (label(base + other) == here).astype(f32)
        return jnp.where(lane == 7, here.astype(f32), same)

    lane = iota((rows + 16, 128), 1)
    row = iota((rows + 16, 128), 0) - 8
    whole_table = columns(jnp.clip(row, 0, rows - 1), lane)
    table_ref[...] = jnp.where((row >= 0) & (row < rows), whole_table, 0.0)
    col_ref[...] = columns(iota((rows, 128), 0), iota((rows, 128), 1))
    lab_ref[...] = label(base + iota((8, rows), 1)).astype(f32)


def head_row(par_ref, k):
    return jnp.where(iota((1, 128), 1) < H, par_ref[k : k + 1, 0:128], 0.0)


def rates(par_ref):
    return jnp.where(iota((1, 128), 1) < H, -jnp.exp(par_ref[BASE_RATE : BASE_RATE + 1, 0:128]), 0.0)


def skip_row(par_ref, spread):
    return expand_row(head_row(par_ref, SKIP), spread)


def conv_kernel(
    rc_ref, halo_ref, e_ref, col_ref, par_ref, sp_ref,
    q_ref, ds_ref, dt_ref, cum_ref, all_ref, lin_ref, pack_ref,
):
    spread = sp_ref[...]
    tri = (iota((Q, Q), 0) >= iota((Q, Q), 1)).astype(bf16)
    rate = rates(par_ref)
    bias = head_row(par_ref, STEP_BIAS)
    state = jnp.zeros((STATE, DI), f32)
    offset = jnp.zeros((1, 128), f32)
    decay = jnp.ones((1, 128), f32)
    for c in range(rc_ref.shape[0] // Q):
        rows = slice(c * Q, (c + 1) * Q)
        col = col_ref[rows, :]
        dt = jax.nn.softplus(e_ref[rows, :] + bias)
        cum = tri_sum(tri, dt * rate)
        dt_ref[rows, :] = dt
        cum_ref[rows, :] = cum
        all_ref[rows, :] = cum + offset
        for j in range(CONVCH // 128):
            lanes = slice(j * 128, (j + 1) * 128)
            if c == 0:
                window = jnp.concatenate([halo_ref[:, lanes], rc_ref[0:Q, lanes]], axis=0)
            else:
                window = rc_ref[c * Q - 16 : (c + 1) * Q, lanes]
            window = window.astype(f32)
            pre = par_ref[TAP_BIAS : TAP_BIAS + 1, lanes] + par_ref[3:4, lanes] * window[16:]
            for d in range(1, CONV):
                pre = pre + par_ref[3 - d : 4 - d, lanes] * window[16 - d : 16 + Q - d] * col[:, d - 1 : d]
            gate = jax.nn.sigmoid(pre)
            out = pre * gate
            q_ref[rows, lanes] = out
            ds_ref[rows, lanes] = (gate + out * (1.0 - gate)).astype(bf16)
        end = cum[Q - 1 : Q, :]
        weight = dt * jnp.exp(end - cum) * col[:, 4:5]
        scaled, scaled_low = split(q_ref[rows, 0:DI] * expand(weight, spread))
        b_rows, b_low = split(q_ref[rows, DI : DI + STATE].T)
        lin_ref[c, 0:STATE], lin_ref[c, STATE:] = split(state)
        step = jnp.exp(end) * col[Q - 1 : Q, 3:4]
        state = state * expand_row(step, spread) + product(b_rows, b_low, scaled, scaled_low)
        decay = decay * step
        offset = offset + end
    wide = expand_row(decay, spread)
    for half in range(2):
        lanes = slice(half * HALF, (half + 1) * HALF)
        pack_ref[half, 0:STATE, :] = state[:, lanes]
        pack_ref[half, STATE:, :] = jnp.broadcast_to(wide[:, lanes], (8, HALF))


def intra_kernel(q_ref, dt_ref, cum_ref, col_ref, lab_ref, lin_ref, par_ref, sp_ref, y_ref):
    spread = sp_ref[...]
    col = col_ref[...]
    cum = cum_ref[...]
    cum_t = cum.T
    x = q_ref[:, 0:DI]
    b_rows, b_low = split(q_ref[:, DI : DI + STATE])
    c_rows, c_low = split(q_ref[:, DI + STATE :])
    x_dt, x_low = split(x * expand(dt_ref[...], spread))
    scores = nt(c_rows, b_rows) + (nt(c_rows, b_low) + nt(c_low, b_rows))
    same = (col[:, 7:8] == lab_ref[0:1, :]) & (iota((Q, Q), 0) >= iota((Q, Q), 1))
    shut = jnp.where(same, 0.0, masked)
    reach = expand(jnp.exp(cum) * col[:, 3:4], spread)
    base = product(c_rows, c_low, lin_ref[0, 0:STATE], lin_ref[0, STATE:]) * reach + skip_row(par_ref, spread) * x
    for j in range(H // 2):
        lanes = slice(j * 128, (j + 1) * 128)
        mixing, mixing_low = split(
            jnp.concatenate(
                [
                    jnp.exp(cum[:, h : h + 1] - cum_t[h : h + 1, :] + shut) * scores
                    for h in (2 * j, 2 * j + 1)
                ],
                axis=1,
            )
        )
        pair = two_heads(x_dt[:, lanes])
        y_ref[:, lanes] = (
            base[:, lanes]
            + nn(mixing, pair)
            + (nn(mixing_low, pair) + nn(mixing, two_heads(x_low[:, lanes])))
        )


def gate_kernel(
    y0_ref, z_ref, c_ref, all_ref, col_ref, inc_ref, par_ref, w_ref, x_ref, sp_ref,
    y_ref, v_ref, out_ref,
):
    reach = jnp.exp(all_ref[...]) * col_ref[:, 5:6]
    y = y0_ref[...] + expand(reach, sp_ref[...]) * product(
        *split(c_ref[...]), *split(inc_ref[...])
    )
    y_ref[...] = y
    z = z_ref[...]
    gated = y * (z * jax.nn.sigmoid(z))
    scale = lax.rsqrt(jnp.mean(gated * gated, axis=1, keepdims=True) + epsilon)
    v = (gated * scale * par_ref[GAIN : GAIN + 1, 0:DI]).astype(bf16)
    v_ref[...] = v
    out_ref[...] = (x_ref[...].astype(f32) + nn(v, w_ref[...])).astype(bf16)


def gate_back_kernel(
    g_ref, w_ref, y_ref, z_ref, par_ref, c_ref, all_ref, col_ref, decay_ref, sp_ref,
    dy_ref, dz_ref, dgain_ref, pack_ref, total_ref,
):
    step = pl.program_id(0)
    dv = nt(g_ref[...], w_ref[...])
    y = y_ref[...]
    z = z_ref[...]
    gate = jax.nn.sigmoid(z)
    silu = z * gate
    gated = y * silu
    scale = lax.rsqrt(jnp.mean(gated * gated, axis=1, keepdims=True) + epsilon)
    normed = gated * scale
    dn = dv * par_ref[GAIN : GAIN + 1, 0:DI]
    dgated = scale * (dn - normed * jnp.mean(dn * normed, axis=1, keepdims=True))
    dz_ref[...] = (dgated * y * (gate + silu * (1.0 - gate))).astype(bf16)
    dy = (dgated * silu).astype(bf16)
    dy_ref[...] = dy
    reach = jnp.exp(all_ref[...]) * col_ref[:, 5:6]
    reached = (dy.astype(f32) * expand(reach, sp_ref[...])).astype(bf16)
    part = tn(c_ref[...], reached)
    gain_part = jnp.sum(dv * normed, axis=0, keepdims=True)

    @pl.when(step == 0)
    def _():
        total_ref[...] = part
        dgain_ref[...] = gain_part

    @pl.when(step > 0)
    def _():
        total_ref[...] += part
        dgain_ref[...] += gain_part

    @pl.when(step == pl.num_programs(0) - 1)
    def _():
        for half in range(2):
            pack_ref[half, 0:STATE, :] = total_ref[:, half * HALF : (half + 1) * HALF].astype(bf16)
            pack_ref[half, STATE:, :] = decay_rows(decay_ref[half, STATE : STATE + 1, :])


def intra_back_kernel(
    q_ref, dt_ref, cum_ref, all_ref, col_ref, lab_ref, lin_ref, inc_ref, dy_ref, y_ref, par_ref, sp_ref,
    dx_ref, dbc_ref, hs_ref, carry_ref,
):
    @pl.when(pl.program_id(0) == 0)
    def _():
        carry_ref[...] = jnp.zeros_like(carry_ref)

    spread = sp_ref[...]
    col = col_ref[...]
    cum = cum_ref[...]
    cum_t = cum.T
    x = q_ref[:, 0:DI]
    b_rows, b_low = split(q_ref[:, DI : DI + STATE])
    c_rows, c_low = split(q_ref[:, DI + STATE :])
    dy = dy_ref[...]
    dy32 = dy.astype(f32)
    x_wide = x * expand(dt_ref[...], spread)
    x_dt = x_wide.astype(bf16)
    end = cum[Q - 1 : Q, :]
    leave = expand(jnp.exp(end - cum) * col[:, 4:5], spread)
    carry = carry_ref[...]
    carry_high, carry_low = split(carry)
    base = product(b_rows, b_low, carry_high, carry_low) * leave
    scores = nt(b_rows, c_rows) + (nt(b_low, c_rows) + nt(b_rows, c_low))
    same = (col[:, 7:8] == lab_ref[0:1, :]) & (iota((Q, Q), 1) >= iota((Q, Q), 0))
    shut = jnp.where(same, 0.0, masked)
    dscores = jnp.zeros((Q, Q), f32)
    for j in range(H // 2):
        lanes = slice(j * 128, (j + 1) * 128)
        dy_pair = dy[:, lanes]
        grads = nt(two_heads(x_dt[:, lanes]), dy_pair)
        mixing = []
        for k in range(2):
            h = 2 * j + k
            kernel = jnp.exp(cum_t[h : h + 1, :] - cum[:, h : h + 1] + shut)
            mixing.append(kernel * scores)
            dscores = dscores + grads[k * Q : (k + 1) * Q] * kernel
        mixing, mixing_low = split(jnp.concatenate(mixing, axis=1))
        pair = two_heads(dy_pair)
        dx_ref[:, lanes] = base[:, lanes] + nn(mixing, pair) + nn(mixing_low, pair)
    dx = dx_ref[...]
    near, near_low = split(dy32 * expand(jnp.exp(cum) * col[:, 3:4], spread))
    far = (dy32 * expand(jnp.exp(all_ref[...]) * col[:, 5:6], spread)).astype(bf16)
    low = dscores.astype(bf16)
    inc_high, inc_low = split(inc_ref[...])
    left = (x_wide * leave).astype(bf16)
    dbc_ref[:, 0:STATE] = nn(low, c_rows) + nt(left, carry_high)
    dbc_ref[:, STATE:] = (
        nn(dscores.T.astype(bf16), b_rows)
        + nt(near, lin_ref[0, 0:STATE])
        + nt(near, lin_ref[0, STATE:])
        + nt(far, inc_high)
        + nt(far, inc_low)
    )
    hs_ref[:, 0:128] = head_sum(
        dy32 * (y_ref[...] - skip_row(par_ref, spread) * x) - x_wide * dx, spread
    )
    hs_ref[:, 128:] = head_sum(x * dx, spread)
    step = jnp.exp(end) * col[Q - 1 : Q, 3:4]
    c_rows, c_low = split(q_ref[:, DI + STATE :].T)
    carry_ref[...] = carry * expand_row(step, spread) + product(c_rows, c_low, near, near_low)


def conv_back_kernel(
    outg_ref, inc_ref, q_ref, ds_ref, dt_ref, all_ref, col_ref, e_ref, rc_ref, halo_ref,
    dy_ref, dx_ref, dbc_ref, hs_ref, par_ref, sp_ref,
    dre_ref, tail_ref, back_ref, dw_ref, dh_ref, pre_ref, sum_ref,
):
    count = q_ref.shape[0] // Q
    spread = sp_ref[...]
    outg = outg_ref[...]
    last = all_ref[count * Q - 1 : count * Q, :]
    skip = skip_row(par_ref, spread)
    rate = rates(par_ref)
    bias = head_row(par_ref, STEP_BIAS)
    total = jnp.zeros((1, 128), f32)
    skip_total = jnp.zeros((1, 128), f32)
    pre_ref[0:8, :] = jnp.zeros((8, CONVCH), f32)
    pre_ref[8 + count * Q :, :] = jnp.zeros((8, CONVCH), f32)
    for c in range(count):
        rows = slice(c * Q, (c + 1) * Q)
        moved = slice(8 + c * Q, 8 + (c + 1) * Q)
        col = col_ref[moved, :]
        x = q_ref[rows, 0:DI]
        dy = dy_ref[rows, :].astype(f32)
        wide_dt = expand(dt_ref[rows, :], spread)
        x_dt = (x * wide_dt).astype(bf16).astype(f32)
        leave = expand(jnp.exp(last - all_ref[rows, :]) * col[:, 6:7], spread)
        dx_far = leave * nn(q_ref[rows, DI : DI + STATE].astype(bf16), outg)
        dx = dx_ref[rows, :] + dx_far
        db = dbc_ref[rows, 0:STATE] + nt((x_dt * leave).astype(bf16), outg)
        far = head_sum(x_dt * dx_far, spread)
        total = total + jnp.sum(far, axis=0, keepdims=True)
        sum_ref[rows, 0:128] = hs_ref[rows, 0:128] - far
        sum_ref[rows, 128:] = hs_ref[rows, 128:] + head_sum(x * dx_far, spread)
        skip_total = skip_total + jnp.sum(head_sum(x * dy, spread), axis=0, keepdims=True)
        pre_ref[moved, 0:DI] = (wide_dt * dx + skip * dy) * ds_ref[rows, 0:DI].astype(f32)
        pre_ref[moved, DI : DI + STATE] = db * ds_ref[rows, DI : DI + STATE].astype(f32)
        pre_ref[moved, DI + STATE :] = dbc_ref[rows, STATE:] * ds_ref[rows, DI + STATE :].astype(f32)
    kept = jnp.exp(last) * col_ref[7 + count * Q : 8 + count * Q, 5:6]
    both = jnp.sum(outg.astype(f32) * inc_ref[...], axis=0, keepdims=True)
    through = kept * head_sum(jnp.broadcast_to(both, (8, DI)), spread)[0:1]
    tri = (iota((Q, Q), 0) <= iota((Q, Q), 1)).astype(bf16)
    later = total + through
    rate_total = jnp.zeros((1, 128), f32)
    bias_total = jnp.zeros((1, 128), f32)
    for c in reversed(range(count)):
        rows = slice(c * Q, (c + 1) * Q)
        sums = tri_sum(tri, sum_ref[rows, 0:128])
        dlog = sums + later
        later = later + sums[0:1]
        ddt = rate * dlog + sum_ref[rows, 128:]
        de = ddt * jax.nn.sigmoid(e_ref[rows, :] + bias)
        dre_ref[rows, CONVCH:] = jnp.where(iota((Q, 128), 1) < H, de, 0.0).astype(bf16)
        rate_total = rate_total + jnp.sum(dlog * dt_ref[rows, :], axis=0, keepdims=True)
        bias_total = bias_total + jnp.sum(de, axis=0, keepdims=True)
    row = iota((8, 128), 0)
    dh_ref[...] = jnp.where(
        row == 0,
        bias_total,
        jnp.where(row == 1, rate_total * rate, jnp.where(row == 2, skip_total, 0.0)),
    )
    for j in range(CONVCH // 128):
        lanes = slice(j * 128, (j + 1) * 128)
        taps = [par_ref[3 - d : 4 - d, lanes] for d in range(CONV)]
        sums = [jnp.zeros((1, 128), f32) for _ in range(CONV + 1)]
        front = pre_ref[0:16, lanes]
        early = jnp.zeros((8, 128), f32)
        for d in range(1, CONV):
            early = early + taps[d] * (front * col_ref[0:16, d - 1 : d])[d : d + 8]
        back_ref[:, lanes] = early
        for c in range(count):
            rows = slice(c * Q, (c + 1) * Q)
            ahead = pre_ref[8 + c * Q : 16 + (c + 1) * Q, lanes]
            col = col_ref[8 + c * Q : 16 + (c + 1) * Q, :]
            if c == 0:
                window = jnp.concatenate([halo_ref[:, lanes], rc_ref[0:Q, lanes]], axis=0)
            else:
                window = rc_ref[c * Q - 16 : (c + 1) * Q, lanes]
            window = window.astype(f32)
            here = ahead[0:Q]
            sums[CONV] = sums[CONV] + jnp.sum(here, axis=0, keepdims=True)
            sums[3] = sums[3] + jnp.sum(here * window[16:], axis=0, keepdims=True)
            grad = taps[0] * here
            for d in range(1, CONV):
                same = ahead * col[:, d - 1 : d]
                sums[3 - d] = sums[3 - d] + jnp.sum(
                    same[0:Q] * window[16 - d : 16 + Q - d], axis=0, keepdims=True
                )
                grad = grad + taps[d] * same[d : d + Q]
            dre_ref[rows, lanes] = grad.astype(bf16)
            if c == count - 1:
                tail_ref[:, lanes] = grad[Q - 8 :]
        row = iota((8, 128), 0)
        stacked = jnp.zeros((8, 128), f32)
        for k in range(CONV + 1):
            stacked = jnp.where(row == k, sums[k], stacked)
        dw_ref[:, lanes] = stacked


def params(steps):
    return pltpu.CompilerParams(
        dimension_semantics=("arbitrary",) * steps, vmem_limit_bytes=48 * 1024 * 1024
    )


def shape(*dims, dtype=f32):
    return jax.ShapeDtypeStruct(dims, dtype)


def whole(array):
    rank = len(array.shape)
    return pl.BlockSpec(array.shape, lambda *_: (0,) * rank)


def conv_forward(rc, halo, e, col, par, spread):
    rows = rc.shape[0]
    outs = (
        shape(rows, CONVCH),
        shape(rows, CONVCH, dtype=bf16),
        shape(rows, 128),
        shape(rows, 128),
        shape(rows, 128),
        shape(rows // Q, 2 * STATE, DI, dtype=bf16),
        shape(2, PACK_WIDE, HALF),
    )
    return pl.pallas_call(conv_kernel, out_shape=outs, compiler_params=params(0))(
        rc, halo, e, col, par, spread
    )


def intra_forward(q, dt, cum, col, lab, lin, par, spread):
    rows = q.shape[0]

    def by_row(width):
        return pl.BlockSpec((Q, width), lambda i: (i, 0))

    return pl.pallas_call(
        intra_kernel,
        grid=(rows // Q,),
        in_specs=[
            by_row(CONVCH),
            by_row(128),
            by_row(128),
            by_row(128),
            pl.BlockSpec((8, Q), lambda i: (0, i)),
            pl.BlockSpec((1, 2 * STATE, DI), lambda i: (i, 0, 0)),
            whole(par),
            whole(spread),
        ],
        out_specs=by_row(DI),
        out_shape=shape(rows, DI),
        compiler_params=params(1),
        cost_estimate=pl.CostEstimate(
            flops=8 * rows * Q * DI, bytes_accessed=rows * 20000, transcendentals=rows * Q * H
        ),
    )(q, dt, cum, col, lab, lin, par, spread)


def gate_forward(y0, z, q, total, col, inc, par, w_out, hidden, spread):
    rows = y0.shape[0]
    size = 256

    def by_row(width):
        return pl.BlockSpec((size, width), lambda i: (i, 0))

    return pl.pallas_call(
        gate_kernel,
        grid=(rows // size,),
        in_specs=[
            by_row(DI),
            by_row(DI),
            pl.BlockSpec((size, STATE), lambda i: (i, (DI + STATE) // STATE)),
            by_row(128),
            by_row(128),
            whole(inc),
            whole(par),
            whole(w_out),
            by_row(D),
            whole(spread),
        ],
        out_specs=(by_row(DI), by_row(DI), by_row(D)),
        out_shape=(shape(rows, DI), shape(rows, DI, dtype=bf16), shape(rows, D, dtype=bf16)),
        compiler_params=params(1),
    )(y0, z, q, total, col, inc, par, w_out, hidden, spread)


def gate_backward(grad, w_out, y, z, par, q, total, col, pack, spread):
    rows = y.shape[0]
    size = 256

    def by_row(width):
        return pl.BlockSpec((size, width), lambda i: (i, 0))

    outs = (
        shape(rows, DI, dtype=bf16),
        shape(rows, DI, dtype=bf16),
        shape(1, DI),
        shape(2, PACK, HALF, dtype=bf16),
    )
    return pl.pallas_call(
        gate_back_kernel,
        grid=(rows // size,),
        in_specs=[
            by_row(D),
            whole(w_out),
            by_row(DI),
            by_row(DI),
            whole(par),
            pl.BlockSpec((size, STATE), lambda i: (i, (DI + STATE) // STATE)),
            by_row(128),
            by_row(128),
            whole(pack),
            whole(spread),
        ],
        out_specs=(by_row(DI), by_row(DI), whole(outs[2]), whole(outs[3])),
        out_shape=outs,
        scratch_shapes=[pltpu.VMEM((STATE, DI), f32)],
        compiler_params=params(1),
    )(grad, w_out, y, z, par, q, total, col, pack, spread)


def intra_backward(q, dt, cum, total, col, lab, lin, inc, dy, y, par, spread):
    rows = q.shape[0]
    top = rows // Q - 1

    def by_row(width):
        return pl.BlockSpec((Q, width), lambda i: (top - i, 0))

    return pl.pallas_call(
        intra_back_kernel,
        grid=(rows // Q,),
        in_specs=[
            by_row(CONVCH),
            by_row(128),
            by_row(128),
            by_row(128),
            by_row(128),
            pl.BlockSpec((8, Q), lambda i: (0, top - i)),
            pl.BlockSpec((1, 2 * STATE, DI), lambda i: (top - i, 0, 0)),
            whole(inc),
            by_row(DI),
            by_row(DI),
            whole(par),
            whole(spread),
        ],
        out_specs=(by_row(DI), by_row(256), by_row(256)),
        out_shape=(shape(rows, DI), shape(rows, 256), shape(rows, 256)),
        scratch_shapes=[pltpu.VMEM((STATE, DI), f32)],
        compiler_params=params(1),
        cost_estimate=pl.CostEstimate(
            flops=30 * rows * Q * DI, bytes_accessed=rows * 30000, transcendentals=rows * Q * H
        ),
    )(q, dt, cum, total, col, lab, lin, inc, dy, y, par, spread)


def conv_backward(outg, inc, q, ds, dt, total, col, e, rc, halo, dy, dx, dbc, hs, par, spread):
    rows = q.shape[0]
    outs = (
        shape(rows, CONVCH + 128, dtype=bf16),
        shape(8, CONVCH),
        shape(8, CONVCH),
        shape(8, CONVCH),
        shape(8, 128),
    )
    return pl.pallas_call(
        conv_back_kernel,
        out_shape=outs,
        scratch_shapes=[pltpu.VMEM((rows + 16, CONVCH), f32), pltpu.VMEM((rows, 256), f32)],
        compiler_params=params(0),
    )(outg, inc, q, ds, dt, total, col, e, rc, halo, dy, dx, dbc, hs, par, spread)


def pick(first, a, b):
    return jnp.where(first, a, b)


def unpack(block):
    wide = block.astype(f32)
    if block.dtype == f32:
        return wide[STATE : STATE + 1], wide[:STATE]
    return wide[STATE : STATE + 1] + wide[STATE + 1 : STATE + 2], wide[:STATE]


def pack_up(pair, kind):
    if kind == f32:
        decay = jnp.broadcast_to(pair[0], (8, HALF))
        return jnp.concatenate([pair[1], decay], axis=0)
    return jnp.concatenate([pair[1].astype(bf16), decay_rows(pair[0])], axis=0)


def combine(earlier, later):
    return (earlier[0] * later[0], later[0] * earlier[1] + later[1])


def after(arrays, event):
    return lax.optimization_barrier((tuple(arrays), event))[0]


def chain_scan(pack, reverse, beside):
    section = lax.axis_index("section")
    size = lax.axis_size("seq")
    kept = lax.dynamic_index_in_dim(pack, section, 0, keepdims=False)
    given = lax.dynamic_index_in_dim(pack, 1 - section, 0, keepdims=False)
    got = lax.ppermute(given, "section", SWAP)
    leads = (section == 1) if reverse else (section == 0)
    lead = unpack(pick(leads, kept, got))
    follow = unpack(pick(leads, got, kept))
    reached = combine(lead, follow)
    before = None
    distance = 2
    results = []
    while distance < size:
        route = [(i, i + distance) for i in range(size - distance)]
        if reverse:
            route = [(b, a) for a, b in route]
        sent = pack_up(reached, pack.dtype)
        arrived = lax.ppermute(sent, "seq", route)
        if beside:
            needed, other = beside.pop(0)(sent)
            arrived, needed = tie(arrived, needed)
            results.append((needed, other))
        arrived = unpack(arrived)
        before = arrived if before is None else combine(arrived, before)
        reached = combine(arrived, reached)
        distance *= 2
    first = before[1]
    second = lead[1] + lead[0] * first
    own = pick(leads, first, second).astype(pack.dtype)
    other = lax.ppermute(pick(leads, second, first).astype(pack.dtype), "section", SWAP)
    low = section == 0
    incoming = jnp.concatenate([pick(low, own, other), pick(low, other, own)], axis=1)
    return incoming, results


def spread_layer(shard, layer):
    section, row = lax.axis_index("section"), lax.axis_index("fsdp")
    parts = lax.axis_size("fsdp")
    here = section == layer
    across = [(layer, 1 - layer)]
    own = pick(here, shard, lax.ppermute(shard, "section", across))
    blocks = []
    for shift in range(1, parts):
        route = [(layer * parts + i, layer * parts + (i + shift) % parts) for i in range(parts)]
        moved = lax.ppermute(shard, ("section", "fsdp"), route)
        blocks.append(pick(here, moved, lax.ppermute(moved, "section", across)))
    blocks = [own] + blocks
    if parts == 2:
        low = row == 0
        return jnp.concatenate([pick(low, blocks[0], blocks[1]), pick(low, blocks[1], blocks[0])], axis=0)
    ordered = []
    for k in range(parts):
        block = blocks[0]
        for shift in range(1, parts):
            block = pick((row - shift) % parts == k, blocks[shift], block)
        ordered.append(block)
    return jnp.concatenate(ordered, axis=0)


def fold(make):
    section, row = lax.axis_index("section"), lax.axis_index("fsdp")
    parts = lax.axis_size("fsdp")
    got = lax.ppermute(make(1 - section).astype(bf16), "section", SWAP)
    summed = (make(section) + got.astype(f32)).astype(bf16)
    if parts == 2:
        kept = lax.dynamic_index_in_dim(summed, row, 0, keepdims=False)
        given = lax.dynamic_index_in_dim(summed, 1 - row, 0, keepdims=False)
        got = lax.ppermute(given, "fsdp", SWAP)
        return (kept.astype(f32) + got.astype(f32)).astype(bf16)
    return lax.psum_scatter(summed, "fsdp", scatter_dimension=0, tiled=False)


def pair_sum(array):
    size, bit = lax.axis_size("seq"), lax.axis_index("seq") % 2
    halves = array.reshape(2, -1, array.shape[1])
    kept = lax.dynamic_index_in_dim(halves, bit, 0, keepdims=False)
    given = lax.dynamic_index_in_dim(halves, 1 - bit, 0, keepdims=False)
    got = lax.ppermute(given, "seq", [(i, i ^ 1) for i in range(size)])
    return (kept.astype(f32) + got.astype(f32)).astype(bf16)


def pair_collect(array):
    size, low = lax.axis_size("seq"), lax.axis_index("seq") % 2 == 0
    got = lax.ppermute(array, "seq", [(i, i ^ 1) for i in range(size)])
    return jnp.concatenate([pick(low, array, got), pick(low, got, array)], axis=0)


def strides():
    size = lax.axis_size("seq")
    return [[i for i in range(size) if i % 2 == b] for b in range(2)]


def scatter_sum(array):
    count = lax.axis_size("seq") // 2
    blocks = array.reshape(count, -1, array.shape[1])
    got = lax.all_to_all(blocks, "seq", 0, 0, axis_index_groups=strides())
    return jnp.sum(got.astype(f32), axis=0).astype(bf16)


def collect(part):
    count = lax.axis_size("seq") // 2
    everyone = jnp.broadcast_to(part[None], (count,) + part.shape)
    got = lax.all_to_all(everyone, "seq", 0, 0, axis_index_groups=strides())
    return got.reshape(-1, part.shape[1])


def sum_everywhere(array):
    for axis in ("fsdp", "seq"):
        size = lax.axis_size(axis)
        distance = 1
        while distance < size:
            array = array + lax.ppermute(array, axis, [(i, i ^ distance) for i in range(size)])
            distance *= 2
    return array


def tie(*arrays):
    return lax.optimization_barrier(arrays)


def place_kernel(section_ref, early_ref, early_got_ref, late_ref, late_got_ref, e_ref, in_ref, out_ref):
    low = section_ref[0] == 0
    early, early_got = early_ref[...].astype(f32), early_got_ref[...].astype(f32)
    late, late_got = late_ref[...].astype(f32), late_got_ref[...].astype(f32)
    for half in range(2):
        own = low if half == 0 else jnp.logical_not(low)
        both = jnp.where(own, early, early_got)
        in_ref[:, half * HALF : (half + 1) * HALF] = both[:, :HALF]
        for k in range(2):
            at = HALF + k * (D // 2)
            out_ref[k, :, half * (D // 2) : (half + 1) * (D // 2)] = both[:, at : at + D // 2]
        at = DI + half * (CONVCH // 2)
        in_ref[:, at : at + CONVCH // 2] = jnp.where(own, late, late_got)
    in_ref[:, DI + CONVCH :] = e_ref[:, :H]


def place(early, early_got, late, late_got, e):
    rows = early.shape[0]
    size = rows // 4

    def by_row(width):
        return pl.BlockSpec((size, width), lambda i: (i, 0))

    section = lax.axis_index("section").astype(jnp.int32)[None]
    width = DI + CONVCH + H
    w_in, w_out = pl.pallas_call(
        place_kernel,
        grid=(4,),
        in_specs=[
            pl.BlockSpec(memory_space=pltpu.SMEM),
            by_row(DI),
            by_row(DI),
            by_row(CONVCH // 2),
            by_row(CONVCH // 2),
            by_row(128),
        ],
        out_specs=(by_row(width), pl.BlockSpec((2, size, D), lambda i: (0, i, 0))),
        out_shape=(shape(rows, width), shape(2, rows, D)),
        compiler_params=params(1),
    )(section, early, early_got, late, late_got, e)
    return w_in[None], w_out.reshape(1, 2 * rows, D)


def labels(lengths, order, base, rows):
    documents = jnp.concatenate([lengths, order, base[None]]).astype(jnp.int32)
    return pl.pallas_call(
        label_kernel,
        in_specs=[pl.BlockSpec(memory_space=pltpu.SMEM)],
        out_shape=(shape(rows + 16, 128), shape(rows, 128), shape(8, rows)),
        compiler_params=params(0),
    )(documents)


def parameter_table(norm_gain, conv_w, conv_b, dt_bias, a_log, skip_scale, gate_gain):
    def row(array):
        return jnp.pad(array, ((0, 0), (0, CONVCH - array.shape[1])))

    pieces = [conv_w, conv_b, row(norm_gain), row(gate_gain), row(dt_bias), row(a_log), row(skip_scale)]
    return jnp.pad(jnp.concatenate(pieces, axis=0), ((0, 6), (0, 0)))


def local(
    tokens, cotangent, lengths, doc_order, norm_gain, w_in, conv_w, conv_b, dt_bias, a_log,
    skip_scale, gate_gain, w_out,
):
    rows = tokens.shape[2]
    section, seq = lax.axis_index("section"), lax.axis_index("seq")
    size = lax.axis_size("seq")
    micro = seq % 2
    aligned = section == micro
    spot = (seq // 2) * 2 + section

    def flat(s, i):
        return s * size + i

    everywhere = ("section", "seq")
    exchange = [
        (flat(s, 2 * k + s), flat(s, 2 * k + 1 - s)) for k in range(size // 2) for s in range(2)
    ]

    def to_chain(array):
        given = lax.dynamic_index_in_dim(array[:, 0], 1 - section, 0, keepdims=False)
        own = lax.dynamic_index_in_dim(array[:, 0], section, 0, keepdims=False)
        return pick(aligned, own, lax.ppermute(given, everywhere, exchange))

    first_in, first_z, first_out = w_in[0, :, DI:], w_in[0, :, :DI], w_out[0]

    def projection(shard, layer):
        return jnp.pad(spread_layer(shard, layer), ((0, 0), (0, CONVCH + 128 - shard.shape[1])))

    w_conv = [projection(first_in, 0), None]
    hidden = to_chain(tokens)
    second_in, second_z, second_out, w_first = lax.optimization_barrier(
        (first_in, first_z, first_out, w_conv[0])
    )
    w_conv[0] = w_first
    w_gate = [spread_layer(second_z, 0), None]
    w_back = [spread_layer(second_out, 0), None]
    third_in, third_z, third_out, w_back[0] = lax.optimization_barrier(
        (second_in, second_z, second_out, w_back[0])
    )
    w_conv[1] = projection(third_in, 1)
    w_gate[1] = spread_layer(third_z, 1)
    w_back[1] = spread_layer(third_out, 1)
    top_grad = to_chain(cotangent)

    table = parameter_table(
        norm_gain, conv_w[0], conv_b, dt_bias, a_log, skip_scale, gate_gain
    )
    other = lax.ppermute(table, "section", SWAP)
    low = section == 0
    tables = [pick(low, table, other), pick(low, other, table)]
    spread = spread_matrix()

    stream_lengths = lax.dynamic_index_in_dim(lengths[:, 0], micro, 0, keepdims=False)
    stream_order = lax.dynamic_index_in_dim(doc_order[:, 0], micro, 0, keepdims=False)
    col_padded, col, lab = labels(stream_lengths, stream_order, spot * rows, rows)
    follow = [(flat(0, i), flat(1, i)) for i in range(size)] + [
        (flat(1, i), flat(0, i + 2)) for i in range(size - 2)
    ]
    precede = [(b, a) for a, b in follow]

    kept = []
    results = []
    for layer in range(2):
        par = tables[layer]
        wide = hidden.astype(f32)
        scale = lax.rsqrt(jnp.mean(wide * wide, axis=1, keepdims=True) + epsilon)
        u = (wide * scale * par[NORM : NORM + 1, :D]).astype(bf16)
        rc = nn(u, w_conv[layer][:, :CONVCH]).astype(bf16)
        e = nn(u, w_conv[layer][:, CONVCH:])
        halo = lax.ppermute(rc[rows - 16 :], everywhere, follow)
        q, ds, dt, cum, total, lin, pack = conv_forward(
            rc, halo, e, col, par, spread
        )
        inc, ((y0, _), (z, _)) = chain_scan(
            pack,
            False,
            [
                lambda sent: (
                    intra_forward(*after((q, dt, cum, col, lab, lin, par), sent), spread),
                    None,
                ),
                lambda sent: (nn(*after((u, w_gate[layer]), sent)), None),
            ],
        )
        y, v, out = gate_forward(
            y0, z, q, total, col, inc, par, w_back[layer], hidden, spread
        )
        kept.append((hidden, scale, u, rc, e, halo, q, ds, dt, cum, total, lin, pack, inc, z, y, v))
        results.append(out)
        hidden = out

    def columns(a, b):
        return lax.dot_general(a, b, (((0,), (0,)), ((), ())), preferred_element_type=f32)

    parts = lax.axis_size("fsdp")

    def half_of(array, half):
        width = array.shape[1] // 2
        return lax.dynamic_slice_in_dim(array, half * width, width, axis=1)

    def early_grads(u, dz, v, grad):
        def make(half):
            for_in = columns(u, half_of(dz, half)).reshape(parts, -1, HALF)
            for_out = columns(v, half_of(grad, half)).reshape(parts, 2, -1, D // 2)
            return jnp.concatenate([for_in, for_out[:, 0], for_out[:, 1]], axis=2)

        return make

    def late_grads(u, dr):
        return lambda half: columns(u, half_of(dr, half)).reshape(parts, -1, CONVCH // 2)

    grad = top_grad
    input_grads = [None, None]
    early = [None, None]
    late = [None, None]
    small = [None, None]
    for layer in (1, 0):
        par = tables[layer]
        hidden, scale, u, rc, e, halo, q, ds, dt, cum, total, lin, pack, inc, z, y, v = kept[layer]
        dy, dz, dgain, back = gate_backward(
            grad, w_back[layer], y, z, par, q, total, col, pack, spread
        )
        if layer == 0:
            early[1], back = tie(early[1], back)
            early[1] = pair_sum(early[1])

        def beside_first(sent):
            needed = intra_backward(
                *after((q, dt, cum, total, col, lab, lin, inc, dy, y, par), sent), spread
            )
            return needed, None

        def beside_second(sent):
            a, b, c, d = after((v, u, grad, dz), sent)
            ahead = None
            if layer == 0:
                ahead = pair_sum(tie(late[1], early[1], sent)[0])
            return nt(d, w_gate[layer]), (fold(early_grads(b, d, a, c)), ahead)

        outg, (((dx, dbc, hs), _), (du, (early[layer], ahead))) = chain_scan(
            back, True, [beside_first, beside_second]
        )
        if layer == 0:
            outg, first, second = tie(outg, early[1], ahead)
            upper = scatter_sum(jnp.concatenate([first, second], axis=1))
        dre, tail, front, dw, dh = conv_backward(
            outg, inc, q, ds, dt, total, col_padded, e, rc, halo, dy, dx, dbc, hs, par, spread
        )
        returned = lax.ppermute(front, everywhere, precede)
        dre = lax.dynamic_update_slice(dre, (tail + returned).astype(bf16), (rows - 8, 0))
        du = du + nt(dre, w_conv[layer])
        wide = hidden.astype(f32)
        normed = wide * scale
        dn = du * par[NORM : NORM + 1, :D]
        dnorm = jnp.sum(du * normed, axis=0)
        dhidden = scale * (dn - normed * jnp.mean(dn * normed, axis=1, keepdims=True))
        grad_e = columns(dre[:, CONVCH:], u)[:H].reshape(H // 2, 2 * D)
        if layer == 0:
            dre, upper, early[0] = tie(dre, upper, early[0])
            upper = collect(upper)
            early[0] = pair_sum(early[0])
        late[layer] = fold(late_grads(u, dre[:, :CONVCH]))
        grad = (grad.astype(f32) + dhidden).astype(bf16)
        input_grads[layer] = grad
        small[layer] = jnp.concatenate(
            [
                dw[: CONV + 1],
                jnp.pad(dnorm, (0, CONVCH - D))[None],
                jnp.pad(dgain, ((0, 0), (0, CONVCH - DI))),
                jnp.pad(dh[0:3], ((0, 0), (0, CONVCH - 128))),
                jnp.pad(grad_e, ((0, 0), (0, CONVCH - 2 * D))),
            ],
            axis=0,
        )
    late[0], upper, early[0] = tie(late[0], upper, early[0])
    early[0] = scatter_sum(early[0])
    late[0] = pair_sum(late[0])
    upper = pair_collect(upper)
    early[1], late[1] = upper[:, :DI], upper[:, DI:]
    late[0], early[0] = tie(late[0], early[0])
    late[0] = pair_collect(collect(scatter_sum(late[0])))
    early[0] = pair_collect(collect(early[0]))
    early_got = lax.ppermute(pick(low, early[1], early[0]), "section", SWAP)
    late_got = lax.ppermute(pick(low, late[1], late[0]), "section", SWAP)
    mine = pick(low, small[0], small[1]) + lax.ppermute(pick(low, small[1], small[0]), "section", SWAP)
    mine = sum_everywhere(mine)
    grad_e = mine[SKIP + 1 :, : 2 * D].reshape(H, parts, D // parts)
    grad_e = lax.dynamic_index_in_dim(grad_e, lax.axis_index("fsdp"), 1, keepdims=False).T
    shard_in, shard_out = place(
        pick(low, early[0], early[1]),
        early_got,
        pick(low, late[0], late[1]),
        late_got,
        jnp.pad(grad_e, ((0, 0), (0, 128 - H))),
    )

    def to_holders(first, second):
        even = micro == 0
        one, two = [], []
        for k in range(size // 2):
            for s in range(2):
                one += [(flat(s, 2 * k), flat(0, 2 * k + s)), (flat(s, 2 * k + 1), flat(1, 2 * k + s))]
                two += [(flat(s, 2 * k), flat(1, 2 * k + s)), (flat(s, 2 * k + 1), flat(0, 2 * k + s))]
        got_one = lax.ppermute(pick(even, first, second), everywhere, one)
        got_two = lax.ppermute(pick(even, second, first), everywhere, two)
        stacked = jnp.stack([pick(low, got_one, got_two), pick(low, got_two, got_one)])
        return stacked[None, :, None]

    activations = to_holders(results[0], results[1])
    grads = to_holders(input_grads[0], input_grads[1])
    return (
        activations,
        grads,
        mine[NORM : NORM + 1, :D],
        shard_in,
        mine[None, :CONV],
        mine[TAP_BIAS : TAP_BIAS + 1],
        mine[STEP_BIAS : STEP_BIAS + 1, :H],
        mine[BASE_RATE : BASE_RATE + 1, :H],
        mine[SKIP : SKIP + 1, :H],
        mine[GAIN : GAIN + 1, :DI],
        shard_out,
    )


def solution(mesh):
    in_specs = (
        P(None, "fsdp", "seq", None),
        P(None, "fsdp", "seq", None),
        P(None, "fsdp", None),
        P(None, "fsdp", None),
        P("section", None),
        P("section", "fsdp", None),
        P("section", None, None),
        P("section", None),
        P("section", None),
        P("section", None),
        P("section", None),
        P("section", None),
        P("section", "fsdp", None),
    )
    out_specs = (
        P("section", None, "fsdp", "seq", None),
        P("section", None, "fsdp", "seq", None),
        P("section", None),
        P("section", "fsdp", None),
        P("section", None, None),
        P("section", None),
        P("section", None),
        P("section", None),
        P("section", None),
        P("section", None),
        P("section", "fsdp", None),
    )
    return jax.shard_map(local, mesh=mesh, in_specs=in_specs, out_specs=out_specs, check_vma=False)
```

time: 1440 us -> 602 us (0.42)
  matrix products: 346 us -> 42.2 us
  waiting for transfers between devices: 404 us -> 139 us
  other arithmetic: 317 us -> 67.4 us
  blocking collectives: 196 us -> 0 us
  Pallas kernels: 0 us -> 143 us
  starting transfers between devices: 23.6 us -> 146 us
  local copies, waits for them, and re-layouts: 116 us -> 47.8 us
  between operations: 21.1 us -> 3.81 us
    dot_general x63 -> x24, matrix products: 346 us -> 42.2 us  [the longest x14 19.9 us: columns(): lax.dot_general(a, b, (((0,), (0,)), ((), ())), preferred_element_type=f32)]
    all_gather x8 -> x0, waiting for transfers between devices: 254 us -> none  [the longest x3 164 us: carried_in(): everything = jax.tree.map(lambda part: lax.all_gather(part, axis), value)]
    pallas_call x0 -> x14, Pallas kernels: none -> 143 us  [the longest x2 34.8 us: intra_backward(): pl.pallas_call(intra_back_kernel, grid=(rows // Q,), in_specs=[by_row(CON...]
    all_gather x6 -> x0, blocking collectives: 117 us -> none  [the longest x3 63.9 us: carried_in(): everything = jax.tree.map(lambda part: lax.all_gather(part, axis), value)]
    ppermute x10 -> x67, waiting for transfers between devices: 18.4 us -> 131 us  [the longest x4 33.7 us: fold(): got = lax.ppermute(given, 'fsdp', SWAP)]
    ppermute x10 -> x67, starting transfers between devices: 22.9 us -> 124 us  [the longest x8 20.1 us: chain_scan(): arrived = lax.ppermute(sent, 'seq', route)]
    psum x1 -> x0, blocking collectives: 78.9 us -> none  [local(): lax.psum((sum_norm, sum_conv_w, sum_conv_b, sum_step, sum_rates, sum_skip...]
    reduce_sum x30 -> x5, other arithmetic: 72.4 us -> 3.38 us  [the longest x2 1.88 us: local(): scale = lax.rsqrt(jnp.mean(wide * wide, axis=1, keepdims=True) + epsilon)]
  transfers between devices with their start and end apart: 21 -> 73, of which waited for: 16 -> 19; matrix products, arithmetic and copies ran while one was open for 21% -> 21% of each run, Pallas kernels for 0% -> 18%
where the time goes in v1:
time: 602 us; the launch traced here: 590 us
  starting transfers between devices  146 us (24%)
  Pallas kernels  143 us (24%)
  waiting for transfers between devices  139 us (23%)
  other arithmetic  67.4 us (11%)
  local copies, waits for them, and re-layouts  47.8 us (8%)
  matrix products  42.2 us (7%)
    pallas_call x2, Pallas kernels, intra_backward(): pl.pallas_call(intra_back_kernel, grid=(rows // Q,), in_specs=[by_row(CON...  34.8 us
    ppermute x4, waiting for transfers between devices, fold(): got = lax.ppermute(given, 'fsdp', SWAP)  33.7 us
    pallas_call x2, Pallas kernels, conv_backward(): pl.pallas_call(conv_back_kernel, out_shape=outs, scratch_shapes=[pltpu.VM...  32.3 us
    ppermute x4, waiting for transfers between devices, sum_everywhere(): lax.ppermute(array, axis, [(i, i ^ distance) for i in range(size)])  31.7 us
    ppermute x8, waiting for transfers between devices, chain_scan(): arrived = lax.ppermute(sent, 'seq', route)  25.7 us
    select_n x27, other arithmetic, pick(): return jnp.where(first, a, b)  24.3 us
    unnamed x231, local copies, waits for them, and re-layouts  23.7 us
    ppermute x8, starting transfers between devices, chain_scan(): arrived = lax.ppermute(sent, 'seq', route)  20.1 us
  transfers between devices with their start and end apart: 73, of which 19 were waited for; matrix products, arithmetic and copies ran while one was open for 21% of the time, Pallas kernels for 18%

profile of v1, /device:TPU:0, one launch (start us, length us, event | category | flops | bytes accessed | tf_op | source)
XLA Modules:
  0.0 590.0 jit_solution(13078487112568868466)
XLA Ops:
  3.4 5.0 collective-permute-start.3
  10.9 4.3 collective-permute-start
  18.1 7.1 %collective-permute-done.3 = bf16[384,1816]{0,1:T(8,128)(2,1)} collective-permute-done((bf16[384,1816]{0,1:T(8,128)(2,1)}, bf16[384,1816]{0,1:T(8,128)(2,1)}, u32[]{:S(2)}, u32[]{:S(2)}) %collective-permute-start.3) | collective-permute-done | bytes 1394720 | tf_op jit(solution)/shard_map/ppermute | solution.py:682
  35.3 3.9 collective-permute-start.14
  43.0 9.7 %shard_map.213 = (f32[512,1792]{1,0:T(8,128)}, bf16[512,1792]{1,0:T(8,128)(2,1)S(1)}, f32[512,128]{1,0:T(8,128)S(1)}, f32[512,128]{1,0:T(8,128)S(1)}, f32[512,12...) custom-call(bf16[512,1792]{1,0:T(8,128)(2,1)} %copy-done.66, ...), custom_call_target="tpu_custom_call" | custom-call | tf_op jit(solution)/shard_map/pallas_call | solution.py:464
  61.9 4.2 collective-permute-start.7
  68.6 8.1 %shard_map.214.y0_ref = f32[512,1536]{1,0:T(8,128)S(1)} custom-call(f32[512,1792]{1,0:T(8,128)} %get-tuple-element.238.q_ref.c_ref, f32[512,128]{1,0:T(8,128)S(1)} %get-tuple-element.239.dt_ref, f32[512,128]{1,0:T(8,128)S(1)} %get-tuple-element.240.cum_ref, f32[512,128]{1,0:T(8,128)S(1)} %get-tuple-element.242.col_ref, ...), custom_call_target="tpu_custom_call" | custom-call | flops 805306368 | bytes 10240000 | tf_op jit(solution)/shard_map/pallas_call | solution.py:475
  78.3 4.5 collective-permute-start.8
  97.9 4.5 collective-permute-start.32
  105.7 8.1 %shard_map.215 = (f32[512,1536]{1,0:T(8,128)}, bf16[512,1536]{1,0:T(8,128)(2,1)S(1)}, bf16[512,768]{1,0:T(8,128)(2,1)S(1)}) custom-call(f32[512,1536]{1,0:T(8,128)} %copy-done.3, f32[512,1536]{1,0:T(8,128)} %fusion.118.z_ref, f32[512,1792]{1,0:T(8,128)} %get-tuple-element.238.q_ref.c_ref, f32[512,128]{1,0:T(8,128)S(1)} %get-tuple-element.241.all_ref, ...), custom_call_target="tpu_custom_call" | custom-call | tf_op jit(solution)/shard_map/pallas_call | solution.py:504
  122.9 12.6 %collective-permute-start.19 = (bf16[16,1792]{1,0:T(8,128)(2,1)S(1)}, bf16[16,1792]{1,0:T(8,128)(2,1)S(1)}, u32[]{:S(2)}, u32[]{:S(2)}) collective-permute-start(bf16[16,1792]{1,0:T(8,128)(2,1)S(1)} %slice.316), channel_id=1, source_target_pairs={{0,16},{2,18},{4,20},{6,22},{8,24},{10,26},{12,28},{14,30},{16,4},... | collective-permute-start | bytes 172040 | tf_op jit(solution)/shard_map/ppermute | solution.py:889
  137.2 9.6 %shard_map.216 = (f32[512,1792]{1,0:T(8,128)}, bf16[512,1792]{1,0:T(8,128)(2,1)S(1)}, f32[512,128]{1,0:T(8,128)S(1)}, f32[512,128]{1,0:T(8,128)S(1)}, f32[512,12...) custom-call(bf16[512,1792]{1,0:T(8,128)(2,1)} %copy-done.67, ...), custom_call_target="tpu_custom_call" | custom-call | tf_op jit(solution)/shard_map/pallas_call | solution.py:464
  151.6 3.1 collective-permute-start.21
  156.8 8.9 %shard_map.217.y0_ref = f32[512,1536]{1,0:T(8,128)S(1)} custom-call(f32[512,1792]{1,0:T(8,128)} %get-tuple-element.203.q_ref.c_ref, f32[512,128]{1,0:T(8,128)S(1)} %get-tuple-element.204.dt_ref, f32[512,128]{1,0:T(8,128)S(1)} %get-tuple-element.205.cum_ref, f32[512,128]{1,0:T(8,128)S(1)} %get-tuple-element.242.col_ref, ...), custom_call_target="tpu_custom_call" | custom-call | flops 805306368 | bytes 10240000 | tf_op jit(solution)/shard_map/pallas_call | solution.py:475
  171.6 5.1 collective-permute-done.22
  182.1 7.9 %shard_map.218 = (f32[512,1536]{1,0:T(8,128)}, bf16[512,1536]{1,0:T(8,128)(2,1)S(1)}, bf16[512,768]{1,0:T(8,128)(2,1)S(1)}) custom-call(f32[512,1536]{1,0:T(8,128)} %copy-done.4, f32[512,1536]{1,0:T(8,128)} %fusion.119.z_ref, f32[512,1792]{1,0:T(8,128)} %get-tuple-element.203.q_ref.c_ref, f32[512,128]{1,0:T(8,128)S(1)} %get-tuple-element.206.all_ref, ...), custom_call_target="tpu_custom_call" | custom-call | tf_op jit(solution)/shard_map/pallas_call | solution.py:504
  191.1 9.1 %shard_map.219 = (bf16[512,1536]{1,0:T(8,128)(2,1)S(1)}, bf16[512,1536]{1,0:T(8,128)(2,1)}, f32[1,1536]{1,0:T(1,128)S(1)}, bf16[2,144,768]{2,1,0:T(8,128)(2,1)}) custom-call(bf16[512,768]{1,0:T(8,128)(2,1)S(1)} %bitcast_select_fusion.g_ref, bf16[1536,768]{1,0:T(8,128)(2,1)} %pad_maximum_fusion.4.w_ref, f32[512,1536]{1,0:T(8,128)} %get-tuple-element.212.y_ref, ...), custom_call_target="tpu_custom_call" | custom-call | tf_op jit(solution)/shard_map/pallas_call | solution.py:538
  207.4 17.6 %shard_map.220 = (f32[512,1536]{1,0:T(8,128)}, f32[512,256]{1,0:T(8,128)S(1)}, f32[512,256]{1,0:T(8,128)S(1)}) custom-call(f32[512,1792]{1,0:T(8,128)} %get-tuple-element.203.q_ref.c_ref, f32[512,128]{1,0:T(8,128)S(1)} %copy-done.29, f32[512,128]{1,0:T(8,128)S(1)} %copy-done.39, f32[512,128]{1,0:T(8,128)S(1)} %copy-done.18, ...), custom_call_target="tpu_custom_call" | custom-call | flops 3019898880 | bytes 15360000 | tf_op jit(solution)/shard_map/pallas_call | solution.py:567
  231.5 15.9 %collective-permute-done.35 = bf16[144,768]{1,0:T(8,128)(2,1)S(1)} collective-permute-done((bf16[144,768]{1,0:T(8,128)(2,1)S(1)}, bf16[144,768]{1,0:T(8,128)(2,1)S(1)}, u32[]{:S(2)}, u32[]{:S(2)}) %collective-permute-start.35) | collective-permute-done | bytes 221216 | tf_op jit(solution)/shard_map/ppermute | solution.py:655
  249.3 16.4 %shard_map.221 = (bf16[512,1920]{1,0:T(8,128)(2,1)}, f32[8,1792]{1,0:T(8,128)S(1)}, f32[8,1792]{1,0:T(8,128)S(1)}, f32[8,1792]{1,0:T(8,128)S(1)}, f32[8,128]{1,0:T(8,128)S(1)}) custom-call(bf16[128,1536]{1,0:T(8,128)(2,1)S(1)} %pad_maximum_fusion.17.outg_ref, f32[128,1536]{1,0:T(8,128)S(1)} %pad_maximum_fusion.10.inc_ref, ...), custom_call_target="tpu_custom_call" | custom-call | tf_op jit(solution)/shard_map/pallas_call | solution.py:603
  288.7 4.1 fusion.34
  293.9 8.6 %shard_map.222 = (bf16[512,1536]{1,0:T(8,128)(2,1)S(1)}, bf16[512,1536]{1,0:T(8,128)(2,1)}, f32[1,1536]{1,0:T(1,128)S(1)}, bf16[2,144,768]{2,1,0:T(8,128)(2,1)S(1)}) custom-call(bf16[512,768]{1,0:T(8,128)(2,1)S(1)} %fusion.33.g_ref, bf16[1536,768]{1,0:T(8,128)(2,1)} %pad_maximum_fusion.2.w_ref, f32[512,1536]{1,0:T(8,128)} %get-tuple-element.247.y_ref, ...), custom_call_target="tpu_custom_call" | custom-call | tf_op jit(solution)/shard_map/pallas_call | solution.py:538
  302.7 23.1 %collective-permute-done.39 = bf16[384,1536]{1,0:T(8,128)(2,1)S(1)} collective-permute-done((bf16[384,1536]{1,0:T(8,128)(2,1)S(1)}, bf16[384,1536]{1,0:T(8,128)(2,1)S(1)}, u32[]{:S(2)}, u32[]{:S(2)}) %collective-permute-start.39) | collective-permute-done | bytes 1179680 | tf_op jit(solution)/shard_map/ppermute | solution.py:705
  326.4 4.0 collective-permute-start.44
  332.2 17.2 %shard_map.223 = (f32[512,1536]{1,0:T(8,128)}, f32[512,256]{1,0:T(8,128)S(1)}, f32[512,256]{1,0:T(8,128)S(1)}) custom-call(f32[512,1792]{1,0:T(8,128)} %get-tuple-element.238.q_ref.c_ref, f32[512,128]{1,0:T(8,128)S(1)} %copy-done.24, f32[512,128]{1,0:T(8,128)S(1)} %copy-done.37, f32[512,128]{1,0:T(8,128)S(1)} %get-tuple-element.241.all_ref, ...), custom_call_target="tpu_custom_call" | custom-call | flops 3019898880 | bytes 15360000 | tf_op jit(solution)/shard_map/pallas_call | solution.py:567
  363.8 4.7 collective-permute-done.42
  371.1 8.3 %collective-permute-done.47 = bf16[192,896]{1,0:T(8,128)(2,1)S(1)} collective-permute-done((bf16[192,896]{1,0:T(8,128)(2,1)S(1)}, bf16[192,896]{1,0:T(8,128)(2,1)S(1)}, u32[]{:S(2)}, u32[]{:S(2)}) %collective-permute-start.47) | collective-permute-done | bytes 344096 | tf_op jit(solution)/shard_map/ppermute | solution.py:715
  380.5 4.2 all-to-all-start
  384.8 3.7 fusion.3
  392.5 7.7 %collective-permute-start.30 = (bf16[512,768]{1,0:T(8,128)(2,1)}, bf16[512,768]{1,0:T(8,128)(2,1)}, u32[]{:S(2)}, u32[]{:S(2)}) collective-permute-start(bf16[512,768]{1,0:T(8,128)(2,1)} %get-tuple-element.366), channel_id=1, source_target_pairs={{0,0},{2,16},{16,2},{18,18},{4,4},{6,20},{20,6},{22,22},{8,8},{10,... | collective-permute-start | bytes 2359304 | tf_op jit(solution)/shard_map/ppermute | solution.py:1023
  400.4 15.9 %shard_map.224 = (bf16[512,1920]{1,0:T(8,128)(2,1)}, f32[8,1792]{1,0:T(8,128)S(1)}, f32[8,1792]{1,0:T(8,128)S(1)}, f32[8,1792]{1,0:T(8,128)S(1)}, f32[8,128]{1,0:T(8,128)S(1)}) custom-call(bf16[128,1536]{1,0:T(8,128)(2,1)S(1)} %copy-done.32, f32[128,1536]{1,0:T(8,128)S(1)} %copy-done.2, f32[512,1792]{1,0:T(8,128)} %get-tuple-element.238.q_ref.c_ref, ...), custom_call_target="tpu_custom_call" | custom-call | tf_op jit(solution)/shard_map/pallas_call | solution.py:603
  422.9 3.1 fusion.10
  431.9 3.1 fusion.26
  442.4 4.2 all-to-all-start.1
  451.3 3.9 collective-permute-done.60
  457.2 10.5 %collective-permute-done.59 = bf16[384,896]{1,0:T(8,128)(2,1)S(1)} collective-permute-done((bf16[384,896]{1,0:T(8,128)(2,1)S(1)}, bf16[384,896]{1,0:T(8,128)(2,1)S(1)}, u32[]{:S(2)}, u32[]{:S(2)}) %collective-permute-start.59) | collective-permute-done | bytes 688160 | tf_op jit(solution)/shard_map/ppermute | solution.py:705
  470.1 3.5 all-to-all-start.2
  473.6 3.5 broadcast_select_fusion.29
  479.7 6.5 %collective-permute-done.61 = bf16[192,896]{1,0:T(8,128)(2,1)S(1)} collective-permute-done((bf16[192,896]{1,0:T(8,128)(2,1)S(1)}, bf16[192,896]{1,0:T(8,128)(2,1)S(1)}, u32[]{:S(2)}, u32[]{:S(2)}) %collective-permute-start.61) | collective-permute-done | bytes 344096 | tf_op jit(solution)/shard_map/ppermute | solution.py:715
  489.1 3.6 all-to-all-start.4
  498.6 20.0 %collective-permute-done.53 = f32[22,1792]{1,0:T(8,128)S(1)} collective-permute-done((f32[22,1792]{1,0:T(8,128)S(1)}, f32[22,1792]{1,0:T(8,128)S(1)}, u32[]{:S(2)}, u32[]{:S(2)}) %collective-permute-start.53) | collective-permute-done | bytes 157728 | tf_op jit(solution)/shard_map/ppermute | solution.py:749
  521.8 3.6 all-to-all-start.3
  533.8 11.6 %collective-permute-done.55 = f32[22,1792]{1,0:T(8,128)S(1)} collective-permute-done((f32[22,1792]{1,0:T(8,128)S(1)}, f32[22,1792]{1,0:T(8,128)S(1)}, u32[]{:S(2)}, u32[]{:S(2)}) %collective-permute-start.55) | collective-permute-done | bytes 157728 | tf_op jit(solution)/shard_map/ppermute | solution.py:749
  546.4 3.5 all-to-all-start.5
  551.9 5.4 all-to-all-done.5
  557.5 8.3 %collective-permute-done.62 = bf16[192,1536]{1,0:T(8,128)(2,1)S(1)} collective-permute-done((bf16[192,1536]{1,0:T(8,128)(2,1)S(1)}, bf16[192,1536]{1,0:T(8,128)(2,1)S(1)}, u32[]{:S(2)}, u32[]{:S(2)}) %collective-permute-start.62) | collective-permute-done | bytes 589856 | tf_op jit(solution)/shard_map/ppermute | solution.py:721
  578.8 4.8 shard_map.225
  583.6 6.0 %copy.36 = f32[1,384,3352]{1,2,0:T(8,128)} copy(f32[1,384,3352]{2,1,0:T(8,128)} %bitcast.210) | data formatting | bytes 10297344
  (548 shorter events, 214.2 us)
Async XLA Ops:
  3.4 21.8 %collective-permute-start.3 = (bf16[384,1816]{0,1:T(8,128)(2,1)}, bf16[384,1816]{0,1:T(8,128)(2,1)}, u32[]{:S(2)}, u32[]{:S(2)}) collective-permute-start(bf16[384,1816]{0,1:T(8,128)(2,1)} %slice_bitcast_fusion), channel_id=1, source_target_pairs={{0,1},{1,0},{2,3},{3,2},{4,5},{5,4},{6,7},{7,6},{8,9},{9,8},{10,11... | collective-permute-start | bytes 4184072 | tf_op jit(solution)/shard_map/ppermute | solution.py:682
  8.4 23.3 %collective-permute-start.2 = (bf16[384,1816]{0,1:T(8,128)(2,1)}, bf16[384,1816]{0,1:T(8,128)(2,1)}, u32[]{:S(2)}, u32[]{:S(2)}) collective-permute-start(bf16[384,1816]{0,1:T(8,128)(2,1)} %slice_bitcast_fusion), channel_id=1, source_target_pairs={{0,16},{1,17},{2,18},{3,19},{4,20},{5,21},{6,22},{7,23},{8,24},{9,... | collective-permute-start | bytes 4184072 | tf_op jit(solution)/shard_map/ppermute | solution.py:678
  10.9 18.9 %collective-permute-start = (bf16[512,768]{1,0:T(8,128)(2,1)S(1)}, bf16[512,768]{1,0:T(8,128)(2,1)}, u32[]{:S(2)}, u32[]{:S(2)}) collective-permute-start(bf16[512,768]{1,0:T(8,128)(2,1)S(1)} %dynamic-slice_bitcast_fusion.3), channel_id=1, source_target_pairs={{0,2},{18,16},{4,6},{22,20},{8,10},{26,24},{12,14},{30,28},{1,3},{... | collective-permute-start | bytes 2359304 | tf_op jit(solution)/shard_map/ppermute | solution.py:841
  15.4 14.3 %collective-permute-start.1 = (f32[16,1792]{1,0:T(8,128)S(1)}, f32[16,1792]{1,0:T(8,128)S(1)}, u32[]{:S(2)}, u32[]{:S(2)}) collective-permute-start(f32[16,1792]{1,0:T(8,128)S(1)} %pad.65), channel_id=1, source_target_pairs={{0,16},{16,0},{1,17},{17,1},{2,18},{18,2},{3,19},{19,3},{4,20},{20... | collective-permute-start | bytes 344072 | tf_op jit(solution)/shard_map/ppermute | solution.py:867
  35.3 24.1 %collective-permute-start.14 = (bf16[768,768]{1,0:T(8,128)(2,1)S(1)}, bf16[768,768]{1,0:T(8,128)(2,1)S(1)}, u32[]{:S(2)}, u32[]{:S(2)}) collective-permute-start(bf16[768,768]{1,0:T(8,128)(2,1)S(1)} %bitcast.215), channel_id=1, source_target_pairs={{0,1},{1,0},{2,3},{3,2},{4,5},{5,4},{6,7},{7,6},{8,9},{9,8},{10,11... | collective-permute-start | bytes 3538952 | tf_op jit(solution)/shard_map/ppermute | solution.py:682
  55.5 21.2 %collective-permute-start.10 = (bf16[384,1536]{1,0:T(8,128)(2,1)}, bf16[384,1536]{1,0:T(8,128)(2,1)S(1)}, u32[]{:S(2)}, u32[]{:S(2)}) collective-permute-start(bf16[384,1536]{1,0:T(8,128)(2,1)} %bitcast.4), channel_id=1, source_target_pairs={{0,1},{1,0},{2,3},{3,2},{4,5},{5,4},{6,7},{7,6},{8,9},{9,8},{10,11... | collective-permute-start | bytes 3538952 | tf_op jit(solution)/shard_map/ppermute | solution.py:682
  57.9 24.8 %collective-permute-start.13 = (bf16[768,768]{1,0:T(8,128)(2,1)S(1)}, bf16[768,768]{1,0:T(8,128)(2,1)S(1)}, u32[]{:S(2)}, u32[]{:S(2)}) collective-permute-start(bf16[768,768]{1,0:T(8,128)(2,1)S(1)} %bitcast.216), channel_id=1, source_target_pairs={{0,16},{1,17},{2,18},{3,19},{4,20},{5,21},{6,22},{7,23},{8,24},{9,... | collective-permute-start | bytes 3538952 | tf_op jit(solution)/shard_map/ppermute | solution.py:678
  59.4 24.4 %collective-permute-start.15 = (bf16[768,768]{1,0:T(8,128)(2,1)S(1)}, bf16[768,768]{1,0:T(8,128)(2,1)}, u32[]{:S(2)}, u32[]{:S(2)}) collective-permute-start(bf16[768,768]{1,0:T(8,128)(2,1)S(1)} %collective-permute-done.14), channel_id=1, source_target_pairs={{0,16},{1,17},{2,18},{3,19},{4,20},{5,21},{6,22},{7,23},{8,24},{9,... | collective-permute-start | bytes 3538952 | tf_op jit(solution)/shard_map/ppermute | solution.py:683
  61.9 14.8 %collective-permute-start.7 = (f32[136,768]{1,0:T(8,128)S(1)}, f32[136,768]{1,0:T(8,128)S(1)}, u32[]{:S(2)}, u32[]{:S(2)}) collective-permute-start(f32[136,768]{1,0:T(8,128)S(1)} %pad_maximum_fusion.13), channel_id=1, source_target_pairs={{0,4},{2,6},{4,8},{6,10},{8,12},{10,14},{1,5},{3,7},{5,9},{7,11},{... | collective-permute-start | bytes 1253384 | tf_op jit(solution)/shard_map/ppermute | solution.py:655
  66.1 21.4 %collective-permute-start.9 = (bf16[384,1536]{1,0:T(8,128)(2,1)}, bf16[384,1536]{1,0:T(8,128)(2,1)}, u32[]{:S(2)}, u32[]{:S(2)}) collective-permute-start(bf16[384,1536]{1,0:T(8,128)(2,1)} %bitcast.4), channel_id=1, source_target_pairs={{0,16},{1,17},{2,18},{3,19},{4,20},{5,21},{6,22},{7,23},{8,24},{9,... | collective-permute-start | bytes 3538952 | tf_op jit(solution)/shard_map/ppermute | solution.py:678
  78.3 15.2 %collective-permute-start.8 = (f32[136,768]{1,0:T(8,128)S(1)}, f32[136,768]{1,0:T(8,128)S(1)}, u32[]{:S(2)}, u32[]{:S(2)}) collective-permute-start(f32[136,768]{1,0:T(8,128)S(1)} %pad_maximum_fusion.14), channel_id=1, source_target_pairs={{0,8},{2,10},{4,12},{6,14},{1,9},{3,11},{5,13},{7,15},{16,24},{18,... | collective-permute-start | bytes 1253384 | tf_op jit(solution)/shard_map/ppermute | solution.py:655
  94.3 23.3 %collective-permute-start.16 = (bf16[384,1816]{0,1:T(8,128)(2,1)}, bf16[384,1816]{0,1:T(8,128)(2,1)}, u32[]{:S(2)}, u32[]{:S(2)}) collective-permute-start(bf16[384,1816]{0,1:T(8,128)(2,1)} %slice_bitcast_fusion), channel_id=1, source_target_pairs={{16,0},{17,1},{18,2},{19,3},{20,4},{21,5},{22,6},{23,7},{24,8},{25... | collective-permute-start | bytes 4184072 | tf_op jit(solution)/shard_map/ppermute | solution.py:678
  95.6 23.3 %collective-permute-start.18 = (bf16[384,1816]{0,1:T(8,128)(2,1)}, bf16[384,1816]{0,1:T(8,128)(2,1)}, u32[]{:S(2)}, u32[]{:S(2)}) collective-permute-start(bf16[384,1816]{0,1:T(8,128)(2,1)} %collective-permute-done.17), channel_id=1, source_target_pairs={{16,0},{17,1},{18,2},{19,3},{20,4},{21,5},{22,6},{23,7},{24,8},{25... | collective-permute-start | bytes 4184072 | tf_op jit(solution)/shard_map/ppermute | solution.py:683
  97.9 49.1 %collective-permute-start.32 = (bf16[512,768]{1,0:T(8,128)(2,1)}, bf16[512,768]{1,0:T(8,128)(2,1)}, u32[]{:S(2)}, u32[]{:S(2)}) collective-permute-start(bf16[512,768]{1,0:T(8,128)(2,1)} %dynamic-slice_bitcast_fusion.2), channel_id=1, source_target_pairs={{0,2},{18,16},{4,6},{22,20},{8,10},{26,24},{12,14},{30,28},{1,3},{... | collective-permute-start | bytes 2359304 | tf_op jit(solution)/shard_map/ppermute | solution.py:841
  103.2 51.6 %collective-permute-start.23 = (bf16[384,1536]{1,0:T(8,128)(2,1)}, bf16[384,1536]{1,0:T(8,128)(2,1)}, u32[]{:S(2)}, u32[]{:S(2)}) collective-permute-start(bf16[384,1536]{1,0:T(8,128)(2,1)} %bitcast.4), channel_id=1, source_target_pairs={{16,0},{17,1},{18,2},{19,3},{20,4},{21,5},{22,6},{23,7},{24,8},{25... | collective-permute-start | bytes 3538952 | tf_op jit(solution)/shard_map/ppermute | solution.py:678
  115.9 33.4 %collective-permute-start.28 = (bf16[768,768]{1,0:T(8,128)(2,1)S(1)}, bf16[768,768]{1,0:T(8,128)(2,1)}, u32[]{:S(2)}, u32[]{:S(2)}) collective-permute-start(bf16[768,768]{1,0:T(8,128)(2,1)S(1)} %bitcast.218), channel_id=1, source_target_pairs={{16,17},{17,16},{18,19},{19,18},{20,21},{21,20},{22,23},{23,22},{2... | collective-permute-start | bytes 3538952 | tf_op jit(solution)/shard_map/ppermute | solution.py:682
  117.6 37.1 %collective-permute-start.25 = (bf16[384,1536]{1,0:T(8,128)(2,1)S(1)}, bf16[384,1536]{1,0:T(8,128)(2,1)}, u32[]{:S(2)}, u32[]{:S(2)}) collective-permute-start(bf16[384,1536]{1,0:T(8,128)(2,1)S(1)} %collective-permute-done.24), channel_id=1, source_target_pairs={{16,0},{17,1},{18,2},{19,3},{20,4},{21,5},{22,6},{23,7},{24,8},{25... | collective-permute-start | bytes 3538952 | tf_op jit(solution)/shard_map/ppermute | solution.py:683
  122.9 14.3 %collective-permute-start.19 = (bf16[16,1792]{1,0:T(8,128)(2,1)S(1)}, bf16[16,1792]{1,0:T(8,128)(2,1)S(1)}, u32[]{:S(2)}, u32[]{:S(2)}) collective-permute-start(bf16[16,1792]{1,0:T(8,128)(2,1)S(1)} %slice.316), channel_id=1, source_target_pairs={{0,16},{2,18},{4,20},{6,22},{8,24},{10,26},{12,28},{14,30},{16,4},... | collective-permute-start | bytes 172040 | tf_op jit(solution)/shard_map/ppermute | solution.py:889
  148.1 30.4 %collective-permute-start.27 = (bf16[768,768]{1,0:T(8,128)(2,1)S(1)}, bf16[768,768]{1,0:T(8,128)(2,1)}, u32[]{:S(2)}, u32[]{:S(2)}) collective-permute-start(bf16[768,768]{1,0:T(8,128)(2,1)S(1)} %bitcast.219), channel_id=1, source_target_pairs={{16,0},{17,1},{18,2},{19,3},{20,4},{21,5},{22,6},{23,7},{24,8},{25... | collective-permute-start | bytes 3538952 | tf_op jit(solution)/shard_map/ppermute | solution.py:678
  149.4 29.1 %collective-permute-start.29 = (bf16[768,768]{1,0:T(8,128)(2,1)}, bf16[768,768]{1,0:T(8,128)(2,1)}, u32[]{:S(2)}, u32[]{:S(2)}) collective-permute-start(bf16[768,768]{1,0:T(8,128)(2,1)} %collective-permute-done.28), channel_id=1, source_target_pairs={{16,0},{17,1},{18,2},{19,3},{20,4},{21,5},{22,6},{23,7},{24,8},{25... | collective-permute-start | bytes 3538952 | tf_op jit(solution)/shard_map/ppermute | solution.py:683
  206.1 19.0 %collective-permute-start.34 = (bf16[144,768]{1,0:T(8,128)(2,1)S(1)}, bf16[144,768]{1,0:T(8,128)(2,1)S(1)}, u32[]{:S(2)}, u32[]{:S(2)}) collective-permute-start(bf16[144,768]{1,0:T(8,128)(2,1)S(1)} %pad_maximum_fusion.19), channel_id=1, source_target_pairs={{4,0},{6,2},{8,4},{10,6},{12,8},{14,10},{5,1},{7,3},{9,5},{11,7},{... | collective-permute-start | bytes 663560 | tf_op jit(solution)/shard_map/ppermute | solution.py:655
  225.3 22.1 %collective-permute-start.35 = (bf16[144,768]{1,0:T(8,128)(2,1)S(1)}, bf16[144,768]{1,0:T(8,128)(2,1)S(1)}, u32[]{:S(2)}, u32[]{:S(2)}) collective-permute-start(bf16[144,768]{1,0:T(8,128)(2,1)S(1)} %pad_maximum_fusion.20), channel_id=1, source_target_pairs={{8,0},{10,2},{12,4},{14,6},{9,1},{11,3},{13,5},{15,7},{24,16},{26,... | collective-permute-start | bytes 663560 | tf_op jit(solution)/shard_map/ppermute | solution.py:655
  268.5 16.2 %collective-permute-start.38 = (bf16[2,384,1536]{2,1,0:T(8,128)(2,1)}, bf16[2,384,1536]{2,1,0:T(8,128)(2,1)}, u32[]{:S(2)}, u32[]{:S(2)}) collective-permute-start(bf16[2,384,1536]{2,1,0:T(8,128)(2,1)} %pad_maximum_fusion.5), channel_id=1, source_target_pairs={{0,16},{16,0},{1,17},{17,1},{2,18},{18,2},{3,19},{19,3},{4,20},{20... | collective-permute-start | bytes 7077896 | tf_op jit(solution)/shard_map/ppermute | solution.py:700
  283.1 19.4 %collective-permute-start.46 = (bf16[384,896]{1,0:T(8,128)(2,1)S(1)}, bf16[384,896]{1,0:T(8,128)(2,1)S(1)}, u32[]{:S(2)}, u32[]{:S(2)}) collective-permute-start(bf16[384,896]{1,0:T(8,128)(2,1)S(1)} %dynamic-slice_bitcast_fusion.5), channel_id=1, source_target_pairs={{0,1},{1,0},{2,3},{3,2},{4,5},{5,4},{6,7},{7,6},{8,9},{9,8},{10,11... | collective-permute-start | bytes 2064392 | tf_op jit(solution)/shard_map/ppermute | solution.py:705
  287.2 38.6 %collective-permute-start.39 = (bf16[384,1536]{1,0:T(8,128)(2,1)S(1)}, bf16[384,1536]{1,0:T(8,128)(2,1)S(1)}, u32[]{:S(2)}, u32[]{:S(2)}) collective-permute-start(bf16[384,1536]{1,0:T(8,128)(2,1)S(1)} %dynamic-slice_bitcast_fusion.1), channel_id=1, source_target_pairs={{0,1},{1,0},{2,3},{3,2},{4,5},{5,4},{6,7},{7,6},{8,9},{9,8},{10,11... | collective-permute-start | bytes 3538952 | tf_op jit(solution)/shard_map/ppermute | solution.py:705
  326.4 42.3 %collective-permute-start.44 = (bf16[192,1536]{1,0:T(8,128)(2,1)S(1)}, bf16[192,1536]{1,0:T(8,128)(2,1)S(1)}, u32[]{:S(2)}, u32[]{:S(2)}) collective-permute-start(bf16[192,1536]{1,0:T(8,128)(2,1)S(1)} %dynamic-slice_bitcast_fusion.7), channel_id=1, source_target_pairs={{0,2},{2,0},{4,6},{6,4},{8,10},{10,8},{12,14},{14,12},{1,3},{3,1},... | collective-permute-start | bytes 1769480 | tf_op jit(solution)/shard_map/ppermute | solution.py:715
  330.7 18.7 %collective-permute-start.41 = (bf16[144,768]{1,0:T(8,128)(2,1)S(1)}, bf16[144,768]{1,0:T(8,128)(2,1)S(1)}, u32[]{:S(2)}, u32[]{:S(2)}) collective-permute-start(bf16[144,768]{1,0:T(8,128)(2,1)S(1)} %pad_maximum_fusion.21), channel_id=1, source_target_pairs={{4,0},{6,2},{8,4},{10,6},{12,8},{14,10},{5,1},{7,3},{9,5},{11,7},{... | collective-permute-start | bytes 663560 | tf_op jit(solution)/shard_map/ppermute | solution.py:655
  353.3 15.2 %collective-permute-start.42 = (bf16[144,768]{1,0:T(8,128)(2,1)S(1)}, bf16[144,768]{1,0:T(8,128)(2,1)S(1)}, u32[]{:S(2)}, u32[]{:S(2)}) collective-permute-start(bf16[144,768]{1,0:T(8,128)(2,1)S(1)} %pad_maximum_fusion.22), channel_id=1, source_target_pairs={{8,0},{10,2},{12,4},{14,6},{9,1},{11,3},{13,5},{15,7},{24,16},{26,... | collective-permute-start | bytes 663560 | tf_op jit(solution)/shard_map/ppermute | solution.py:655
  359.9 24.9 %collective-permute-start.56 = (bf16[2,384,1536]{2,1,0:T(8,128)(2,1)}, bf16[2,384,1536]{2,1,0:T(8,128)(2,1)}, u32[]{:S(2)}, u32[]{:S(2)}) collective-permute-start(bf16[2,384,1536]{2,1,0:T(8,128)(2,1)} %pad_maximum_fusion.6), channel_id=1, source_target_pairs={{0,16},{16,0},{1,17},{17,1},{2,18},{18,2},{3,19},{19,3},{4,20},{20... | collective-permute-start | bytes 7077896 | tf_op jit(solution)/shard_map/ppermute | solution.py:700
  380.5 41.1 %all-to-all-start = ((bf16[4,48,2432]{2,1,0:T(8,128)(2,1)}), bf16[4,48,2432]{2,1,0:T(8,128)(2,1)}, u32[]{:S(2)}, u32[]{:S(2)}) async-start(bf16[4,48,2432]{2,1,0:T(8,128)(2,1)} %bitcast.221), calls=%async_computation | async-start | bytes 1867776 | tf_op jit(solution)/shard_map/all_to_all | solution.py:733
  389.6 33.3 %collective-permute-start.57 = (bf16[384,1536]{1,0:T(8,128)(2,1)}, bf16[384,1536]{1,0:T(8,128)(2,1)}, u32[]{:S(2)}, u32[]{:S(2)}) collective-permute-start(bf16[384,1536]{1,0:T(8,128)(2,1)} %dynamic-slice_bitcast_fusion), channel_id=1, source_target_pairs={{0,1},{1,0},{2,3},{3,2},{4,5},{5,4},{6,7},{7,6},{8,9},{9,8},{10,11... | collective-permute-start | bytes 3538952 | tf_op jit(solution)/shard_map/ppermute | solution.py:705
  392.5 126.1 %collective-permute-start.30 = (bf16[512,768]{1,0:T(8,128)(2,1)}, bf16[512,768]{1,0:T(8,128)(2,1)}, u32[]{:S(2)}, u32[]{:S(2)}) collective-permute-start(bf16[512,768]{1,0:T(8,128)(2,1)} %get-tuple-element.366), channel_id=1, source_target_pairs={{0,0},{2,16},{16,2},{18,18},{4,4},{6,20},{20,6},{22,22},{8,8},{10,... | collective-permute-start | bytes 2359304 | tf_op jit(solution)/shard_map/ppermute | solution.py:1023
  400.2 125.2 %collective-permute-start.31 = (bf16[512,768]{1,0:T(8,128)(2,1)}, bf16[512,768]{1,0:T(8,128)(2,1)}, u32[]{:S(2)}, u32[]{:S(2)}) collective-permute-start(bf16[512,768]{1,0:T(8,128)(2,1)} %get-tuple-element.367), channel_id=1, source_target_pairs={{0,16},{2,0},{16,18},{18,2},{4,20},{6,4},{20,22},{22,6},{8,24},{10... | collective-permute-start | bytes 2359304 | tf_op jit(solution)/shard_map/ppermute | solution.py:1024
  429.2 19.6 %collective-permute-start.58 = (bf16[2,384,896]{2,1,0:T(8,128)(2,1)}, bf16[2,384,896]{2,1,0:T(8,128)(2,1)}, u32[]{:S(2)}, u32[]{:S(2)}) collective-permute-start(bf16[2,384,896]{2,1,0:T(8,128)(2,1)} %bitcast.60), channel_id=1, source_target_pairs={{0,16},{16,0},{1,17},{17,1},{2,18},{18,2},{3,19},{19,3},{4,20},{20... | collective-permute-start | bytes 4128776 | tf_op jit(solution)/shard_map/ppermute | solution.py:700
  436.1 41.4 %collective-permute-start.51 = (f32[22,1792]{1,0:T(8,128)}, f32[22,1792]{1,0:T(8,128)}, u32[]{:S(2)}, u32[]{:S(2)}) collective-permute-start(f32[22,1792]{1,0:T(8,128)} %broadcast_select_fusion.46), channel_id=1, source_target_pairs={{0,16},{16,0},{1,17},{17,1},{2,18},{18,2},{3,19},{19,3},{4,20},{20... | collective-permute-start | bytes 473096 | tf_op jit(solution)/shard_map/ppermute | solution.py:1004
  439.4 15.8 %collective-permute-start.60 = (bf16[192,1536]{1,0:T(8,128)(2,1)}, bf16[192,1536]{1,0:T(8,128)(2,1)}, u32[]{:S(2)}, u32[]{:S(2)}) collective-permute-start(bf16[192,1536]{1,0:T(8,128)(2,1)} %dynamic-slice_bitcast_fusion.6), channel_id=1, source_target_pairs={{0,2},{2,0},{4,6},{6,4},{8,10},{10,8},{12,14},{14,12},{1,3},{3,1},... | collective-permute-start | bytes 1769480 | tf_op jit(solution)/shard_map/ppermute | solution.py:715
  442.4 27.7 %all-to-all-start.1 = ((bf16[4,48,2432]{2,1,0:T(8,128)(2,1)}), bf16[4,48,2432]{2,1,0:T(8,128)(2,1)}, u32[]{:S(2)}, u32[]{:S(2)}) async-start(bf16[4,48,2432]{2,1,0:T(8,128)(2,1)} %broadcast_in_dim.190), calls=%async_computation.1 | async-start | bytes 1867776 | tf_op jit(solution)/shard_map/all_to_all | solution.py:740
  450.6 17.1 %collective-permute-start.59 = (bf16[384,896]{1,0:T(8,128)(2,1)S(1)}, bf16[384,896]{1,0:T(8,128)(2,1)S(1)}, u32[]{:S(2)}, u32[]{:S(2)}) collective-permute-start(bf16[384,896]{1,0:T(8,128)(2,1)S(1)} %dynamic-slice_bitcast_fusion.4), channel_id=1, source_target_pairs={{0,1},{1,0},{2,3},{3,2},{4,5},{5,4},{6,7},{7,6},{8,9},{9,8},{10,11... | collective-permute-start | bytes 2064392 | tf_op jit(solution)/shard_map/ppermute | solution.py:705
  470.1 18.9 %all-to-all-start.2 = ((bf16[4,48,1536]{2,1,0:T(8,128)(2,1)}), bf16[4,48,1536]{2,1,0:T(8,128)(2,1)S(1)}, u32[]{:S(2)}, u32[]{:S(2)}) async-start(bf16[4,48,1536]{2,1,0:T(8,128)(2,1)} %bitcast.70), calls=%async_computation.2 | async-start | bytes 1179648 | tf_op jit(solution)/shard_map/all_to_all | solution.py:733
  479.1 16.1 %collective-permute-start.52 = (f32[22,1792]{1,0:T(8,128)}, f32[22,1792]{1,0:T(8,128)S(1)}, u32[]{:S(2)}, u32[]{:S(2)}) collective-permute-start(f32[22,1792]{1,0:T(8,128)} %select_add_fusion), channel_id=1, source_target_pairs={{0,1},{1,0},{2,3},{3,2},{4,5},{5,4},{6,7},{7,6},{8,9},{9,8},{10,11... | collective-permute-start | bytes 473096 | tf_op jit(solution)/shard_map/ppermute | solution.py:749
  489.1 31.9 %all-to-all-start.4 = ((bf16[4,48,896]{2,1,0:T(8,128)(2,1)}), bf16[4,48,896]{2,1,0:T(8,128)(2,1)S(1)}, u32[]{:S(2)}, u32[]{:S(2)}) async-start(bf16[4,48,896]{2,1,0:T(8,128)(2,1)} %bitcast.72), calls=%async_computation.4 | async-start | bytes 688128 | tf_op jit(solution)/shard_map/all_to_all | solution.py:733
  493.6 37.6 %collective-permute-start.50 = (bf16[512,768]{1,0:T(8,128)(2,1)}, bf16[512,768]{1,0:T(8,128)(2,1)S(1)}, u32[]{:S(2)}, u32[]{:S(2)}) collective-permute-start(bf16[512,768]{1,0:T(8,128)(2,1)} %broadcast_select_fusion.28), channel_id=1, source_target_pairs={{0,16},{2,0},{16,18},{18,2},{4,20},{6,4},{20,22},{22,6},{8,24},{10... | collective-permute-start | bytes 2359304 | tf_op jit(solution)/shard_map/ppermute | solution.py:1024
  493.6 37.6 %collective-permute-start.49 = (bf16[512,768]{1,0:T(8,128)(2,1)S(1)}, bf16[512,768]{1,0:T(8,128)(2,1)}, u32[]{:S(2)}, u32[]{:S(2)}) collective-permute-start(bf16[512,768]{1,0:T(8,128)(2,1)S(1)} %copy-done.93), channel_id=1, source_target_pairs={{0,0},{2,16},{16,2},{18,18},{4,4},{6,20},{20,6},{22,22},{8,8},{10,... | collective-permute-start | bytes 2359304 | tf_op jit(solution)/shard_map/ppermute | solution.py:1023
  496.1 22.5 %collective-permute-start.53 = (f32[22,1792]{1,0:T(8,128)S(1)}, f32[22,1792]{1,0:T(8,128)S(1)}, u32[]{:S(2)}, u32[]{:S(2)}) collective-permute-start(f32[22,1792]{1,0:T(8,128)S(1)} %add.332), channel_id=1, source_target_pairs={{0,2},{2,0},{4,6},{6,4},{8,10},{10,8},{12,14},{14,12},{1,3},{3,1},... | collective-permute-start | bytes 473096 | tf_op jit(solution)/shard_map/ppermute | solution.py:749
  518.6 31.6 %collective-permute-start.63 = (bf16[192,2432]{1,0:T(8,128)(2,1)}, bf16[192,2432]{1,0:T(8,128)(2,1)}, u32[]{:S(2)}, u32[]{:S(2)}) collective-permute-start(bf16[192,2432]{1,0:T(8,128)(2,1)} %bitcast.63), channel_id=1, source_target_pairs={{0,2},{2,0},{4,6},{6,4},{8,10},{10,8},{12,14},{14,12},{1,3},{3,1},... | collective-permute-start | bytes 2801672 | tf_op jit(solution)/shard_map/ppermute | solution.py:721
  521.8 23.8 %all-to-all-start.3 = ((bf16[4,48,1536]{2,1,0:T(8,128)(2,1)}), bf16[4,48,1536]{2,1,0:T(8,128)(2,1)S(1)}, u32[]{:S(2)}, u32[]{:S(2)}) async-start(bf16[4,48,1536]{2,1,0:T(8,128)(2,1)} %broadcast_in_dim.191), calls=%async_computation.3 | async-start | bytes 1179648 | tf_op jit(solution)/shard_map/all_to_all | solution.py:740
  528.3 17.2 %collective-permute-start.55 = (f32[22,1792]{1,0:T(8,128)S(1)}, f32[22,1792]{1,0:T(8,128)S(1)}, u32[]{:S(2)}, u32[]{:S(2)}) collective-permute-start(f32[22,1792]{1,0:T(8,128)S(1)} %add.334), channel_id=1, source_target_pairs={{0,8},{2,10},{4,12},{6,14},{8,0},{10,2},{12,4},{14,6},{1,9},{3,11}... | collective-permute-start | bytes 473096 | tf_op jit(solution)/shard_map/ppermute | solution.py:749
  549.9 16.0 %collective-permute-start.62 = (bf16[192,1536]{1,0:T(8,128)(2,1)S(1)}, bf16[192,1536]{1,0:T(8,128)(2,1)S(1)}, u32[]{:S(2)}, u32[]{:S(2)}) collective-permute-start(bf16[192,1536]{1,0:T(8,128)(2,1)S(1)} %bitcast.226), channel_id=1, source_target_pairs={{0,2},{2,0},{4,6},{6,4},{8,10},{10,8},{12,14},{14,12},{1,3},{3,1},... | collective-permute-start | bytes 1769480 | tf_op jit(solution)/shard_map/ppermute | solution.py:721
  (140 other events, 1172.7 us)

commit v2 on v1

--- a/solution.py
+++ b/solution.py
@@ -341,7 +341,7 @@
 def conv_back_kernel(
     outg_ref, inc_ref, q_ref, ds_ref, dt_ref, all_ref, col_ref, e_ref, rc_ref, halo_ref,
     dy_ref, dx_ref, dbc_ref, hs_ref, par_ref, sp_ref,
-    dre_ref, tail_ref, back_ref, dw_ref, dh_ref, pre_ref, sum_ref,
+    dr_ref, de_ref, tail_ref, back_ref, dw_ref, dh_ref, pre_ref, sum_ref,
 ):
     count = q_ref.shape[0] // Q
     spread = sp_ref[...]
@@ -388,7 +388,7 @@
         later = later + sums[0:1]
         ddt = rate * dlog + sum_ref[rows, 128:]
         de = ddt * jax.nn.sigmoid(e_ref[rows, :] + bias)
-        dre_ref[rows, CONVCH:] = jnp.where(iota((Q, 128), 1) < H, de, 0.0).astype(bf16)
+        de_ref[rows, :] = jnp.where(iota((Q, 128), 1) < H, de, 0.0).astype(bf16)
         rate_total = rate_total + jnp.sum(dlog * dt_ref[rows, :], axis=0, keepdims=True)
         bias_total = bias_total + jnp.sum(de, axis=0, keepdims=True)
     row = iota((8, 128), 0)
@@ -425,7 +425,7 @@
                     same[0:Q] * window[16 - d : 16 + Q - d], axis=0, keepdims=True
                 )
                 grad = grad + taps[d] * same[d : d + Q]
-            dre_ref[rows, lanes] = grad.astype(bf16)
+            dr_ref[rows, lanes] = grad.astype(bf16)
             if c == count - 1:
                 tail_ref[:, lanes] = grad[Q - 8 :]
         row = iota((8, 128), 0)
@@ -594,7 +594,8 @@
 def conv_backward(outg, inc, q, ds, dt, total, col, e, rc, halo, dy, dx, dbc, hs, par, spread):
     rows = q.shape[0]
     outs = (
-        shape(rows, CONVCH + 128, dtype=bf16),
+        shape(rows, CONVCH, dtype=bf16),
+        shape(rows, 128, dtype=bf16),
         shape(8, CONVCH),
         shape(8, CONVCH),
         shape(8, CONVCH),
@@ -628,10 +629,6 @@
 
 def combine(earlier, later):
     return (earlier[0] * later[0], later[0] * earlier[1] + later[1])
-
-
-def after(arrays, event):
-    return lax.optimization_barrier((tuple(arrays), event))[0]
 
 
 def chain_scan(pack, reverse, beside):
@@ -647,16 +644,21 @@
     before = None
     distance = 2
     results = []
+    other = None
     while distance < size:
         route = [(i, i + distance) for i in range(size - distance)]
         if reverse:
             route = [(b, a) for a, b in route]
         sent = pack_up(reached, pack.dtype)
-        arrived = lax.ppermute(sent, "seq", route)
         if beside:
-            needed, other = beside.pop(0)(sent)
+            arrays, work = beside.pop(0)
+            sent, arrays = tie(sent, arrays)
+            arrived = lax.ppermute(sent, "seq", route)
+            needed, other = work(other, *arrays)
             arrived, needed = tie(arrived, needed)
             results.append((needed, other))
+        else:
+            arrived = lax.ppermute(sent, "seq", route)
         arrived = unpack(arrived)
         before = arrived if before is None else combine(arrived, before)
         reached = combine(arrived, reached)
@@ -670,35 +672,34 @@
     return incoming, results
 
 
-def spread_layer(shard, layer):
+def move_rows(shard, layer):
+    parts = lax.axis_size("fsdp")
+    blocks = [shard]
+    for shift in range(1, parts):
+        route = [(layer * parts + i, layer * parts + (i + shift) % parts) for i in range(parts)]
+        blocks.append(lax.ppermute(shard, ("section", "fsdp"), route))
+    return blocks
+
+
+def share(blocks, layer):
     section, row = lax.axis_index("section"), lax.axis_index("fsdp")
     parts = lax.axis_size("fsdp")
-    here = section == layer
     across = [(layer, 1 - layer)]
-    own = pick(here, shard, lax.ppermute(shard, "section", across))
-    blocks = []
-    for shift in range(1, parts):
-        route = [(layer * parts + i, layer * parts + (i + shift) % parts) for i in range(parts)]
-        moved = lax.ppermute(shard, ("section", "fsdp"), route)
-        blocks.append(pick(here, moved, lax.ppermute(moved, "section", across)))
-    blocks = [own] + blocks
+    blocks = [pick(section == layer, block, lax.ppermute(block, "section", across)) for block in blocks]
     if parts == 2:
         low = row == 0
-        return jnp.concatenate([pick(low, blocks[0], blocks[1]), pick(low, blocks[1], blocks[0])], axis=0)
+        return [pick(low, blocks[0], blocks[1]), pick(low, blocks[1], blocks[0])]
     ordered = []
     for k in range(parts):
         block = blocks[0]
         for shift in range(1, parts):
             block = pick((row - shift) % parts == k, blocks[shift], block)
         ordered.append(block)
-    return jnp.concatenate(ordered, axis=0)
-
-
-def fold(make):
-    section, row = lax.axis_index("section"), lax.axis_index("fsdp")
-    parts = lax.axis_size("fsdp")
-    got = lax.ppermute(make(1 - section).astype(bf16), "section", SWAP)
-    summed = (make(section) + got.astype(f32)).astype(bf16)
+    return ordered
+
+
+def row_sum(summed):
+    row, parts = lax.axis_index("fsdp"), lax.axis_size("fsdp")
     if parts == 2:
         kept = lax.dynamic_index_in_dim(summed, row, 0, keepdims=False)
         given = lax.dynamic_index_in_dim(summed, 1 - row, 0, keepdims=False)
@@ -707,95 +708,88 @@
     return lax.psum_scatter(summed, "fsdp", scatter_dimension=0, tiled=False)
 
 
-def pair_sum(array):
-    size, bit = lax.axis_size("seq"), lax.axis_index("seq") % 2
+def halve(array, distance):
+    size, bit = lax.axis_size("seq"), (lax.axis_index("seq") // distance) % 2
     halves = array.reshape(2, -1, array.shape[1])
     kept = lax.dynamic_index_in_dim(halves, bit, 0, keepdims=False)
     given = lax.dynamic_index_in_dim(halves, 1 - bit, 0, keepdims=False)
-    got = lax.ppermute(given, "seq", [(i, i ^ 1) for i in range(size)])
+    got = lax.ppermute(given, "seq", [(i, i ^ distance) for i in range(size)])
     return (kept.astype(f32) + got.astype(f32)).astype(bf16)
 
 
-def pair_collect(array):
-    size, low = lax.axis_size("seq"), lax.axis_index("seq") % 2 == 0
-    got = lax.ppermute(array, "seq", [(i, i ^ 1) for i in range(size)])
+def rejoin(array, distance):
+    size, low = lax.axis_size("seq"), (lax.axis_index("seq") // distance) % 2 == 0
+    got = lax.ppermute(array, "seq", [(i, i ^ distance) for i in range(size)])
     return jnp.concatenate([pick(low, array, got), pick(low, got, array)], axis=0)
 
 
-def strides():
-    size = lax.axis_size("seq")
-    return [[i for i in range(size) if i % 2 == b] for b in range(2)]
-
-
-def scatter_sum(array):
-    count = lax.axis_size("seq") // 2
-    blocks = array.reshape(count, -1, array.shape[1])
-    got = lax.all_to_all(blocks, "seq", 0, 0, axis_index_groups=strides())
-    return jnp.sum(got.astype(f32), axis=0).astype(bf16)
-
-
-def collect(part):
-    count = lax.axis_size("seq") // 2
-    everyone = jnp.broadcast_to(part[None], (count,) + part.shape)
-    got = lax.all_to_all(everyone, "seq", 0, 0, axis_index_groups=strides())
-    return got.reshape(-1, part.shape[1])
-
-
-def sum_everywhere(array):
+def distances():
+    found = [1]
+    while 2 * found[-1] < lax.axis_size("seq"):
+        found.append(2 * found[-1])
+    return found
+
+
+def exchanges():
+    found = []
     for axis in ("fsdp", "seq"):
-        size = lax.axis_size(axis)
         distance = 1
-        while distance < size:
-            array = array + lax.ppermute(array, axis, [(i, i ^ distance) for i in range(size)])
+        while distance < lax.axis_size(axis):
+            found.append((axis, distance))
             distance *= 2
-    return array
+    return found
+
+
+def exchange_sum(array, step):
+    axis, distance = step
+    partners = [(i, i ^ distance) for i in range(lax.axis_size(axis))]
+    return array + lax.ppermute(array, axis, partners)
 
 
 def tie(*arrays):
     return lax.optimization_barrier(arrays)
 
 
-def place_kernel(section_ref, early_ref, early_got_ref, late_ref, late_got_ref, e_ref, in_ref, out_ref):
+def place_kernel(
+    section_ref, early_ref, early_got_ref, late_ref, late_got_ref, e_ref, in_ref, out_ref
+):
     low = section_ref[0] == 0
-    early, early_got = early_ref[...].astype(f32), early_got_ref[...].astype(f32)
-    late, late_got = late_ref[...].astype(f32), late_got_ref[...].astype(f32)
+    conv_rows = CONVCH // 2
     for half in range(2):
         own = low if half == 0 else jnp.logical_not(low)
-        both = jnp.where(own, early, early_got)
-        in_ref[:, half * HALF : (half + 1) * HALF] = both[:, :HALF]
-        for k in range(2):
-            at = HALF + k * (D // 2)
-            out_ref[k, :, half * (D // 2) : (half + 1) * (D // 2)] = both[:, at : at + D // 2]
-        at = DI + half * (CONVCH // 2)
-        in_ref[:, at : at + CONVCH // 2] = jnp.where(own, late, late_got)
-    in_ref[:, DI + CONVCH :] = e_ref[:, :H]
-
-
-def place(early, early_got, late, late_got, e):
-    rows = early.shape[0]
-    size = rows // 4
-
-    def by_row(width):
-        return pl.BlockSpec((size, width), lambda i: (i, 0))
-
-    section = lax.axis_index("section").astype(jnp.int32)[None]
-    width = DI + CONVCH + H
-    w_in, w_out = pl.pallas_call(
-        place_kernel,
-        grid=(4,),
-        in_specs=[
-            pl.BlockSpec(memory_space=pltpu.SMEM),
-            by_row(DI),
-            by_row(DI),
-            by_row(CONVCH // 2),
-            by_row(CONVCH // 2),
-            by_row(128),
-        ],
-        out_specs=(by_row(width), pl.BlockSpec((2, size, D), lambda i: (0, i, 0))),
-        out_shape=(shape(rows, width), shape(2, rows, D)),
-        compiler_params=params(1),
-    )(section, early, early_got, late, late_got, e)
-    return w_in[None], w_out.reshape(1, 2 * rows, D)
+
+        def block(ref, got_ref, start, count):
+            rows = slice(start, start + count)
+            return jnp.where(own, ref[rows, :], got_ref[rows, :]).astype(f32)
+
+        in_ref[half * HALF : (half + 1) * HALF, :] = block(early_ref, early_got_ref, 0, HALF)
+        lanes = slice(half * (D // 2), (half + 1) * (D // 2))
+        out_ref[:, lanes] = block(early_ref, early_got_ref, HALF, HALF)
+        at = DI + half * conv_rows
+        in_ref[at : at + conv_rows, :] = block(late_ref, late_got_ref, 0, conv_rows)
+    in_ref[DI + CONVCH :, :] = e_ref[...]
+
+
+def place(early, early_got, late, late_got, e, rows_out):
+    section = lax.axis_index("section")
+    width = early.shape[1]
+    if rows_out == HALF:
+        vmem = pl.BlockSpec(memory_space=pltpu.VMEM)
+        w_in, w_out = pl.pallas_call(
+            place_kernel,
+            in_specs=[pl.BlockSpec(memory_space=pltpu.SMEM)] + [vmem] * 5,
+            out_shape=(shape(DI + CONVCH + H, width), shape(rows_out, D)),
+            compiler_params=params(0),
+        )(section.astype(jnp.int32)[None], early, early_got, late, late_got, e)
+        return w_in.T[None], w_out[None]
+    gates, convs, backs = [], [], []
+    for half in range(2):
+        array = pick(section == half, early, early_got).astype(f32)
+        gates.append(array[:HALF])
+        backs += [array[at : at + rows_out] for at in range(HALF, 2 * HALF, rows_out)]
+        convs.append(pick(section == half, late, late_got).astype(f32))
+    w_in = jnp.concatenate(gates + convs + [e], axis=0)
+    return w_in.T[None], jnp.concatenate(backs, axis=1)[None]
 
 
 def labels(lengths, order, base, rows):
@@ -840,25 +834,35 @@
         own = lax.dynamic_index_in_dim(array[:, 0], section, 0, keepdims=False)
         return pick(aligned, own, lax.ppermute(given, everywhere, exchange))
 
-    first_in, first_z, first_out = w_in[0, :, DI:], w_in[0, :, :DI], w_out[0]
-
-    def projection(shard, layer):
-        return jnp.pad(spread_layer(shard, layer), ((0, 0), (0, CONVCH + 128 - shard.shape[1])))
-
-    w_conv = [projection(first_in, 0), None]
+    turned = w_in[0].T
+    shard_conv = jnp.pad(turned[DI:], ((0, 8), (0, 0)))
+    width = turned.shape[1]
+    rows_out = w_out.shape[1]
+    pieces = [w_out[0, :, k * width : (k + 1) * width] for k in range(D // width)]
+    shard_rest = jnp.concatenate([turned[:DI]] + pieces, axis=0)
+
+    def join_conv(blocks):
+        whole_rows = jnp.concatenate([block[: CONVCH + 32] for block in blocks], axis=1)
+        return whole_rows[:CONVCH], jnp.pad(whole_rows[CONVCH:], ((0, 96), (0, 0)))
+
+    def join_rest(blocks):
+        gate = jnp.concatenate([block[:DI] for block in blocks], axis=1)
+        back = [
+            jnp.concatenate(
+                [block[at : at + rows_out] for at in range(DI, block.shape[0], rows_out)], axis=1
+            )
+            for block in blocks
+        ]
+        return gate, jnp.concatenate(back, axis=0)
+
+    w_conv, w_step, w_gate, w_back = [[None, None] for _ in range(4)]
+    blocks = move_rows(shard_conv, 0)
     hidden = to_chain(tokens)
-    second_in, second_z, second_out, w_first = lax.optimization_barrier(
-        (first_in, first_z, first_out, w_conv[0])
-    )
-    w_conv[0] = w_first
-    w_gate = [spread_layer(second_z, 0), None]
-    w_back = [spread_layer(second_out, 0), None]
-    third_in, third_z, third_out, w_back[0] = lax.optimization_barrier(
-        (second_in, second_z, second_out, w_back[0])
-    )
-    w_conv[1] = projection(third_in, 1)
-    w_gate[1] = spread_layer(third_z, 1)
-    w_back[1] = spread_layer(third_out, 1)
+    blocks = share(blocks, 0)
+    shard_conv, shard_rest, blocks, cotangent = tie(shard_conv, shard_rest, blocks, cotangent)
+    w_conv[0], w_step[0] = join_conv(blocks)
+    moved_rest = move_rows(shard_rest, 0)
+
     top_grad = to_chain(cotangent)
 
     table = parameter_table(
@@ -877,30 +881,59 @@
     ]
     precede = [(b, a) for a, b in follow]
 
+    def to_holders(array, layer):
+        return tuple(
+            lax.ppermute(
+                array,
+                everywhere,
+                [
+                    (flat(s, 2 * k + m), flat(layer, 2 * k + s))
+                    for k in range(size // 2)
+                    for s in range(2)
+                ],
+            )
+            for m in range(2)
+        )
+
+    def held(first, second):
+        stacked = jnp.stack([pick(low, first[m], second[m]) for m in range(2)])
+        return stacked[None, :, None]
+
     kept = []
     results = []
     for layer in range(2):
         par = tables[layer]
+        if layer == 1:
+            w_conv[1], w_step[1] = join_conv(second_conv)
         wide = hidden.astype(f32)
         scale = lax.rsqrt(jnp.mean(wide * wide, axis=1, keepdims=True) + epsilon)
         u = (wide * scale * par[NORM : NORM + 1, :D]).astype(bf16)
-        rc = nn(u, w_conv[layer][:, :CONVCH]).astype(bf16)
-        e = nn(u, w_conv[layer][:, CONVCH:])
+        rc = nt(u, w_conv[layer]).astype(bf16)
+        e = nt(u, w_step[layer])
         halo = lax.ppermute(rc[rows - 16 :], everywhere, follow)
         q, ds, dt, cum, total, lin, pack = conv_forward(
             rc, halo, e, col, par, spread
         )
-        inc, ((y0, _), (z, _)) = chain_scan(
+        def beside_first(_, shards, *arrays):
+            following = move_rows(shards, 1) if layer == 0 else ()
+            return intra_forward(*arrays, spread), following
+
+        def beside_second(following, moved, u):
+            gate, back = join_rest(share(moved, layer))
+            return nt(u, gate), (gate, back, following)
+
+        inc, ((y0, _), (z, (w_gate[layer], w_back[layer], following))) = chain_scan(
             pack,
             False,
             [
-                lambda sent: (
-                    intra_forward(*after((q, dt, cum, col, lab, lin, par), sent), spread),
-                    None,
-                ),
-                lambda sent: (nn(*after((u, w_gate[layer]), sent)), None),
+                ((shard_conv, q, dt, cum, col, lab, lin, par), beside_first),
+                ((moved_rest, u), beside_second),
             ],
         )
+        if layer == 0:
+            inc, following, shard_rest, top_grad = tie(inc, following, shard_rest, top_grad)
+            second_conv = share(following, 1)
+            moved_rest = move_rows(shard_rest, 1)
         y, v, out = gate_forward(
             y0, z, q, total, col, inc, par, w_back[layer], hidden, spread
         )
@@ -917,71 +950,103 @@
         width = array.shape[1] // 2
         return lax.dynamic_slice_in_dim(array, half * width, width, axis=1)
 
+    def by_part(array):
+        width = D // parts
+        return jnp.stack([array[:, k * width : (k + 1) * width] for k in range(parts)])
+
     def early_grads(u, dz, v, grad):
         def make(half):
-            for_in = columns(u, half_of(dz, half)).reshape(parts, -1, HALF)
-            for_out = columns(v, half_of(grad, half)).reshape(parts, 2, -1, D // 2)
-            return jnp.concatenate([for_in, for_out[:, 0], for_out[:, 1]], axis=2)
+            for_in = by_part(columns(half_of(dz, half), u))
+            for_out = columns(v, half_of(grad, half)).reshape(parts, -1, D // 2)
+            step = D // parts
+            pieces = [for_out[:, :, at : at + step] for at in range(0, D // 2, step)]
+            return jnp.concatenate([for_in] + pieces, axis=1)
 
         return make
 
     def late_grads(u, dr):
-        return lambda half: columns(u, half_of(dr, half)).reshape(parts, -1, CONVCH // 2)
+        return lambda half: by_part(columns(half_of(dr, half), u))
 
     grad = top_grad
-    input_grads = [None, None]
     early = [None, None]
     late = [None, None]
-    small = [None, None]
+    pieces = [None, None]
+    acts = [None, None]
+    grads = [None, None]
     for layer in (1, 0):
         par = tables[layer]
         hidden, scale, u, rc, e, halo, q, ds, dt, cum, total, lin, pack, inc, z, y, v = kept[layer]
         dy, dz, dgain, back = gate_backward(
             grad, w_back[layer], y, z, par, q, total, col, pack, spread
         )
+        extra = ()
         if layer == 0:
-            early[1], back = tie(early[1], back)
-            early[1] = pair_sum(early[1])
-
-        def beside_first(sent):
-            needed = intra_backward(
-                *after((q, dt, cum, total, col, lab, lin, inc, dy, y, par), sent), spread
-            )
-            return needed, None
-
-        def beside_second(sent):
-            a, b, c, d = after((v, u, grad, dz), sent)
-            ahead = None
+            back, early[1], late[1] = tie(back, early[1], late[1])
+            extra = late[1]
+        given = early_grads(u, dz, v, grad)(1 - section).astype(bf16)
+
+        def first(_, extra, given, *arrays):
             if layer == 0:
-                ahead = pair_sum(tie(late[1], early[1], sent)[0])
-            return nt(d, w_gate[layer]), (fold(early_grads(b, d, a, c)), ahead)
-
-        outg, (((dx, dbc, hs), _), (du, (early[layer], ahead))) = chain_scan(
-            back, True, [beside_first, beside_second]
+                extra = halve(extra, 1)
+            got = lax.ppermute(given, "section", SWAP)
+            return (intra_backward(*arrays, spread), extra, got), None
+
+        def second(_, u, dz, v, grad):
+            return (nn(dz, w_gate[layer]), early_grads(u, dz, v, grad)(section)), None
+
+        outg, ((((dx, dbc, hs), extra, got), _), ((du, kept_half), _)) = chain_scan(
+            back,
+            True,
+            [
+                ((extra, given, q, dt, cum, total, col, lab, lin, inc, dy, y, par), first),
+                ((u, dz, v, grad), second),
+            ],
         )
+        summed = (kept_half + got.astype(f32)).astype(bf16)
+        early[layer] = row_sum(summed)
         if layer == 0:
-            outg, first, second = tie(outg, early[1], ahead)
-            upper = scatter_sum(jnp.concatenate([first, second], axis=1))
-        dre, tail, front, dw, dh = conv_backward(
+            outg, extra, holding = tie(outg, extra, holding)
+            upper = halve(jnp.concatenate([early[1], extra], axis=0), 2)
+            grads[1] = to_holders(holding, 1)
+        else:
+            outg, results = tie(outg, results)
+            acts = [to_holders(results[k], k) for k in range(2)]
+        dr, de, tail, front, dw, dh = conv_backward(
             outg, inc, q, ds, dt, total, col_padded, e, rc, halo, dy, dx, dbc, hs, par, spread
         )
+        if layer == 1:
+            front, early[1] = tie(front, early[1])
+            early[1] = halve(early[1], 1)
         returned = lax.ppermute(front, everywhere, precede)
-        dre = lax.dynamic_update_slice(dre, (tail + returned).astype(bf16), (rows - 8, 0))
-        du = du + nt(dre, w_conv[layer])
+        if layer == 0:
+            returned, pieces[1], upper = tie(returned, pieces[1], upper)
+            upper = halve(upper, 4) if size > 4 else upper
+        dr = lax.dynamic_update_slice(dr, (tail + returned).astype(bf16), (rows - 8, 0))
+        given = late_grads(u, dr)(1 - section).astype(bf16)
+        given, dr, de = tie(given, dr, de)
+        got = lax.ppermute(given, "section", SWAP)
+        summed = (late_grads(u, dr)(section) + got.astype(f32)).astype(bf16)
+        if layer == 0:
+            summed, early[0], grads[1] = tie(summed, early[0], grads[1])
+            early[0] = halve(early[0], 1)
+        late[layer] = row_sum(summed)
+        du = du + nn(dr, w_conv[layer]) + nn(de, w_step[layer])
         wide = hidden.astype(f32)
         normed = wide * scale
         dn = du * par[NORM : NORM + 1, :D]
         dnorm = jnp.sum(du * normed, axis=0)
         dhidden = scale * (dn - normed * jnp.mean(dn * normed, axis=1, keepdims=True))
-        grad_e = columns(dre[:, CONVCH:], u)[:H].reshape(H // 2, 2 * D)
-        if layer == 0:
-            dre, upper, early[0] = tie(dre, upper, early[0])
-            upper = collect(upper)
-            early[0] = pair_sum(early[0])
-        late[layer] = fold(late_grads(u, dre[:, :CONVCH]))
+        grad_e = columns(de, u)[:H].reshape(H // 2, 2 * D)
         grad = (grad.astype(f32) + dhidden).astype(bf16)
-        input_grads[layer] = grad
-        small[layer] = jnp.concatenate(
+        if layer == 1:
+            grad, acts = tie(grad, acts)
+            holding = grad
+        else:
+            grads[0] = to_holders(grad, 0)
+        pieces[layer] = (dw, dnorm, dgain, dh, grad_e)
+
+    def table_of(dw, dnorm, dgain, dh, grad_e):
+        return jnp.concatenate(
             [
                 dw[: CONV + 1],
                 jnp.pad(dnorm, (0, CONVCH - D))[None],
@@ -991,45 +1056,40 @@
             ],
             axis=0,
         )
-    late[0], upper, early[0] = tie(late[0], upper, early[0])
-    early[0] = scatter_sum(early[0])
-    late[0] = pair_sum(late[0])
-    upper = pair_collect(upper)
-    early[1], late[1] = upper[:, :DI], upper[:, DI:]
-    late[0], early[0] = tie(late[0], early[0])
-    late[0] = pair_collect(collect(scatter_sum(late[0])))
-    early[0] = pair_collect(collect(early[0]))
+
+    steps = exchanges()
+    small = [table_of(*pieces[layer]) for layer in range(2)]
+    mine = pick(low, small[0], small[1]) + lax.ppermute(pick(low, small[1], small[0]), "section", SWAP)
+    mine = exchange_sum(mine, steps[0])
+    late[0], early[0], mine, grads[0], upper = tie(late[0], early[0], mine, grads[0], upper)
+    far = distances()
+    late[0] = halve(late[0], 1)
+    mine = exchange_sum(mine, steps[1])
+    late[0], mine = tie(late[0], mine)
+    for distance in far[3:]:
+        upper = halve(upper, distance)
+    for distance in far[1:]:
+        late[0] = halve(late[0], distance)
+        early[0] = halve(early[0], distance)
+    for step in steps[2:]:
+        mine = exchange_sum(mine, step)
+    for distance in reversed(far[1:]):
+        late[0] = rejoin(late[0], distance)
+        early[0] = rejoin(early[0], distance)
+        upper = rejoin(upper, distance)
+    late[0] = rejoin(late[0], 1)
+    early[0] = rejoin(early[0], 1)
+    split_at = early[0].shape[0] // 2
+    early[1], late[1] = rejoin(upper[:split_at], 1), rejoin(upper[split_at:], 1)
     early_got = lax.ppermute(pick(low, early[1], early[0]), "section", SWAP)
     late_got = lax.ppermute(pick(low, late[1], late[0]), "section", SWAP)
-    mine = pick(low, small[0], small[1]) + lax.ppermute(pick(low, small[1], small[0]), "section", SWAP)
-    mine = sum_everywhere(mine)
-    grad_e = mine[SKIP + 1 :, : 2 * D].reshape(H, parts, D // parts)
-    grad_e = lax.dynamic_index_in_dim(grad_e, lax.axis_index("fsdp"), 1, keepdims=False).T
-    shard_in, shard_out = place(
-        pick(low, early[0], early[1]),
-        early_got,
-        pick(low, late[0], late[1]),
-        late_got,
-        jnp.pad(grad_e, ((0, 0), (0, 128 - H))),
-    )
-
-    def to_holders(first, second):
-        even = micro == 0
-        one, two = [], []
-        for k in range(size // 2):
-            for s in range(2):
-                one += [(flat(s, 2 * k), flat(0, 2 * k + s)), (flat(s, 2 * k + 1), flat(1, 2 * k + s))]
-                two += [(flat(s, 2 * k), flat(1, 2 * k + s)), (flat(s, 2 * k + 1), flat(0, 2 * k + s))]
-        got_one = lax.ppermute(pick(even, first, second), everywhere, one)
-        got_two = lax.ppermute(pick(even, second, first), everywhere, two)
-        stacked = jnp.stack([pick(low, got_one, got_two), pick(low, got_two, got_one)])
-        return stacked[None, :, None]
-
-    activations = to_holders(results[0], results[1])
-    grads = to_holders(input_grads[0], input_grads[1])
+    early_own, late_own = pick(low, early[0], early[1]), pick(low, late[0], late[1])
+    grad_e = mine[SKIP + 1 :, : 2 * D].reshape(H, D)
+    grad_e = lax.dynamic_slice_in_dim(grad_e, lax.axis_index("fsdp") * width, width, axis=1)
+    shard_in, shard_out = place(early_own, early_got, late_own, late_got, grad_e, rows_out)
     return (
-        activations,
-        grads,
+        held(*acts),
+        held(*grads),
         mine[NORM : NORM + 1, :D],
         shard_in,
         mine[None, :CONV],

time: 602 us -> 591 us (0.982)
  starting transfers between devices: 146 us -> 137 us
  waiting for transfers between devices: 139 us -> 148 us
    all_to_all x6 -> x0, starting transfers between devices: 22.6 us -> none  [the longest x3 11.3 us: collect(): got = lax.all_to_all(everyone, 'seq', 0, 0, axis_index_groups=strides())]
    ppermute x41 -> x52, waiting for transfers between devices: 102 us -> 121 us  [the longest x10 41.9 us: rejoin(): got = lax.ppermute(array, 'seq', [(i, i ^ distance) for i in range(size)])]
    ppermute x41 -> x52, starting transfers between devices: 71.7 us -> 82.1 us  [the longest x8 19.9 us: to_holders(): lax.ppermute(array, everywhere, [(flat(s, 2 * k + m), flat(layer, 2 * k +...]
    all_to_all x6 -> x0, waiting for transfers between devices: 8.68 us -> none  [the longest x3 6.74 us: collect(): got = lax.all_to_all(everyone, 'seq', 0, 0, axis_index_groups=strides())]
    select_n x27 -> x29, other arithmetic: 24.3 us -> 16.9 us  [pick(): return jnp.where(first, a, b)]
    ppermute x8, starting transfers between devices: 20.1 us -> 26.5 us  [chain_scan(): arrived = lax.ppermute(sent, 'seq', route)]
    ppermute x2, starting transfers between devices: 13.9 us -> 7.55 us  [local(): halo = lax.ppermute(rc[rows - 16:], everywhere, follow)]
    unnamed x231 -> x317, local copies, waits for them, and re-layouts: 23.7 us -> 26.8 us
  transfers between devices with their start and end apart: 73 -> 78, of which waited for: 19 -> 27; matrix products, arithmetic and copies ran while one was open for 21% -> 18% of each run, Pallas kernels for 18% -> 20%
where the time goes in v2:
time: 591 us; the launch traced here: 583 us
  waiting for transfers between devices  148 us (25%)
  Pallas kernels  140 us (24%)
  starting transfers between devices  137 us (23%)
  other arithmetic  69.1 us (12%)
  local copies, waits for them, and re-layouts  47.7 us (8%)
  matrix products  36.8 us (6%)
    ppermute x10, waiting for transfers between devices, rejoin(): got = lax.ppermute(array, 'seq', [(i, i ^ distance) for i in range(size)])  41.9 us
    ppermute x10, waiting for transfers between devices, halve(): got = lax.ppermute(given, 'seq', [(i, i ^ distance) for i in range(size)])  35.4 us
    pallas_call x2, Pallas kernels, intra_backward(): pl.pallas_call(intra_back_kernel, grid=(rows // Q,), in_specs=[by_row(CON...  34.5 us
    pallas_call x2, Pallas kernels, conv_backward(): pl.pallas_call(conv_back_kernel, out_shape=outs, scratch_shapes=[pltpu.VM...  30.8 us
    unnamed x317, local copies, waits for them, and re-layouts  26.8 us
    ppermute x8, starting transfers between devices, chain_scan(): arrived = lax.ppermute(sent, 'seq', route)  26.5 us
    ppermute x8, waiting for transfers between devices, chain_scan(): arrived = lax.ppermute(sent, 'seq', route)  20 us
    ppermute x8, starting transfers between devices, to_holders(): lax.ppermute(array, everywhere, [(flat(s, 2 * k + m), flat(layer, 2 * k +...  19.9 us
  transfers between devices with their start and end apart: 78, of which 27 were waited for; matrix products, arithmetic and copies ran while one was open for 18% of the time, Pallas kernels for 20%

profile of v2, /device:TPU:0, one launch (start us, length us, event | category | flops | bytes accessed | tf_op | source)
XLA Modules:
  0.0 583.0 jit_solution(2560504946636618965)
XLA Ops:
  4.5 3.4 collective-permute-start.2
  8.0 4.2 collective-permute-start.3
  13.2 3.6 collective-permute-start
  20.5 8.6 %collective-permute-done.3 = bf16[1824,384]{1,0:T(8,128)(2,1)} collective-permute-done((bf16[1824,384]{1,0:T(8,128)(2,1)}, bf16[1824,384]{1,0:T(8,128)(2,1)}, u32[]{:S(2)}, u32[]{:S(2)}) %collective-permute-start.3) | collective-permute-done | bytes 1400864 | tf_op jit(solution)/shard_map/ppermute | solution.py:680
  41.5 4.1 collective-permute-start.8
  46.0 9.7 %shard_map.213 = (f32[512,1792]{1,0:T(8,128)}, bf16[512,1792]{1,0:T(8,128)(2,1)S(1)}, f32[512,128]{1,0:T(8,128)S(1)}, f32[512,128]{1,0:T(8,128)S(1)}, f32[512,12...) custom-call(bf16[512,1792]{1,0:T(8,128)(2,1)} %copy-done.89, ...), custom_call_target="tpu_custom_call" | custom-call | tf_op jit(solution)/shard_map/pallas_call | solution.py:464
  57.8 4.1 collective-permute-start.7
  61.9 8.1 %shard_map.214.y0_ref = f32[512,1536]{1,0:T(8,128)S(1)} custom-call(f32[512,1792]{1,0:T(8,128)} %get-tuple-element.320.q_ref.c_ref, f32[512,128]{1,0:T(8,128)S(1)} %get-tuple-element.321.dt_ref, f32[512,128]{1,0:T(8,128)S(1)} %get-tuple-element.322.cum_ref, f32[512,128]{1,0:T(8,128)S(1)} %get-tuple-element.324.col_ref, ...), custom_call_target="tpu_custom_call" | custom-call | flops 805306368 | bytes 10240000 | tf_op jit(solution)/shard_map/pallas_call | solution.py:475
  76.3 4.8 collective-permute-start.14
  82.8 5.1 collective-permute-start.9
  92.5 3.1 fusion.35.z_ref
  105.8 7.9 %shard_map.215 = (f32[512,1536]{1,0:T(8,128)}, bf16[512,1536]{1,0:T(8,128)(2,1)S(1)}, bf16[512,768]{1,0:T(8,128)(2,1)S(1)}) custom-call(f32[512,1536]{1,0:T(8,128)} %copy-done.5, f32[512,1536]{1,0:T(8,128)} %fusion.35.z_ref, f32[512,1792]{1,0:T(8,128)} %get-tuple-element.320.q_ref.c_ref, f32[512,128]{1,0:T(8,128)S(1)} %get-tuple-element.323.all_ref, ...), custom_call_target="tpu_custom_call" | custom-call | tf_op jit(solution)/shard_map/pallas_call | solution.py:504
  116.5 6.3 %collective-permute-start.17 = (bf16[16,1792]{1,0:T(8,128)(2,1)S(1)}, bf16[16,1792]{1,0:T(8,128)(2,1)S(1)}, u32[]{:S(2)}, u32[]{:S(2)}) collective-permute-start(bf16[16,1792]{1,0:T(8,128)(2,1)S(1)} %slice.399), channel_id=1, source_target_pairs={{0,16},{2,18},{4,20},{6,22},{8,24},{10,26},{12,28},{14,30},{16,4},... | collective-permute-start | bytes 172040 | tf_op jit(solution)/shard_map/ppermute | solution.py:913
  123.7 9.7 %shard_map.216 = (f32[512,1792]{1,0:T(8,128)}, bf16[512,1792]{1,0:T(8,128)(2,1)S(1)}, f32[512,128]{1,0:T(8,128)S(1)}, f32[512,128]{1,0:T(8,128)S(1)}, f32[512,12...) custom-call(bf16[512,1792]{1,0:T(8,128)(2,1)} %copy-done.90, ...), custom_call_target="tpu_custom_call" | custom-call | tf_op jit(solution)/shard_map/pallas_call | solution.py:464
  133.4 3.6 collective-permute-start.18
  138.7 6.1 %collective-permute-start.19 = (f32[136,768]{1,0:T(8,128)S(1)}, f32[136,768]{1,0:T(8,128)S(1)}, u32[]{:S(2)}, u32[]{:S(2)}) collective-permute-start(f32[136,768]{1,0:T(8,128)S(1)} %pad_maximum_fusion.25), channel_id=1, source_target_pairs={{0,4},{2,6},{4,8},{6,10},{8,12},{10,14},{1,5},{3,7},{5,9},{7,11},{... | collective-permute-start | bytes 1253384 | tf_op jit(solution)/shard_map/ppermute | solution.py:656
  144.8 8.1 %shard_map.217.y0_ref = f32[512,1536]{1,0:T(8,128)S(1)} custom-call(f32[512,1792]{1,0:T(8,128)} %get-tuple-element.264.q_ref.c_ref, f32[512,128]{1,0:T(8,128)S(1)} %get-tuple-element.265.dt_ref, f32[512,128]{1,0:T(8,128)S(1)} %get-tuple-element.266.cum_ref, f32[512,128]{1,0:T(8,128)S(1)} %get-tuple-element.324.col_ref, ...), custom_call_target="tpu_custom_call" | custom-call | flops 805306368 | bytes 10240000 | tf_op jit(solution)/shard_map/pallas_call | solution.py:475
  158.1 5.5 collective-permute-start.23
  165.6 3.0 broadcast_select_fusion.5
  170.4 3.0 fusion.33.z_ref
  178.1 8.1 %shard_map.218 = (f32[512,1536]{1,0:T(8,128)}, bf16[512,1536]{1,0:T(8,128)(2,1)S(1)}, bf16[512,768]{1,0:T(8,128)(2,1)S(1)}) custom-call(f32[512,1536]{1,0:T(8,128)} %copy-done.6, f32[512,1536]{1,0:T(8,128)} %fusion.33.z_ref, f32[512,1792]{1,0:T(8,128)} %get-tuple-element.264.q_ref.c_ref, f32[512,128]{1,0:T(8,128)S(1)} %copy-done.24, ...), custom_call_target="tpu_custom_call" | custom-call | tf_op jit(solution)/shard_map/pallas_call | solution.py:504
  187.0 9.2 %shard_map.219 = (bf16[512,1536]{1,0:T(8,128)(2,1)S(1)}, bf16[512,1536]{1,0:T(8,128)(2,1)}, f32[1,1536]{1,0:T(1,128)S(1)}, bf16[2,144,768]{2,1,0:T(8,128)(2,1)S(1)}) custom-call(bf16[512,768]{1,0:T(8,128)(2,1)S(1)} %copy-done.7, bf16[1536,768]{1,0:T(8,128)(2,1)} %maximum_maximum_fusion.1.w_ref, f32[512,1536]{1,0:T(8,128)} %get-tuple-element.273.y_ref, ...), custom_call_target="tpu_custom_call" | custom-call | tf_op jit(solution)/shard_map/pallas_call | solution.py:538
  212.0 17.2 %shard_map.220 = (f32[512,1536]{1,0:T(8,128)}, f32[512,256]{1,0:T(8,128)S(1)}, f32[512,256]{1,0:T(8,128)S(1)}) custom-call(f32[512,1792]{1,0:T(8,128)} %get-tuple-element.264.q_ref.c_ref, f32[512,128]{1,0:T(8,128)S(1)} %copy-done.36, f32[512,128]{1,0:T(8,128)S(1)} %copy-done.48, f32[512,128]{1,0:T(8,128)S(1)} %copy-done.25, ...), custom_call_target="tpu_custom_call" | custom-call | flops 3019898880 | bytes 15360000 | tf_op jit(solution)/shard_map/pallas_call | solution.py:567
  240.1 14.1 %collective-permute-done.28 = bf16[144,768]{1,0:T(8,128)(2,1)S(1)} collective-permute-done((bf16[144,768]{1,0:T(8,128)(2,1)S(1)}, bf16[144,768]{1,0:T(8,128)(2,1)S(1)}, u32[]{:S(2)}, u32[]{:S(2)}) %collective-permute-start.28) | collective-permute-done | bytes 221216 | tf_op jit(solution)/shard_map/ppermute | solution.py:656
  267.7 8.0 %collective-permute-start.34 = (bf16[512,768]{1,0:T(8,128)(2,1)}, bf16[512,768]{1,0:T(8,128)(2,1)}, u32[]{:S(2)}, u32[]{:S(2)}) collective-permute-start(bf16[512,768]{1,0:T(8,128)(2,1)} %copy-done.65), channel_id=1, source_target_pairs={{0,16},{16,18},{4,20},{20,22},{8,24},{24,26},{12,28},{28,30},{1,17... | collective-permute-start | bytes 2359304 | tf_op jit(solution)/shard_map/ppermute | solution.py:886
  281.5 15.5 %shard_map.221 = (bf16[512,1792]{1,0:T(8,128)(2,1)}, bf16[512,128]{1,0:T(8,128)(2,1)S(1)}, f32[8,1792]{1,0:T(8,128)S(1)}, f32[8,1792]{1,0:T(8,128)S(1)}, f32[8,1792]{1,0:T(8,128)S(1)}, /*index=5*/f32[8,128]{1,0:T(8,128)S(1)}) custom-call(bf16[128,1536]{1,0:T(8,128)(2,1)S(1)} %pad_maximum_fusion.27.outg_ref, f32[128,1536]{1,0:T(8,128)S(1)} %copy-done.4, ...), custom_call_target="tpu_custom_call" | custom-call | tf_op jit(solution)/shard_map/pallas_call | solution.py:604
  309.4 5.7 collective-permute-start.36
  315.1 8.7 %shard_map.222 = (bf16[512,1536]{1,0:T(8,128)(2,1)S(1)}, bf16[512,1536]{1,0:T(8,128)(2,1)}, f32[1,1536]{1,0:T(1,128)S(1)}, bf16[2,144,768]{2,1,0:T(8,128)(2,1)S(1)}) custom-call(bf16[512,768]{1,0:T(8,128)(2,1)S(1)} %fusion.29.g_ref, bf16[1536,768]{1,0:T(8,128)(2,1)} %maximum_maximum_fusion.w_ref, f32[512,1536]{1,0:T(8,128)} %get-tuple-element.329.y_ref, ...), custom_call_target="tpu_custom_call" | custom-call | tf_op jit(solution)/shard_map/pallas_call | solution.py:538
  333.6 13.1 %collective-permute-done.38 = bf16[896,384]{1,0:T(8,128)(2,1)S(1)} collective-permute-done((bf16[896,384]{1,0:T(8,128)(2,1)S(1)}, bf16[896,384]{1,0:T(8,128)(2,1)S(1)}, u32[]{:S(2)}, u32[]{:S(2)}) %collective-permute-start.38) | collective-permute-done | bytes 688160 | tf_op jit(solution)/shard_map/ppermute | solution.py:706
  357.9 17.2 %shard_map.223 = (f32[512,1536]{1,0:T(8,128)}, f32[512,256]{1,0:T(8,128)S(1)}, f32[512,256]{1,0:T(8,128)S(1)}) custom-call(f32[512,1792]{1,0:T(8,128)} %get-tuple-element.320.q_ref.c_ref, f32[512,128]{1,0:T(8,128)S(1)} %copy-done.32, f32[512,128]{1,0:T(8,128)S(1)} %copy-done.46, f32[512,128]{1,0:T(8,128)S(1)} %get-tuple-element.323.all_ref, ...), custom_call_target="tpu_custom_call" | custom-call | flops 3019898880 | bytes 15360000 | tf_op jit(solution)/shard_map/pallas_call | solution.py:567
  386.9 4.7 collective-permute-done.43
  403.4 3.2 collective-permute-start.49
  408.4 15.3 %shard_map.224 = (bf16[512,1792]{1,0:T(8,128)(2,1)}, bf16[512,128]{1,0:T(8,128)(2,1)S(1)}, f32[8,1792]{1,0:T(8,128)S(1)}, f32[8,1792]{1,0:T(8,128)S(1)}, f32[8,1792]{1,0:T(8,128)S(1)}, /*index=5*/f32[8,128]{1,0:T(8,128)S(1)}) custom-call(bf16[128,1536]{1,0:T(8,128)(2,1)S(1)} %pad_maximum_fusion.28.outg_ref, f32[128,1536]{1,0:T(8,128)S(1)} %pad_maximum_fusion.16.inc_ref, ...), custom_call_target="tpu_custom_call" | custom-call | tf_op jit(solution)/shard_map/pallas_call | solution.py:604
  447.4 3.5 collective-permute-start.53
  455.4 10.8 %collective-permute-done.57 = bf16[304,384]{1,0:T(8,128)(2,1)S(1)} collective-permute-done((bf16[304,384]{1,0:T(8,128)(2,1)S(1)}, bf16[304,384]{1,0:T(8,128)(2,1)S(1)}, u32[]{:S(2)}, u32[]{:S(2)}) %collective-permute-start.57) | collective-permute-done | bytes 233504 | tf_op jit(solution)/shard_map/ppermute | solution.py:716
  467.2 6.8 %collective-permute-done.54 = f32[22,1792]{1,0:T(8,128)S(1)} collective-permute-done((f32[22,1792]{1,0:T(8,128)S(1)}, f32[22,1792]{1,0:T(8,128)S(1)}, u32[]{:S(2)}, u32[]{:S(2)}) %collective-permute-start.54) | collective-permute-done | bytes 157728 | tf_op jit(solution)/shard_map/ppermute | solution.py:746
  481.2 5.9 %collective-permute-done.59 = f32[22,1792]{1,0:T(8,128)S(1)} collective-permute-done((f32[22,1792]{1,0:T(8,128)S(1)}, f32[22,1792]{1,0:T(8,128)S(1)}, u32[]{:S(2)}, u32[]{:S(2)}) %collective-permute-start.59) | collective-permute-done | bytes 157728 | tf_op jit(solution)/shard_map/ppermute | solution.py:746
  488.5 2.9 collective-permute-done.62
  494.1 8.6 %collective-permute-done.63 = bf16[192,384]{1,0:T(8,128)(2,1)S(1)} collective-permute-done((bf16[192,384]{1,0:T(8,128)(2,1)S(1)}, bf16[192,384]{1,0:T(8,128)(2,1)S(1)}, u32[]{:S(2)}, u32[]{:S(2)}) %collective-permute-start.63) | collective-permute-done | bytes 147488 | tf_op jit(solution)/shard_map/ppermute | solution.py:716
  502.7 3.4 collective-permute-start.64
  506.2 5.9 %collective-permute-done.60 = f32[22,1792]{1,0:T(8,128)S(1)} collective-permute-done((f32[22,1792]{1,0:T(8,128)S(1)}, f32[22,1792]{1,0:T(8,128)S(1)}, u32[]{:S(2)}, u32[]{:S(2)}) %collective-permute-start.60) | collective-permute-done | bytes 157728 | tf_op jit(solution)/shard_map/ppermute | solution.py:746
  515.3 10.3 %collective-permute-done.72 = bf16[112,384]{1,0:T(8,128)(2,1)S(1)} collective-permute-done((bf16[112,384]{1,0:T(8,128)(2,1)S(1)}, bf16[112,384]{1,0:T(8,128)(2,1)S(1)}, u32[]{:S(2)}, u32[]{:S(2)}) %collective-permute-start.72) | collective-permute-done | bytes 86048 | tf_op jit(solution)/shard_map/ppermute | solution.py:716
  528.4 3.7 collective-permute-done.73
  534.6 5.7 collective-permute-done.74
  542.7 13.4 %collective-permute-done.76 = bf16[448,384]{1,0:T(8,128)(2,1)S(1)} collective-permute-done((bf16[448,384]{1,0:T(8,128)(2,1)S(1)}, bf16[448,384]{1,0:T(8,128)(2,1)S(1)}, u32[]{:S(2)}, u32[]{:S(2)}) %collective-permute-start.76) | collective-permute-done | bytes 344096 | tf_op jit(solution)/shard_map/ppermute | solution.py:722
  556.3 12.4 %collective-permute-done.66 = bf16[768,384]{1,0:T(8,128)(2,1)S(1)} collective-permute-done((bf16[768,384]{1,0:T(8,128)(2,1)S(1)}, bf16[768,384]{1,0:T(8,128)(2,1)S(1)}, u32[]{:S(2)}, u32[]{:S(2)}) %collective-permute-start.66) | collective-permute-done | bytes 589856 | tf_op jit(solution)/shard_map/ppermute | solution.py:722
  569.6 5.5 collective-permute-done.75
  578.6 3.9 shard_map.225
  (680 shorter events, 224.0 us)
Async XLA Ops:
  4.5 31.0 %collective-permute-start.2 = (bf16[1824,384]{1,0:T(8,128)(2,1)}, bf16[1824,384]{1,0:T(8,128)(2,1)}, u32[]{:S(2)}, u32[]{:S(2)}) collective-permute-start(bf16[1824,384]{1,0:T(8,128)(2,1)} %pad.66), channel_id=1, source_target_pairs={{0,16},{1,17},{2,18},{3,19},{4,20},{5,21},{6,22},{7,23},{8,24},{9,... | collective-permute-start | bytes 4202504 | tf_op jit(solution)/shard_map/ppermute | solution.py:688
  8.0 21.1 %collective-permute-start.3 = (bf16[1824,384]{1,0:T(8,128)(2,1)}, bf16[1824,384]{1,0:T(8,128)(2,1)}, u32[]{:S(2)}, u32[]{:S(2)}) collective-permute-start(bf16[1824,384]{1,0:T(8,128)(2,1)} %pad.66), channel_id=1, source_target_pairs={{0,1},{1,0},{2,3},{3,2},{4,5},{5,4},{6,7},{7,6},{8,9},{9,8},{10,11... | collective-permute-start | bytes 4202504 | tf_op jit(solution)/shard_map/ppermute | solution.py:680
  13.2 20.5 %collective-permute-start = (bf16[512,768]{1,0:T(8,128)(2,1)}, bf16[512,768]{1,0:T(8,128)(2,1)S(1)}, u32[]{:S(2)}, u32[]{:S(2)}) collective-permute-start(bf16[512,768]{1,0:T(8,128)(2,1)} %dynamic-slice_bitcast_fusion.3), channel_id=1, source_target_pairs={{0,2},{18,16},{4,6},{22,20},{8,10},{26,24},{12,14},{30,28},{1,3},{... | collective-permute-start | bytes 2359304 | tf_op jit(solution)/shard_map/ppermute | solution.py:835
  17.0 16.6 %collective-permute-start.1 = (f32[16,1792]{1,0:T(8,128)S(1)}, f32[16,1792]{1,0:T(8,128)S(1)}, u32[]{:S(2)}, u32[]{:S(2)}) collective-permute-start(f32[16,1792]{1,0:T(8,128)S(1)} %pad.65), channel_id=1, source_target_pairs={{0,16},{16,0},{1,17},{17,1},{2,18},{18,2},{3,19},{19,3},{4,20},{20... | collective-permute-start | bytes 344072 | tf_op jit(solution)/shard_map/ppermute | solution.py:871
  41.5 30.9 %collective-permute-start.8 = (bf16[3072,384]{1,0:T(8,128)(2,1)}, bf16[3072,384]{1,0:T(8,128)(2,1)S(1)}, u32[]{:S(2)}, u32[]{:S(2)}) collective-permute-start(bf16[3072,384]{1,0:T(8,128)(2,1)} %pad_maximum_fusion.2), channel_id=1, source_target_pairs={{0,1},{1,0},{2,3},{3,2},{4,5},{5,4},{6,7},{7,6},{8,9},{9,8},{10,11... | collective-permute-start | bytes 7077896 | tf_op jit(solution)/shard_map/ppermute | solution.py:680
  72.5 15.5 %collective-permute-start.10 = (bf16[3072,384]{1,0:T(8,128)(2,1)}, bf16[3072,384]{1,0:T(8,128)(2,1)S(1)}, u32[]{:S(2)}, u32[]{:S(2)}) collective-permute-start(bf16[3072,384]{1,0:T(8,128)(2,1)} %pad_maximum_fusion.2), channel_id=1, source_target_pairs={{0,16},{1,17},{2,18},{3,19},{4,20},{5,21},{6,22},{7,23},{8,24},{9,... | collective-permute-start | bytes 7077896 | tf_op jit(solution)/shard_map/ppermute | solution.py:688
  73.9 14.1 %collective-permute-start.11 = (bf16[3072,384]{1,0:T(8,128)(2,1)S(1)}, bf16[3072,384]{1,0:T(8,128)(2,1)S(1)}, u32[]{:S(2)}, u32[]{:S(2)}) collective-permute-start(bf16[3072,384]{1,0:T(8,128)(2,1)S(1)} %collective-permute-done.8), channel_id=1, source_target_pairs={{0,16},{1,17},{2,18},{3,19},{4,20},{5,21},{6,22},{7,23},{8,24},{9,... | collective-permute-start | bytes 7077896 | tf_op jit(solution)/shard_map/ppermute | solution.py:688
  76.3 20.1 %collective-permute-start.14 = (bf16[512,768]{1,0:T(8,128)(2,1)}, bf16[512,768]{1,0:T(8,128)(2,1)}, u32[]{:S(2)}, u32[]{:S(2)}) collective-permute-start(bf16[512,768]{1,0:T(8,128)(2,1)} %dynamic-slice_bitcast_fusion.2), channel_id=1, source_target_pairs={{0,2},{18,16},{4,6},{22,20},{8,10},{26,24},{12,14},{30,28},{1,3},{... | collective-permute-start | bytes 2359304 | tf_op jit(solution)/shard_map/ppermute | solution.py:835
  81.1 17.7 %collective-permute-start.13 = (bf16[1824,384]{1,0:T(8,128)(2,1)}, bf16[1824,384]{1,0:T(8,128)(2,1)}, u32[]{:S(2)}, u32[]{:S(2)}) collective-permute-start(bf16[1824,384]{1,0:T(8,128)(2,1)} %pad.66), channel_id=1, source_target_pairs={{16,17},{17,16},{18,19},{19,18},{20,21},{21,20},{22,23},{23,22},{2... | collective-permute-start | bytes 4202504 | tf_op jit(solution)/shard_map/ppermute | solution.py:680
  98.8 15.4 %collective-permute-start.15 = (bf16[1824,384]{1,0:T(8,128)(2,1)}, bf16[1824,384]{1,0:T(8,128)(2,1)S(1)}, u32[]{:S(2)}, u32[]{:S(2)}) collective-permute-start(bf16[1824,384]{1,0:T(8,128)(2,1)} %pad.66), channel_id=1, source_target_pairs={{16,0},{17,1},{18,2},{19,3},{20,4},{21,5},{22,6},{23,7},{24,8},{25... | collective-permute-start | bytes 4202504 | tf_op jit(solution)/shard_map/ppermute | solution.py:688
  100.3 13.9 %collective-permute-start.16 = (bf16[1824,384]{1,0:T(8,128)(2,1)}, bf16[1824,384]{1,0:T(8,128)(2,1)S(1)}, u32[]{:S(2)}, u32[]{:S(2)}) collective-permute-start(bf16[1824,384]{1,0:T(8,128)(2,1)} %collective-permute-done.13), channel_id=1, source_target_pairs={{16,0},{17,1},{18,2},{19,3},{20,4},{21,5},{22,6},{23,7},{24,8},{25... | collective-permute-start | bytes 4202504 | tf_op jit(solution)/shard_map/ppermute | solution.py:688
  103.7 51.8 %collective-permute-start.20 = (bf16[3072,384]{1,0:T(8,128)(2,1)}, bf16[3072,384]{1,0:T(8,128)(2,1)}, u32[]{:S(2)}, u32[]{:S(2)}) collective-permute-start(bf16[3072,384]{1,0:T(8,128)(2,1)} %pad_maximum_fusion.2), channel_id=1, source_target_pairs={{16,17},{17,16},{18,19},{19,18},{20,21},{21,20},{22,23},{23,22},{2... | collective-permute-start | bytes 7077896 | tf_op jit(solution)/shard_map/ppermute | solution.py:680
  138.7 15.9 %collective-permute-start.19 = (f32[136,768]{1,0:T(8,128)S(1)}, f32[136,768]{1,0:T(8,128)S(1)}, u32[]{:S(2)}, u32[]{:S(2)}) collective-permute-start(f32[136,768]{1,0:T(8,128)S(1)} %pad_maximum_fusion.25), channel_id=1, source_target_pairs={{0,4},{2,6},{4,8},{6,10},{8,12},{10,14},{1,5},{3,7},{5,9},{7,11},{... | collective-permute-start | bytes 1253384 | tf_op jit(solution)/shard_map/ppermute | solution.py:656
  158.1 15.4 %collective-permute-start.23 = (f32[136,768]{1,0:T(8,128)}, f32[136,768]{1,0:T(8,128)S(1)}, u32[]{:S(2)}, u32[]{:S(2)}) collective-permute-start(f32[136,768]{1,0:T(8,128)} %pad_maximum_fusion.26), channel_id=1, source_target_pairs={{0,8},{2,10},{4,12},{6,14},{1,9},{3,11},{5,13},{7,15},{16,24},{18,... | collective-permute-start | bytes 1253384 | tf_op jit(solution)/shard_map/ppermute | solution.py:656
  205.1 24.2 %collective-permute-start.27 = (bf16[2,1536,384]{2,1,0:T(8,128)(2,1)}, bf16[2,1536,384]{2,1,0:T(8,128)(2,1)}, u32[]{:S(2)}, u32[]{:S(2)}) collective-permute-start(bf16[2,1536,384]{2,1,0:T(8,128)(2,1)} %pad_maximum_fusion.5), channel_id=1, source_target_pairs={{0,16},{16,0},{1,17},{17,1},{2,18},{18,2},{3,19},{19,3},{4,20},{20... | collective-permute-start | bytes 7077896 | tf_op jit(solution)/shard_map/ppermute | solution.py:991
  205.1 24.1 %collective-permute-start.26 = (bf16[144,768]{1,0:T(8,128)(2,1)}, bf16[144,768]{1,0:T(8,128)(2,1)S(1)}, u32[]{:S(2)}, u32[]{:S(2)}) collective-permute-start(bf16[144,768]{1,0:T(8,128)(2,1)} %pad_maximum_fusion.31), channel_id=1, source_target_pairs={{4,0},{6,2},{8,4},{10,6},{12,8},{14,10},{5,1},{7,3},{9,5},{11,7},{... | collective-permute-start | bytes 663560 | tf_op jit(solution)/shard_map/ppermute | solution.py:656
  231.1 23.1 %collective-permute-start.28 = (bf16[144,768]{1,0:T(8,128)(2,1)S(1)}, bf16[144,768]{1,0:T(8,128)(2,1)S(1)}, u32[]{:S(2)}, u32[]{:S(2)}) collective-permute-start(bf16[144,768]{1,0:T(8,128)(2,1)S(1)} %pad_maximum_fusion.32), channel_id=1, source_target_pairs={{8,0},{10,2},{12,4},{14,6},{9,1},{11,3},{13,5},{15,7},{24,16},{26,... | collective-permute-start | bytes 663560 | tf_op jit(solution)/shard_map/ppermute | solution.py:656
  258.0 39.0 %collective-permute-start.30 = (bf16[1536,384]{1,0:T(8,128)(2,1)}, bf16[1536,384]{1,0:T(8,128)(2,1)}, u32[]{:S(2)}, u32[]{:S(2)}) collective-permute-start(bf16[1536,384]{1,0:T(8,128)(2,1)} %dynamic-slice_bitcast_fusion.1), channel_id=1, source_target_pairs={{0,1},{1,0},{2,3},{3,2},{4,5},{5,4},{6,7},{7,6},{8,9},{9,8},{10,11... | collective-permute-start | bytes 3538952 | tf_op jit(solution)/shard_map/ppermute | solution.py:706
  264.9 44.5 %collective-permute-start.32 = (bf16[512,768]{1,0:T(8,128)(2,1)S(1)}, bf16[512,768]{1,0:T(8,128)(2,1)}, u32[]{:S(2)}, u32[]{:S(2)}) collective-permute-start(bf16[512,768]{1,0:T(8,128)(2,1)S(1)} %get-tuple-element.303.x_ref), channel_id=1, source_target_pairs={{0,0},{16,2},{4,4},{20,6},{8,8},{24,10},{12,12},{28,14},{1,1},{17,... | collective-permute-start | bytes 2359304 | tf_op jit(solution)/shard_map/ppermute | solution.py:886
  266.4 48.6 %collective-permute-start.33 = (bf16[512,768]{1,0:T(8,128)(2,1)S(1)}, bf16[512,768]{1,0:T(8,128)(2,1)}, u32[]{:S(2)}, u32[]{:S(2)}) collective-permute-start(bf16[512,768]{1,0:T(8,128)(2,1)S(1)} %get-tuple-element.303.x_ref), channel_id=1, source_target_pairs={{2,0},{18,2},{6,4},{22,6},{10,8},{26,10},{14,12},{30,14},{3,1},{19... | collective-permute-start | bytes 2359304 | tf_op jit(solution)/shard_map/ppermute | solution.py:886
  267.7 47.3 %collective-permute-start.34 = (bf16[512,768]{1,0:T(8,128)(2,1)}, bf16[512,768]{1,0:T(8,128)(2,1)}, u32[]{:S(2)}, u32[]{:S(2)}) collective-permute-start(bf16[512,768]{1,0:T(8,128)(2,1)} %copy-done.65), channel_id=1, source_target_pairs={{0,16},{16,18},{4,20},{20,22},{8,24},{24,26},{12,28},{28,30},{1,17... | collective-permute-start | bytes 2359304 | tf_op jit(solution)/shard_map/ppermute | solution.py:886
  275.7 39.4 %collective-permute-start.35 = (bf16[512,768]{1,0:T(8,128)(2,1)}, bf16[512,768]{1,0:T(8,128)(2,1)}, u32[]{:S(2)}, u32[]{:S(2)}) collective-permute-start(bf16[512,768]{1,0:T(8,128)(2,1)} %copy-done.65), channel_id=1, source_target_pairs={{2,16},{18,18},{6,20},{22,22},{10,24},{26,26},{14,28},{30,30},{3,1... | collective-permute-start | bytes 2359304 | tf_op jit(solution)/shard_map/ppermute | solution.py:886
  306.8 20.7 %collective-permute-start.37 = (bf16[2,896,384]{2,1,0:T(8,128)(2,1)}, bf16[2,896,384]{2,1,0:T(8,128)(2,1)}, u32[]{:S(2)}, u32[]{:S(2)}) collective-permute-start(bf16[2,896,384]{2,1,0:T(8,128)(2,1)} %pad_maximum_fusion.11), channel_id=1, source_target_pairs={{0,16},{16,0},{1,17},{17,1},{2,18},{18,2},{3,19},{19,3},{4,20},{20... | collective-permute-start | bytes 4128776 | tf_op jit(solution)/shard_map/ppermute | solution.py:1027
  309.4 22.2 %collective-permute-start.36 = (bf16[768,384]{1,0:T(8,128)(2,1)}, bf16[768,384]{1,0:T(8,128)(2,1)}, u32[]{:S(2)}, u32[]{:S(2)}) collective-permute-start(bf16[768,384]{1,0:T(8,128)(2,1)} %dynamic-slice_bitcast_fusion.7), channel_id=1, source_target_pairs={{0,2},{2,0},{4,6},{6,4},{8,10},{10,8},{12,14},{14,12},{1,3},{3,1},... | collective-permute-start | bytes 1769480 | tf_op jit(solution)/shard_map/ppermute | solution.py:716
  329.2 17.4 %collective-permute-start.38 = (bf16[896,384]{1,0:T(8,128)(2,1)S(1)}, bf16[896,384]{1,0:T(8,128)(2,1)S(1)}, u32[]{:S(2)}, u32[]{:S(2)}) collective-permute-start(bf16[896,384]{1,0:T(8,128)(2,1)S(1)} %dynamic-slice_bitcast_fusion.5), channel_id=1, source_target_pairs={{0,1},{1,0},{2,3},{3,2},{4,5},{5,4},{6,7},{7,6},{8,9},{9,8},{10,11... | collective-permute-start | bytes 2064392 | tf_op jit(solution)/shard_map/ppermute | solution.py:706
  351.2 24.9 %collective-permute-start.42 = (bf16[2,1536,384]{2,1,0:T(8,128)(2,1)}, bf16[2,1536,384]{2,1,0:T(8,128)(2,1)}, u32[]{:S(2)}, u32[]{:S(2)}) collective-permute-start(bf16[2,1536,384]{2,1,0:T(8,128)(2,1)} %pad_maximum_fusion.6), channel_id=1, source_target_pairs={{0,16},{16,0},{1,17},{17,1},{2,18},{18,2},{3,19},{19,3},{4,20},{20... | collective-permute-start | bytes 7077896 | tf_op jit(solution)/shard_map/ppermute | solution.py:991
  352.7 22.5 %collective-permute-start.41 = (bf16[448,384]{1,0:T(8,128)(2,1)S(1)}, bf16[448,384]{1,0:T(8,128)(2,1)S(1)}, u32[]{:S(2)}, u32[]{:S(2)}) collective-permute-start(bf16[448,384]{1,0:T(8,128)(2,1)S(1)} %dynamic-slice_bitcast_fusion.12), channel_id=1, source_target_pairs={{0,2},{2,0},{4,6},{6,4},{8,10},{10,8},{12,14},{14,12},{1,3},{3,1},... | collective-permute-start | bytes 1032200 | tf_op jit(solution)/shard_map/ppermute | solution.py:716
  356.3 19.7 %collective-permute-start.40 = (bf16[144,768]{1,0:T(8,128)(2,1)}, bf16[144,768]{1,0:T(8,128)(2,1)S(1)}, u32[]{:S(2)}, u32[]{:S(2)}) collective-permute-start(bf16[144,768]{1,0:T(8,128)(2,1)} %pad_maximum_fusion.33), channel_id=1, source_target_pairs={{4,0},{6,2},{8,4},{10,6},{12,8},{14,10},{5,1},{7,3},{9,5},{11,7},{... | collective-permute-start | bytes 663560 | tf_op jit(solution)/shard_map/ppermute | solution.py:656
  377.0 14.6 %collective-permute-start.43 = (bf16[144,768]{1,0:T(8,128)(2,1)S(1)}, bf16[144,768]{1,0:T(8,128)(2,1)S(1)}, u32[]{:S(2)}, u32[]{:S(2)}) collective-permute-start(bf16[144,768]{1,0:T(8,128)(2,1)S(1)} %pad_maximum_fusion.34), channel_id=1, source_target_pairs={{8,0},{10,2},{12,4},{14,6},{9,1},{11,3},{13,5},{15,7},{24,16},{26,... | collective-permute-start | bytes 663560 | tf_op jit(solution)/shard_map/ppermute | solution.py:656
  398.4 27.0 %collective-permute-start.46 = (bf16[608,384]{1,0:T(8,128)(2,1)}, bf16[608,384]{1,0:T(8,128)(2,1)S(1)}, u32[]{:S(2)}, u32[]{:S(2)}) collective-permute-start(bf16[608,384]{1,0:T(8,128)(2,1)} %dynamic-slice_bitcast_fusion.8), channel_id=1, source_target_pairs={{0,4},{2,6},{4,0},{6,2},{8,12},{10,14},{12,8},{14,10},{1,5},{3,7},... | collective-permute-start | bytes 1400840 | tf_op jit(solution)/shard_map/ppermute | solution.py:716
  402.5 41.8 %collective-permute-start.48 = (bf16[1536,384]{1,0:T(8,128)(2,1)}, bf16[1536,384]{1,0:T(8,128)(2,1)}, u32[]{:S(2)}, u32[]{:S(2)}) collective-permute-start(bf16[1536,384]{1,0:T(8,128)(2,1)} %dynamic-slice_bitcast_fusion), channel_id=1, source_target_pairs={{0,1},{1,0},{2,3},{3,2},{4,5},{5,4},{6,7},{7,6},{8,9},{9,8},{10,11... | collective-permute-start | bytes 3538952 | tf_op jit(solution)/shard_map/ppermute | solution.py:706
  403.4 49.3 %collective-permute-start.49 = (bf16[512,768]{1,0:T(8,128)(2,1)S(1)}, bf16[512,768]{1,0:T(8,128)(2,1)}, u32[]{:S(2)}, u32[]{:S(2)}) collective-permute-start(bf16[512,768]{1,0:T(8,128)(2,1)S(1)} %copy-done.11), channel_id=1, source_target_pairs={{0,16},{16,18},{4,20},{20,22},{8,24},{24,26},{12,28},{28,30},{1,17... | collective-permute-start | bytes 2359304 | tf_op jit(solution)/shard_map/ppermute | solution.py:886
  406.6 46.5 %collective-permute-start.50 = (bf16[512,768]{1,0:T(8,128)(2,1)S(1)}, bf16[512,768]{1,0:T(8,128)(2,1)}, u32[]{:S(2)}, u32[]{:S(2)}) collective-permute-start(bf16[512,768]{1,0:T(8,128)(2,1)S(1)} %copy-done.11), channel_id=1, source_target_pairs={{2,16},{18,18},{6,20},{22,22},{10,24},{26,26},{14,28},{30,30},{3,1... | collective-permute-start | bytes 2359304 | tf_op jit(solution)/shard_map/ppermute | solution.py:886
  440.1 34.3 %collective-permute-start.55 = (bf16[512,768]{1,0:T(8,128)(2,1)S(1)}, bf16[512,768]{1,0:T(8,128)(2,1)S(1)}, u32[]{:S(2)}, u32[]{:S(2)}) collective-permute-start(bf16[512,768]{1,0:T(8,128)(2,1)S(1)} %fusion.22), channel_id=1, source_target_pairs={{0,0},{16,2},{4,4},{20,6},{8,8},{24,10},{12,12},{28,14},{1,1},{17,... | collective-permute-start | bytes 2359304 | tf_op jit(solution)/shard_map/ppermute | solution.py:886
  444.3 30.2 %collective-permute-start.56 = (bf16[512,768]{1,0:T(8,128)(2,1)S(1)}, bf16[512,768]{1,0:T(8,128)(2,1)S(1)}, u32[]{:S(2)}, u32[]{:S(2)}) collective-permute-start(bf16[512,768]{1,0:T(8,128)(2,1)S(1)} %fusion.22), channel_id=1, source_target_pairs={{2,0},{18,2},{6,4},{22,6},{10,8},{26,10},{14,12},{30,14},{3,1},{19... | collective-permute-start | bytes 2359304 | tf_op jit(solution)/shard_map/ppermute | solution.py:886
  452.7 13.4 %collective-permute-start.57 = (bf16[304,384]{1,0:T(8,128)(2,1)S(1)}, bf16[304,384]{1,0:T(8,128)(2,1)S(1)}, u32[]{:S(2)}, u32[]{:S(2)}) collective-permute-start(bf16[304,384]{1,0:T(8,128)(2,1)S(1)} %dynamic-slice_bitcast_fusion.14), channel_id=1, source_target_pairs={{0,8},{2,10},{4,12},{6,14},{8,0},{10,2},{12,4},{14,6},{1,9},{3,11}... | collective-permute-start | bytes 700424 | tf_op jit(solution)/shard_map/ppermute | solution.py:716
  453.2 21.0 %collective-permute-start.51 = (bf16[896,384]{1,0:T(8,128)(2,1)S(1)}, bf16[896,384]{1,0:T(8,128)(2,1)S(1)}, u32[]{:S(2)}, u32[]{:S(2)}) collective-permute-start(bf16[896,384]{1,0:T(8,128)(2,1)S(1)} %dynamic-slice_bitcast_fusion.4), channel_id=1, source_target_pairs={{0,1},{1,0},{2,3},{3,2},{4,5},{5,4},{6,7},{7,6},{8,9},{9,8},{10,11... | collective-permute-start | bytes 2064392 | tf_op jit(solution)/shard_map/ppermute | solution.py:706
  454.3 19.8 %collective-permute-start.52 = (bf16[768,384]{1,0:T(8,128)(2,1)S(1)}, bf16[768,384]{1,0:T(8,128)(2,1)S(1)}, u32[]{:S(2)}, u32[]{:S(2)}) collective-permute-start(bf16[768,384]{1,0:T(8,128)(2,1)S(1)} %dynamic-slice_bitcast_fusion.6), channel_id=1, source_target_pairs={{0,2},{2,0},{4,6},{6,4},{8,10},{10,8},{12,14},{14,12},{1,3},{3,1},... | collective-permute-start | bytes 1769480 | tf_op jit(solution)/shard_map/ppermute | solution.py:716
  474.5 17.4 %collective-permute-start.58 = (bf16[448,384]{1,0:T(8,128)(2,1)S(1)}, bf16[448,384]{1,0:T(8,128)(2,1)S(1)}, u32[]{:S(2)}, u32[]{:S(2)}) collective-permute-start(bf16[448,384]{1,0:T(8,128)(2,1)S(1)} %dynamic-slice_bitcast_fusion.11), channel_id=1, source_target_pairs={{0,2},{2,0},{4,6},{6,4},{8,10},{10,8},{12,14},{14,12},{1,3},{3,1},... | collective-permute-start | bytes 1032200 | tf_op jit(solution)/shard_map/ppermute | solution.py:716
  488.4 43.8 %collective-permute-start.68 = (bf16[608,384]{1,0:T(8,128)(2,1)S(1)}, bf16[608,384]{1,0:T(8,128)(2,1)S(1)}, u32[]{:S(2)}, u32[]{:S(2)}) collective-permute-start(bf16[608,384]{1,0:T(8,128)(2,1)S(1)} %pad_maximum_fusion.22), channel_id=1, source_target_pairs={{0,4},{2,6},{4,0},{6,2},{8,12},{10,14},{12,8},{14,10},{1,5},{3,7},... | collective-permute-start | bytes 1400840 | tf_op jit(solution)/shard_map/ppermute | solution.py:722
  492.0 20.1 %collective-permute-start.60 = (f32[22,1792]{1,0:T(8,128)S(1)}, f32[22,1792]{1,0:T(8,128)S(1)}, u32[]{:S(2)}, u32[]{:S(2)}) collective-permute-start(f32[22,1792]{1,0:T(8,128)S(1)} %add.421), channel_id=1, source_target_pairs={{0,4},{2,6},{4,0},{6,2},{8,12},{10,14},{12,8},{14,10},{1,5},{3,7},... | collective-permute-start | bytes 473096 | tf_op jit(solution)/shard_map/ppermute | solution.py:746
  492.3 22.6 %collective-permute-start.71 = (bf16[224,384]{1,0:T(8,128)(2,1)S(1)}, bf16[224,384]{1,0:T(8,128)(2,1)S(1)}, u32[]{:S(2)}, u32[]{:S(2)}) collective-permute-start(bf16[224,384]{1,0:T(8,128)(2,1)S(1)} %dynamic-slice_bitcast_fusion.17), channel_id=1, source_target_pairs={{0,4},{2,6},{4,0},{6,2},{8,12},{10,14},{12,8},{14,10},{1,5},{3,7},... | collective-permute-start | bytes 516104 | tf_op jit(solution)/shard_map/ppermute | solution.py:716
  512.1 16.2 %collective-permute-start.61 = (f32[22,1792]{1,0:T(8,128)S(1)}, f32[22,1792]{1,0:T(8,128)S(1)}, u32[]{:S(2)}, u32[]{:S(2)}) collective-permute-start(f32[22,1792]{1,0:T(8,128)S(1)} %add.422), channel_id=1, source_target_pairs={{0,8},{2,10},{4,12},{6,14},{8,0},{10,2},{12,4},{14,6},{1,9},{3,11}... | collective-permute-start | bytes 473096 | tf_op jit(solution)/shard_map/ppermute | solution.py:746
  525.7 14.6 %collective-permute-start.65 = (bf16[384,384]{1,0:T(8,128)(2,1)S(1)}, bf16[384,384]{1,0:T(8,128)(2,1)S(1)}, u32[]{:S(2)}, u32[]{:S(2)}) collective-permute-start(bf16[384,384]{1,0:T(8,128)(2,1)S(1)} %pad_maximum_fusion.30), channel_id=1, source_target_pairs={{0,4},{2,6},{4,0},{6,2},{8,12},{10,14},{12,8},{14,10},{1,5},{3,7},... | collective-permute-start | bytes 884744 | tf_op jit(solution)/shard_map/ppermute | solution.py:722
  532.5 23.7 %collective-permute-start.69 = (bf16[768,384]{1,0:T(8,128)(2,1)S(1)}, bf16[768,384]{1,0:T(8,128)(2,1)S(1)}, u32[]{:S(2)}, u32[]{:S(2)}) collective-permute-start(bf16[768,384]{1,0:T(8,128)(2,1)S(1)} %pad_maximum_fusion.20), channel_id=1, source_target_pairs={{0,2},{2,0},{4,6},{6,4},{8,10},{10,8},{12,14},{14,12},{1,3},{3,1},... | collective-permute-start | bytes 1769480 | tf_op jit(solution)/shard_map/ppermute | solution.py:722
  533.5 22.6 %collective-permute-start.76 = (bf16[448,384]{1,0:T(8,128)(2,1)S(1)}, bf16[448,384]{1,0:T(8,128)(2,1)S(1)}, u32[]{:S(2)}, u32[]{:S(2)}) collective-permute-start(bf16[448,384]{1,0:T(8,128)(2,1)S(1)} %slice.445), channel_id=1, source_target_pairs={{0,2},{2,0},{4,6},{6,4},{8,10},{10,8},{12,14},{14,12},{1,3},{3,1},... | collective-permute-start | bytes 1032200 | tf_op jit(solution)/shard_map/ppermute | solution.py:722
  540.5 28.2 %collective-permute-start.66 = (bf16[768,384]{1,0:T(8,128)(2,1)S(1)}, bf16[768,384]{1,0:T(8,128)(2,1)S(1)}, u32[]{:S(2)}, u32[]{:S(2)}) collective-permute-start(bf16[768,384]{1,0:T(8,128)(2,1)S(1)} %pad_maximum_fusion.21), channel_id=1, source_target_pairs={{0,2},{2,0},{4,6},{6,4},{8,10},{10,8},{12,14},{14,12},{1,3},{3,1},... | collective-permute-start | bytes 1769480 | tf_op jit(solution)/shard_map/ppermute | solution.py:722
  541.6 33.5 %collective-permute-start.75 = (bf16[448,384]{1,0:T(8,128)(2,1)S(1)}, bf16[448,384]{1,0:T(8,128)(2,1)S(1)}, u32[]{:S(2)}, u32[]{:S(2)}) collective-permute-start(bf16[448,384]{1,0:T(8,128)(2,1)S(1)} %pad_maximum_fusion.29), channel_id=1, source_target_pairs={{0,2},{2,0},{4,6},{6,4},{8,10},{10,8},{12,14},{14,12},{1,3},{3,1},... | collective-permute-start | bytes 1032200 | tf_op jit(solution)/shard_map/ppermute | solution.py:722
  (188 other events, 1283.4 us)

commit v3 on v2

--- a/solution.py
+++ b/solution.py
@@ -44,8 +44,7 @@
 
 
 def expand(v, spread):
-    high, low = split(v)
-    return nn(high, spread) + nn(low, spread)
+    return nn(jnp.concatenate(split(v), axis=1), spread)
 
 
 def expand_row(v, spread):
@@ -54,7 +53,7 @@
 
 def head_sum(v, spread):
     high, low = split(v)
-    return nt(high, spread) + nt(low, spread)
+    return nt(high, spread[0:128]) + nt(low, spread[0:128])
 
 
 def tri_sum(tri, v):
@@ -68,7 +67,7 @@
 
 
 def spread_matrix():
-    return (iota((128, DI), 1) // P_SIZE == iota((128, DI), 0)).astype(bf16)
+    return (iota((256, DI), 1) // P_SIZE == iota((256, DI), 0) % 128).astype(bf16)
 
 
 def two_heads(tile):
@@ -136,52 +135,70 @@
 
 
 def conv_kernel(
-    rc_ref, halo_ref, e_ref, col_ref, par_ref, sp_ref,
-    q_ref, ds_ref, dt_ref, cum_ref, all_ref, lin_ref, pack_ref,
+    section_ref, rc_ref, before_ref, halo_ref, e_ref, col_ref, par_ref, sp_ref,
+    q_ref, ds_ref, dt_ref, cum_ref, all_ref, lin_ref, kept_ref, given_ref, state_ref, row_ref,
 ):
+    step = pl.program_id(0)
+
+    @pl.when(step == 0)
+    def _():
+        state_ref[...] = jnp.zeros_like(state_ref)
+        row_ref[0:1, :] = jnp.zeros((1, 128), f32)
+        row_ref[1:2, :] = jnp.ones((1, 128), f32)
+
     spread = sp_ref[...]
     tri = (iota((Q, Q), 0) >= iota((Q, Q), 1)).astype(bf16)
-    rate = rates(par_ref)
-    bias = head_row(par_ref, STEP_BIAS)
-    state = jnp.zeros((STATE, DI), f32)
-    offset = jnp.zeros((1, 128), f32)
-    decay = jnp.ones((1, 128), f32)
-    for c in range(rc_ref.shape[0] // Q):
-        rows = slice(c * Q, (c + 1) * Q)
-        col = col_ref[rows, :]
-        dt = jax.nn.softplus(e_ref[rows, :] + bias)
-        cum = tri_sum(tri, dt * rate)
-        dt_ref[rows, :] = dt
-        cum_ref[rows, :] = cum
-        all_ref[rows, :] = cum + offset
-        for j in range(CONVCH // 128):
-            lanes = slice(j * 128, (j + 1) * 128)
-            if c == 0:
-                window = jnp.concatenate([halo_ref[:, lanes], rc_ref[0:Q, lanes]], axis=0)
-            else:
-                window = rc_ref[c * Q - 16 : (c + 1) * Q, lanes]
-            window = window.astype(f32)
-            pre = par_ref[TAP_BIAS : TAP_BIAS + 1, lanes] + par_ref[3:4, lanes] * window[16:]
-            for d in range(1, CONV):
-                pre = pre + par_ref[3 - d : 4 - d, lanes] * window[16 - d : 16 + Q - d] * col[:, d - 1 : d]
-            gate = jax.nn.sigmoid(pre)
-            out = pre * gate
-            q_ref[rows, lanes] = out
-            ds_ref[rows, lanes] = (gate + out * (1.0 - gate)).astype(bf16)
-        end = cum[Q - 1 : Q, :]
-        weight = dt * jnp.exp(end - cum) * col[:, 4:5]
-        scaled, scaled_low = split(q_ref[rows, 0:DI] * expand(weight, spread))
-        b_rows, b_low = split(q_ref[rows, DI : DI + STATE].T)
-        lin_ref[c, 0:STATE], lin_ref[c, STATE:] = split(state)
-        step = jnp.exp(end) * col[Q - 1 : Q, 3:4]
-        state = state * expand_row(step, spread) + product(b_rows, b_low, scaled, scaled_low)
-        decay = decay * step
-        offset = offset + end
-    wide = expand_row(decay, spread)
-    for half in range(2):
-        lanes = slice(half * HALF, (half + 1) * HALF)
-        pack_ref[half, 0:STATE, :] = state[:, lanes]
-        pack_ref[half, STATE:, :] = jnp.broadcast_to(wide[:, lanes], (8, HALF))
+    col = col_ref[...]
+    dt = jax.nn.softplus(e_ref[...] + head_row(par_ref, STEP_BIAS))
+    cum = tri_sum(tri, dt * rates(par_ref))
+    dt_ref[...] = dt
+    cum_ref[...] = cum
+    all_ref[...] = cum + row_ref[0:1, :]
+    for j in range(CONVCH // 128):
+        lanes = slice(j * 128, (j + 1) * 128)
+        before = jnp.where(step == 0, halo_ref[:, lanes], before_ref[:, lanes])
+        window = jnp.concatenate([before, rc_ref[:, lanes]], axis=0).astype(f32)
+        pre = par_ref[TAP_BIAS : TAP_BIAS + 1, lanes] + par_ref[3:4, lanes] * window[16:]
+        for d in range(1, CONV):
+            pre = pre + par_ref[3 - d : 4 - d, lanes] * window[16 - d : 16 + Q - d] * col[:, d - 1 : d]
+        gate = jax.nn.sigmoid(pre)
+        out = pre * gate
+        q_ref[:, lanes] = out
+        ds_ref[:, lanes] = (gate + out * (1.0 - gate)).astype(bf16)
+    end = cum[Q - 1 : Q, :]
+    weight = dt * jnp.exp(end - cum) * col[:, 4:5]
+    scaled, scaled_low = split(q_ref[:, 0:DI] * expand(weight, spread))
+    b_rows, b_low = split(q_ref[:, DI : DI + STATE].T)
+    state = state_ref[...]
+    lin_ref[0, 0:STATE], lin_ref[0, STATE:] = split(state)
+    fade = jnp.exp(end) * col[Q - 1 : Q, 3:4]
+    state = state * expand_row(fade, spread) + product(b_rows, b_low, scaled, scaled_low)
+    state_ref[...] = state
+    decay = row_ref[1:2, :] * fade
+    row_ref[0:1, :] = row_ref[0:1, :] + end
+    row_ref[1:2, :] = decay
+
+    @pl.when(step == pl.num_programs(0) - 1)
+    def _():
+        wide = expand_row(decay, spread)
+        low = section_ref[0] == 0
+
+        def place_half(half, rows, decays):
+            ours = low if half == 0 else jnp.logical_not(low)
+
+            @pl.when(ours)
+            def _():
+                kept_ref[0:STATE, :] = rows
+                kept_ref[STATE:, :] = decays
+
+            @pl.when(jnp.logical_not(ours))
+            def _():
+                given_ref[0:STATE, :] = rows
+                given_ref[STATE:, :] = decays
+
+        for half in range(2):
+            lanes = slice(half * HALF, (half + 1) * HALF)
+            place_half(half, state[:, lanes], jnp.broadcast_to(wide[:, lanes], (8, HALF)))
 
 
 def intra_kernel(q_ref, dt_ref, cum_ref, col_ref, lab_ref, lin_ref, par_ref, sp_ref, y_ref):
@@ -235,8 +252,8 @@
 
 
 def gate_back_kernel(
-    g_ref, w_ref, y_ref, z_ref, par_ref, c_ref, all_ref, col_ref, decay_ref, sp_ref,
-    dy_ref, dz_ref, dgain_ref, pack_ref, total_ref,
+    section_ref, g_ref, w_ref, y_ref, z_ref, par_ref, c_ref, all_ref, col_ref, kept_ref, given_ref, sp_ref,
+    dy_ref, dz_ref, dgain_ref, to_keep_ref, to_give_ref, total_ref,
 ):
     step = pl.program_id(0)
     dv = nt(g_ref[...], w_ref[...])
@@ -269,9 +286,19 @@
 
     @pl.when(step == pl.num_programs(0) - 1)
     def _():
-        for half in range(2):
-            pack_ref[half, 0:STATE, :] = total_ref[:, half * HALF : (half + 1) * HALF].astype(bf16)
-            pack_ref[half, STATE:, :] = decay_rows(decay_ref[half, STATE : STATE + 1, :])
+        low = section_ref[0] == 0
+        left, right = total_ref[:, 0:HALF], total_ref[:, HALF:]
+        to_keep_ref[0:STATE, :] = jnp.where(low, left, right).astype(bf16)
+        to_give_ref[0:STATE, :] = jnp.where(low, right, left).astype(bf16)
+        to_keep_ref[STATE:, :] = decay_rows(kept_ref[STATE : STATE + 1, :])
+        to_give_ref[STATE:, :] = decay_rows(given_ref[STATE : STATE + 1, :])
+
+
+def four_heads(tile, pair):
+    lane = iota(tile.shape, 1)
+    first = (lane < 128) if pair else ((lane // P_SIZE) % 2 == 0)
+    zero = jnp.zeros_like(tile)
+    return jnp.concatenate([jnp.where(first, tile, zero), jnp.where(first, zero, tile)], axis=0)
 
 
 def intra_back_kernel(
@@ -302,137 +329,154 @@
     same = (col[:, 7:8] == lab_ref[0:1, :]) & (iota((Q, Q), 1) >= iota((Q, Q), 0))
     shut = jnp.where(same, 0.0, masked)
     dscores = jnp.zeros((Q, Q), f32)
-    for j in range(H // 2):
-        lanes = slice(j * 128, (j + 1) * 128)
-        dy_pair = dy[:, lanes]
-        grads = nt(two_heads(x_dt[:, lanes]), dy_pair)
-        mixing = []
+    for g in range(H // 4):
+        wide = slice(g * 256, (g + 1) * 256)
+        grads = nt(four_heads(x_dt[:, wide], False), four_heads(dy[:, wide], True))
         for k in range(2):
-            h = 2 * j + k
-            kernel = jnp.exp(cum_t[h : h + 1, :] - cum[:, h : h + 1] + shut)
-            mixing.append(kernel * scores)
-            dscores = dscores + grads[k * Q : (k + 1) * Q] * kernel
-        mixing, mixing_low = split(jnp.concatenate(mixing, axis=1))
-        pair = two_heads(dy_pair)
-        dx_ref[:, lanes] = base[:, lanes] + nn(mixing, pair) + nn(mixing_low, pair)
+            lanes = slice(g * 256 + k * 128, g * 256 + (k + 1) * 128)
+            mixing = []
+            for m in range(2):
+                h = 4 * g + 2 * k + m
+                kernel = jnp.exp(cum_t[h : h + 1, :] - cum[:, h : h + 1] + shut)
+                mixing.append(kernel * scores)
+                dscores = dscores + grads[m * Q : (m + 1) * Q, k * Q : (k + 1) * Q] * kernel
+            mixed = nn(
+                jnp.concatenate(split(jnp.concatenate(mixing, axis=1)), axis=0),
+                two_heads(dy[:, lanes]),
+            )
+            dx_ref[:, lanes] = base[:, lanes] + (mixed[:Q] + mixed[Q:])
     dx = dx_ref[...]
     near, near_low = split(dy32 * expand(jnp.exp(cum) * col[:, 3:4], spread))
-    far = (dy32 * expand(jnp.exp(all_ref[...]) * col[:, 5:6], spread)).astype(bf16)
+    offset = jnp.exp(all_ref[0:1, :] - cum[0:1, :]) * jnp.max(
+        col[:, 5:6], axis=0, keepdims=True
+    )
+    entered = (
+        lin_ref[0, 0:STATE].astype(f32)
+        + lin_ref[0, STATE:].astype(f32)
+        + expand_row(offset, spread) * inc_ref[...]
+    )
+    entered, entered_low = split(entered)
     low = dscores.astype(bf16)
-    inc_high, inc_low = split(inc_ref[...])
     left = (x_wide * leave).astype(bf16)
     dbc_ref[:, 0:STATE] = nn(low, c_rows) + nt(left, carry_high)
     dbc_ref[:, STATE:] = (
-        nn(dscores.T.astype(bf16), b_rows)
-        + nt(near, lin_ref[0, 0:STATE])
-        + nt(near, lin_ref[0, STATE:])
-        + nt(far, inc_high)
-        + nt(far, inc_low)
+        nn(dscores.T.astype(bf16), b_rows) + nt(near, entered) + nt(near, entered_low)
     )
     hs_ref[:, 0:128] = head_sum(
         dy32 * (y_ref[...] - skip_row(par_ref, spread) * x) - x_wide * dx, spread
     )
-    hs_ref[:, 128:] = head_sum(x * dx, spread)
+    hs_ref[:, 128:] = nt((x * dx).astype(bf16), spread[0:128])
     step = jnp.exp(end) * col[Q - 1 : Q, 3:4]
     c_rows, c_low = split(q_ref[:, DI + STATE :].T)
     carry_ref[...] = carry * expand_row(step, spread) + product(c_rows, c_low, near, near_low)
 
 
 def conv_back_kernel(
-    outg_ref, inc_ref, q_ref, ds_ref, dt_ref, all_ref, col_ref, e_ref, rc_ref, halo_ref,
+    outg_ref, inc_ref, q_ref, ds_ref, dt_ref, all_ref, col_ref, e_ref, rc_ref, before_ref, halo_ref,
     dy_ref, dx_ref, dbc_ref, hs_ref, par_ref, sp_ref,
-    dr_ref, de_ref, tail_ref, back_ref, dw_ref, dh_ref, pre_ref, sum_ref,
+    dr_ref, de_ref, tail_ref, back_ref, dw_ref, dh_ref, pre_ref, sum_ref, row_ref, skip_ref,
 ):
-    count = q_ref.shape[0] // Q
+    count = dt_ref.shape[0] // Q
+    step = pl.program_id(0)
     spread = sp_ref[...]
-    outg = outg_ref[...]
     last = all_ref[count * Q - 1 : count * Q, :]
-    skip = skip_row(par_ref, spread)
-    rate = rates(par_ref)
-    bias = head_row(par_ref, STEP_BIAS)
-    total = jnp.zeros((1, 128), f32)
-    skip_total = jnp.zeros((1, 128), f32)
-    pre_ref[0:8, :] = jnp.zeros((8, CONVCH), f32)
-    pre_ref[8 + count * Q :, :] = jnp.zeros((8, CONVCH), f32)
-    for c in range(count):
-        rows = slice(c * Q, (c + 1) * Q)
-        moved = slice(8 + c * Q, 8 + (c + 1) * Q)
-        col = col_ref[moved, :]
-        x = q_ref[rows, 0:DI]
-        dy = dy_ref[rows, :].astype(f32)
-        wide_dt = expand(dt_ref[rows, :], spread)
-        x_dt = (x * wide_dt).astype(bf16).astype(f32)
-        leave = expand(jnp.exp(last - all_ref[rows, :]) * col[:, 6:7], spread)
-        dx_far = leave * nn(q_ref[rows, DI : DI + STATE].astype(bf16), outg)
-        dx = dx_ref[rows, :] + dx_far
-        db = dbc_ref[rows, 0:STATE] + nt((x_dt * leave).astype(bf16), outg)
-        far = head_sum(x_dt * dx_far, spread)
-        total = total + jnp.sum(far, axis=0, keepdims=True)
-        sum_ref[rows, 0:128] = hs_ref[rows, 0:128] - far
-        sum_ref[rows, 128:] = hs_ref[rows, 128:] + head_sum(x * dx_far, spread)
-        skip_total = skip_total + jnp.sum(head_sum(x * dy, spread), axis=0, keepdims=True)
-        pre_ref[moved, 0:DI] = (wide_dt * dx + skip * dy) * ds_ref[rows, 0:DI].astype(f32)
-        pre_ref[moved, DI : DI + STATE] = db * ds_ref[rows, DI : DI + STATE].astype(f32)
-        pre_ref[moved, DI + STATE :] = dbc_ref[rows, STATE:] * ds_ref[rows, DI + STATE :].astype(f32)
-    kept = jnp.exp(last) * col_ref[7 + count * Q : 8 + count * Q, 5:6]
-    both = jnp.sum(outg.astype(f32) * inc_ref[...], axis=0, keepdims=True)
-    through = kept * head_sum(jnp.broadcast_to(both, (8, DI)), spread)[0:1]
-    tri = (iota((Q, Q), 0) <= iota((Q, Q), 1)).astype(bf16)
-    later = total + through
-    rate_total = jnp.zeros((1, 128), f32)
-    bias_total = jnp.zeros((1, 128), f32)
-    for c in reversed(range(count)):
-        rows = slice(c * Q, (c + 1) * Q)
+
+    @pl.when(step == 0)
+    def _():
+        pre_ref[0:8, :] = jnp.zeros((8, CONVCH), f32)
+        pre_ref[8 + count * Q :, :] = jnp.zeros((8, CONVCH), f32)
+        row_ref[...] = jnp.zeros_like(row_ref)
+        skip_ref[...] = jnp.zeros_like(skip_ref)
+
+    @pl.when(step < count)
+    def _():
+        start = pl.multiple_of(step * Q, Q)
+        rows = pl.ds(start, Q)
+        moved = pl.ds(pl.multiple_of(start + 8, 8), Q)
+        outg = outg_ref[...]
+        dt = dt_ref[rows, :]
+        x = q_ref[:, 0:DI]
+        dy = dy_ref[...].astype(f32)
+        wide_dt = expand(dt, spread)
+        leave = expand(jnp.exp(last - all_ref[rows, :]) * col_ref[moved, 6:7], spread)
+        dx_far = leave * nn(q_ref[:, DI : DI + STATE].astype(bf16), outg)
+        dx = dx_ref[...] + dx_far
+        db = dbc_ref[rows, 0:STATE] + nt((x * wide_dt * leave).astype(bf16), outg)
+        far = head_sum(x * dx_far, spread)
+        row_ref[0:1, :] = row_ref[0:1, :] + jnp.sum(dt * far, axis=0, keepdims=True)
+        sum_ref[rows, 0:128] = hs_ref[rows, 0:128] - dt * far
+        sum_ref[rows, 128:] = hs_ref[rows, 128:] + far
+        skip_ref[0:1, :] = skip_ref[0:1, :] + jnp.sum(x * dy, axis=0, keepdims=True)
+        skip = skip_row(par_ref, spread)
+        pre_ref[moved, 0:DI] = (wide_dt * dx + skip * dy) * ds_ref[:, 0:DI].astype(f32)
+        pre_ref[moved, DI : DI + STATE] = db * ds_ref[:, DI : DI + STATE].astype(f32)
+        pre_ref[moved, DI + STATE :] = dbc_ref[rows, STATE:] * ds_ref[:, DI + STATE :].astype(f32)
+
+    @pl.when(step == count)
+    def _():
+        kept = jnp.exp(last) * col_ref[7 + count * Q : 8 + count * Q, 5:6]
+        both = jnp.sum(outg_ref[...].astype(f32) * inc_ref[...], axis=0, keepdims=True)
+        row_ref[0:1, :] = (
+            row_ref[0:1, :] + kept * head_sum(jnp.broadcast_to(both, (8, DI)), spread)[0:1]
+        )
+        row_ref[3:4, :] = head_sum(skip_ref[...], spread)[0:1]
+        dw_ref[...] = jnp.zeros_like(dw_ref)
+
+    @pl.when(step >= count)
+    def _():
+        c = 2 * count - 1 - step
+        start = pl.multiple_of(c * Q, Q)
+        rows = pl.ds(start, Q)
+        rate = rates(par_ref)
+        tri = (iota((Q, Q), 0) <= iota((Q, Q), 1)).astype(bf16)
         sums = tri_sum(tri, sum_ref[rows, 0:128])
-        dlog = sums + later
-        later = later + sums[0:1]
+        dlog = sums + row_ref[0:1, :]
+        row_ref[0:1, :] = row_ref[0:1, :] + sums[0:1]
         ddt = rate * dlog + sum_ref[rows, 128:]
-        de = ddt * jax.nn.sigmoid(e_ref[rows, :] + bias)
-        de_ref[rows, :] = jnp.where(iota((Q, 128), 1) < H, de, 0.0).astype(bf16)
-        rate_total = rate_total + jnp.sum(dlog * dt_ref[rows, :], axis=0, keepdims=True)
-        bias_total = bias_total + jnp.sum(de, axis=0, keepdims=True)
-    row = iota((8, 128), 0)
-    dh_ref[...] = jnp.where(
-        row == 0,
-        bias_total,
-        jnp.where(row == 1, rate_total * rate, jnp.where(row == 2, skip_total, 0.0)),
-    )
-    for j in range(CONVCH // 128):
-        lanes = slice(j * 128, (j + 1) * 128)
-        taps = [par_ref[3 - d : 4 - d, lanes] for d in range(CONV)]
-        sums = [jnp.zeros((1, 128), f32) for _ in range(CONV + 1)]
-        front = pre_ref[0:16, lanes]
-        early = jnp.zeros((8, 128), f32)
-        for d in range(1, CONV):
-            early = early + taps[d] * (front * col_ref[0:16, d - 1 : d])[d : d + 8]
-        back_ref[:, lanes] = early
-        for c in range(count):
-            rows = slice(c * Q, (c + 1) * Q)
-            ahead = pre_ref[8 + c * Q : 16 + (c + 1) * Q, lanes]
-            col = col_ref[8 + c * Q : 16 + (c + 1) * Q, :]
-            if c == 0:
-                window = jnp.concatenate([halo_ref[:, lanes], rc_ref[0:Q, lanes]], axis=0)
-            else:
-                window = rc_ref[c * Q - 16 : (c + 1) * Q, lanes]
-            window = window.astype(f32)
+        de = ddt * jax.nn.sigmoid(e_ref[rows, :] + head_row(par_ref, STEP_BIAS))
+        de_ref[...] = jnp.where(iota((Q, 128), 1) < H, de, 0.0).astype(bf16)
+        row_ref[1:2, :] = row_ref[1:2, :] + jnp.sum(de, axis=0, keepdims=True)
+        row_ref[2:3, :] = row_ref[2:3, :] + rate * jnp.sum(
+            dlog * dt_ref[rows, :], axis=0, keepdims=True
+        )
+        around = pl.ds(pl.multiple_of(start + 8, 8), Q + 8)
+        col = col_ref[around, :]
+        row = iota((8, 128), 0)
+        for j in range(CONVCH // 128):
+            lanes = slice(j * 128, (j + 1) * 128)
+            taps = [par_ref[3 - d : 4 - d, lanes] for d in range(CONV)]
+            ahead = pre_ref[around, lanes]
+            before = jnp.where(c == 0, halo_ref[:, lanes], before_ref[:, lanes])
+            window = jnp.concatenate([before, rc_ref[:, lanes]], axis=0).astype(f32)
             here = ahead[0:Q]
-            sums[CONV] = sums[CONV] + jnp.sum(here, axis=0, keepdims=True)
-            sums[3] = sums[3] + jnp.sum(here * window[16:], axis=0, keepdims=True)
+            found = [None] * (CONV + 1)
+            found[CONV] = jnp.sum(here, axis=0, keepdims=True)
+            found[3] = jnp.sum(here * window[16:], axis=0, keepdims=True)
             grad = taps[0] * here
             for d in range(1, CONV):
                 same = ahead * col[:, d - 1 : d]
-                sums[3 - d] = sums[3 - d] + jnp.sum(
+                found[3 - d] = jnp.sum(
                     same[0:Q] * window[16 - d : 16 + Q - d], axis=0, keepdims=True
                 )
                 grad = grad + taps[d] * same[d : d + Q]
-            dr_ref[rows, lanes] = grad.astype(bf16)
-            if c == count - 1:
-                tail_ref[:, lanes] = grad[Q - 8 :]
-        row = iota((8, 128), 0)
-        stacked = jnp.zeros((8, 128), f32)
-        for k in range(CONV + 1):
-            stacked = jnp.where(row == k, sums[k], stacked)
-        dw_ref[:, lanes] = stacked
+            dr_ref[:, lanes] = grad.astype(bf16)
+            tail_ref[:, lanes] = jnp.where(step == count, grad[Q - 8 :], tail_ref[:, lanes])
+            stacked = jnp.zeros((8, 128), f32)
+            for k in range(CONV + 1):
+                stacked = jnp.where(row == k, found[k], stacked)
+            dw_ref[:, lanes] = dw_ref[:, lanes] + stacked
+
+    @pl.when(step == 2 * count - 1)
+    def _():
+        dh_ref[0:3, :] = row_ref[1:4, :]
+        for j in range(CONVCH // 128):
+            lanes = slice(j * 128, (j + 1) * 128)
+            front = pre_ref[0:16, lanes]
+            early = jnp.zeros((8, 128), f32)
+            for d in range(1, CONV):
+                tap = par_ref[3 - d : 4 - d, lanes]
+                early = early + tap * (front * col_ref[0:16, d - 1 : d])[d : d + 8]
+            back_ref[:, lanes] = early
 
 
 def params(steps):
@@ -452,6 +496,10 @@
 
 def conv_forward(rc, halo, e, col, par, spread):
     rows = rc.shape[0]
+
+    def by_row(width):
+        return pl.BlockSpec((Q, width), lambda i: (i, 0))
+
     outs = (
         shape(rows, CONVCH),
         shape(rows, CONVCH, dtype=bf16),
@@ -459,11 +507,37 @@
         shape(rows, 128),
         shape(rows, 128),
         shape(rows // Q, 2 * STATE, DI, dtype=bf16),
-        shape(2, PACK_WIDE, HALF),
+        shape(PACK_WIDE, HALF),
+        shape(PACK_WIDE, HALF),
     )
-    return pl.pallas_call(conv_kernel, out_shape=outs, compiler_params=params(0))(
-        rc, halo, e, col, par, spread
-    )
+    section = lax.axis_index("section").astype(jnp.int32)[None]
+    return pl.pallas_call(
+        conv_kernel,
+        grid=(rows // Q,),
+        in_specs=[
+            pl.BlockSpec(memory_space=pltpu.SMEM),
+            by_row(CONVCH),
+            pl.BlockSpec((16, CONVCH), lambda i: (jnp.maximum(i * (Q // 16) - 1, 0), 0)),
+            whole(halo),
+            by_row(128),
+            by_row(128),
+            whole(par),
+            whole(spread),
+        ],
+        out_specs=(
+            by_row(CONVCH),
+            by_row(CONVCH),
+            by_row(128),
+            by_row(128),
+            by_row(128),
+            pl.BlockSpec((1, 2 * STATE, DI), lambda i: (i, 0, 0)),
+            whole(outs[-2]),
+            whole(outs[-1]),
+        ),
+        out_shape=outs,
+        scratch_shapes=[pltpu.VMEM((STATE, DI), f32), pltpu.VMEM((8, 128), f32)],
+        compiler_params=params(1),
+    )(section, rc, rc, halo, e, col, par, spread)
 
 
 def intra_forward(q, dt, cum, col, lab, lin, par, spread):
@@ -522,7 +596,7 @@
     )(y0, z, q, total, col, inc, par, w_out, hidden, spread)
 
 
-def gate_backward(grad, w_out, y, z, par, q, total, col, pack, spread):
+def gate_backward(grad, w_out, y, z, par, q, total, col, kept, given, spread):
     rows = y.shape[0]
     size = 256
 
@@ -533,12 +607,15 @@
         shape(rows, DI, dtype=bf16),
         shape(rows, DI, dtype=bf16),
         shape(1, DI),
-        shape(2, PACK, HALF, dtype=bf16),
+        shape(PACK, HALF, dtype=bf16),
+        shape(PACK, HALF, dtype=bf16),
     )
+    section = lax.axis_index("section").astype(jnp.int32)[None]
     return pl.pallas_call(
         gate_back_kernel,
         grid=(rows // size,),
         in_specs=[
+            pl.BlockSpec(memory_space=pltpu.SMEM),
             by_row(D),
             whole(w_out),
             by_row(DI),
@@ -547,14 +624,15 @@
             pl.BlockSpec((size, STATE), lambda i: (i, (DI + STATE) // STATE)),
             by_row(128),
             by_row(128),
-            whole(pack),
+            whole(kept),
+            whole(given),
             whole(spread),
         ],
-        out_specs=(by_row(DI), by_row(DI), whole(outs[2]), whole(outs[3])),
+        out_specs=(by_row(DI), by_row(DI), whole(outs[2]), whole(outs[3]), whole(outs[4])),
         out_shape=outs,
         scratch_shapes=[pltpu.VMEM((STATE, DI), f32)],
         compiler_params=params(1),
-    )(grad, w_out, y, z, par, q, total, col, pack, spread)
+    )(section, grad, w_out, y, z, par, q, total, col, kept, given, spread)
 
 
 def intra_backward(q, dt, cum, total, col, lab, lin, inc, dy, y, par, spread):
@@ -593,6 +671,17 @@
 
 def conv_backward(outg, inc, q, ds, dt, total, col, e, rc, halo, dy, dx, dbc, hs, par, spread):
     rows = q.shape[0]
+    count = rows // Q
+
+    def first(width):
+        return pl.BlockSpec((Q, width), lambda i: (jnp.minimum(i, count - 1), 0))
+
+    def back(i):
+        return jnp.minimum(2 * count - 1 - i, count - 1)
+
+    def second(width):
+        return pl.BlockSpec((Q, width), lambda i: (back(i), 0))
+
     outs = (
         shape(rows, CONVCH, dtype=bf16),
         shape(rows, 128, dtype=bf16),
@@ -603,10 +692,36 @@
     )
     return pl.pallas_call(
         conv_back_kernel,
+        grid=(2 * count,),
+        in_specs=[
+            whole(outg),
+            whole(inc),
+            first(CONVCH),
+            first(CONVCH),
+            whole(dt),
+            whole(total),
+            whole(col),
+            whole(e),
+            second(CONVCH),
+            pl.BlockSpec((16, CONVCH), lambda i: (jnp.maximum(back(i) * (Q // 16) - 1, 0), 0)),
+            whole(halo),
+            first(DI),
+            first(DI),
+            whole(dbc),
+            whole(hs),
+            whole(par),
+            whole(spread),
+        ],
+        out_specs=(second(CONVCH), second(128)) + tuple(whole(out) for out in outs[2:]),
         out_shape=outs,
-        scratch_shapes=[pltpu.VMEM((rows + 16, CONVCH), f32), pltpu.VMEM((rows, 256), f32)],
-        compiler_params=params(0),
-    )(outg, inc, q, ds, dt, total, col, e, rc, halo, dy, dx, dbc, hs, par, spread)
+        scratch_shapes=[
+            pltpu.VMEM((rows + 16, CONVCH), f32),
+            pltpu.VMEM((rows, 256), f32),
+            pltpu.VMEM((8, 128), f32),
+            pltpu.VMEM((8, DI), f32),
+        ],
+        compiler_params=params(1),
+    )(outg, inc, q, ds, dt, total, col, e, rc, rc, halo, dy, dx, dbc, hs, par, spread)
 
 
 def pick(first, a, b):
@@ -631,11 +746,9 @@
     return (earlier[0] * later[0], later[0] * earlier[1] + later[1])
 
 
-def chain_scan(pack, reverse, beside):
+def chain_scan(kept, given, reverse, beside):
     section = lax.axis_index("section")
     size = lax.axis_size("seq")
-    kept = lax.dynamic_index_in_dim(pack, section, 0, keepdims=False)
-    given = lax.dynamic_index_in_dim(pack, 1 - section, 0, keepdims=False)
     got = lax.ppermute(given, "section", SWAP)
     leads = (section == 1) if reverse else (section == 0)
     lead = unpack(pick(leads, kept, got))
@@ -649,7 +762,7 @@
         route = [(i, i + distance) for i in range(size - distance)]
         if reverse:
             route = [(b, a) for a, b in route]
-        sent = pack_up(reached, pack.dtype)
+        sent = pack_up(reached, kept.dtype)
         if beside:
             arrays, work = beside.pop(0)
             sent, arrays = tie(sent, arrays)
@@ -665,37 +778,40 @@
         distance *= 2
     first = before[1]
     second = lead[1] + lead[0] * first
-    own = pick(leads, first, second).astype(pack.dtype)
-    other = lax.ppermute(pick(leads, second, first).astype(pack.dtype), "section", SWAP)
+    own = pick(leads, first, second).astype(kept.dtype)
+    other = lax.ppermute(pick(leads, second, first).astype(kept.dtype), "section", SWAP)
     low = section == 0
     incoming = jnp.concatenate([pick(low, own, other), pick(low, other, own)], axis=1)
     return incoming, results
 
 
-def move_rows(shard, layer):
+def move_rows(shard):
     parts = lax.axis_size("fsdp")
     blocks = [shard]
     for shift in range(1, parts):
-        route = [(layer * parts + i, layer * parts + (i + shift) % parts) for i in range(parts)]
-        blocks.append(lax.ppermute(shard, ("section", "fsdp"), route))
+        blocks.append(lax.ppermute(shard, "fsdp", [(i, (i + shift) % parts) for i in range(parts)]))
     return blocks
 
 
-def share(blocks, layer):
+def share(blocks):
     section, row = lax.axis_index("section"), lax.axis_index("fsdp")
     parts = lax.axis_size("fsdp")
-    across = [(layer, 1 - layer)]
-    blocks = [pick(section == layer, block, lax.ppermute(block, "section", across)) for block in blocks]
-    if parts == 2:
-        low = row == 0
-        return [pick(low, blocks[0], blocks[1]), pick(low, blocks[1], blocks[0])]
-    ordered = []
-    for k in range(parts):
-        block = blocks[0]
-        for shift in range(1, parts):
-            block = pick((row - shift) % parts == k, blocks[shift], block)
-        ordered.append(block)
-    return ordered
+    others = [lax.ppermute(block, "section", SWAP) for block in blocks]
+    layers = []
+    for layer in range(2):
+        held = [pick(section == layer, a, b) for a, b in zip(blocks, others)]
+        if parts == 2:
+            low = row == 0
+            layers.append([pick(low, held[0], held[1]), pick(low, held[1], held[0])])
+            continue
+        ordered = []
+        for k in range(parts):
+            block = held[0]
+            for shift in range(1, parts):
+                block = pick((row - shift) % parts == k, held[shift], block)
+            ordered.append(block)
+        layers.append(ordered)
+    return layers
 
 
 def row_sum(summed):
@@ -855,15 +971,14 @@
         ]
         return gate, jnp.concatenate(back, axis=0)
 
-    w_conv, w_step, w_gate, w_back = [[None, None] for _ in range(4)]
-    blocks = move_rows(shard_conv, 0)
+    blocks = move_rows(shard_conv)
     hidden = to_chain(tokens)
-    blocks = share(blocks, 0)
-    shard_conv, shard_rest, blocks, cotangent = tie(shard_conv, shard_rest, blocks, cotangent)
-    w_conv[0], w_step[0] = join_conv(blocks)
-    moved_rest = move_rows(shard_rest, 0)
-
     top_grad = to_chain(cotangent)
+    blocks, hidden, shard_rest, top_grad = tie(blocks, hidden, shard_rest, top_grad)
+    joined = [join_conv(layer) for layer in share(blocks)]
+    w_conv, w_step = [[pair[k] for pair in joined] for k in range(2)]
+    moved_rest = move_rows(shard_rest)
+    w_gate, w_back = [None, None], [None, None]
 
     table = parameter_table(
         norm_gain, conv_w[0], conv_b, dt_bias, a_log, skip_scale, gate_gain
@@ -881,63 +996,58 @@
     ]
     precede = [(b, a) for a, b in follow]
 
-    def to_holders(array, layer):
-        return tuple(
-            lax.ppermute(
-                array,
-                everywhere,
-                [
-                    (flat(s, 2 * k + m), flat(layer, 2 * k + s))
-                    for k in range(size // 2)
-                    for s in range(2)
-                ],
-            )
-            for m in range(2)
+    routes = [[], []]
+    for k in range(size // 2):
+        for s in range(2):
+            for m in range(2):
+                for way in range(2):
+                    routes[way].append((flat(s, 2 * k + m), flat((m + way) % 2, 2 * k + s)))
+
+    def to_holders(first, second):
+        even = micro == 0
+        return (
+            lax.ppermute(pick(even, first, second), everywhere, routes[0]),
+            lax.ppermute(pick(even, second, first), everywhere, routes[1]),
         )
 
-    def held(first, second):
-        stacked = jnp.stack([pick(low, first[m], second[m]) for m in range(2)])
-        return stacked[None, :, None]
+    def held(one, two):
+        return jnp.stack([pick(low, one, two), pick(low, two, one)])[None, :, None]
 
     kept = []
     results = []
     for layer in range(2):
         par = tables[layer]
-        if layer == 1:
-            w_conv[1], w_step[1] = join_conv(second_conv)
         wide = hidden.astype(f32)
         scale = lax.rsqrt(jnp.mean(wide * wide, axis=1, keepdims=True) + epsilon)
         u = (wide * scale * par[NORM : NORM + 1, :D]).astype(bf16)
         rc = nt(u, w_conv[layer]).astype(bf16)
         e = nt(u, w_step[layer])
         halo = lax.ppermute(rc[rows - 16 :], everywhere, follow)
-        q, ds, dt, cum, total, lin, pack = conv_forward(
+        q, ds, dt, cum, total, lin, to_keep, to_give = conv_forward(
             rc, halo, e, col, par, spread
         )
-        def beside_first(_, shards, *arrays):
-            following = move_rows(shards, 1) if layer == 0 else ()
-            return intra_forward(*arrays, spread), following
-
-        def beside_second(following, moved, u):
-            gate, back = join_rest(share(moved, layer))
-            return nt(u, gate), (gate, back, following)
-
-        inc, ((y0, _), (z, (w_gate[layer], w_back[layer], following))) = chain_scan(
-            pack,
+        def beside_first(_, *arrays):
+            return intra_forward(*arrays, spread), None
+
+        def beside_second(_, u, moved):
+            if layer == 0:
+                for k, blocks in enumerate(share(moved)):
+                    w_gate[k], w_back[k] = join_rest(blocks)
+            return nt(u, w_gate[layer]), None
+
+        inc, ((y0, _), (z, _)) = chain_scan(
+            to_keep,
+            to_give,
             False,
             [
-                ((shard_conv, q, dt, cum, col, lab, lin, par), beside_first),
-                ((moved_rest, u), beside_second),
+                ((q, dt, cum, col, lab, lin, par), beside_first),
+                ((u, moved_rest if layer == 0 else ()), beside_second),
             ],
         )
-        if layer == 0:
-            inc, following, shard_rest, top_grad = tie(inc, following, shard_rest, top_grad)
-            second_conv = share(following, 1)
-            moved_rest = move_rows(shard_rest, 1)
         y, v, out = gate_forward(
             y0, z, q, total, col, inc, par, w_back[layer], hidden, spread
         )
-        kept.append((hidden, scale, u, rc, e, halo, q, ds, dt, cum, total, lin, pack, inc, z, y, v))
+        kept.append((hidden, scale, u, rc, e, halo, q, ds, dt, cum, total, lin, to_keep, to_give, inc, z, y, v))
         results.append(out)
         hidden = out
 
@@ -975,19 +1085,19 @@
     grads = [None, None]
     for layer in (1, 0):
         par = tables[layer]
-        hidden, scale, u, rc, e, halo, q, ds, dt, cum, total, lin, pack, inc, z, y, v = kept[layer]
-        dy, dz, dgain, back = gate_backward(
-            grad, w_back[layer], y, z, par, q, total, col, pack, spread
+        hidden, scale, u, rc, e, halo, q, ds, dt, cum, total, lin, to_keep, to_give, inc, z, y, v = kept[layer]
+        dy, dz, dgain, back, back_given = gate_backward(
+            grad, w_back[layer], y, z, par, q, total, col, to_keep, to_give, spread
         )
         extra = ()
         if layer == 0:
-            back, early[1], late[1] = tie(back, early[1], late[1])
-            extra = late[1]
+            back, back_given, early[1], late[1], acts = tie(back, back_given, early[1], late[1], acts)
+            extra = (early[1], late[1])
         given = early_grads(u, dz, v, grad)(1 - section).astype(bf16)
 
         def first(_, extra, given, *arrays):
             if layer == 0:
-                extra = halve(extra, 1)
+                extra = (halve(extra[0], 1), halve(extra[1], 1))
             got = lax.ppermute(given, "section", SWAP)
             return (intra_backward(*arrays, spread), extra, got), None
 
@@ -996,6 +1106,7 @@
 
         outg, ((((dx, dbc, hs), extra, got), _), ((du, kept_half), _)) = chain_scan(
             back,
+            back_given,
             True,
             [
                 ((extra, given, q, dt, cum, total, col, lab, lin, inc, dy, y, par), first),
@@ -1005,30 +1116,29 @@
         summed = (kept_half + got.astype(f32)).astype(bf16)
         early[layer] = row_sum(summed)
         if layer == 0:
-            outg, extra, holding = tie(outg, extra, holding)
-            upper = halve(jnp.concatenate([early[1], extra], axis=0), 2)
-            grads[1] = to_holders(holding, 1)
+            outg, extra = tie(outg, extra)
         else:
             outg, results = tie(outg, results)
-            acts = [to_holders(results[k], k) for k in range(2)]
+            acts = to_holders(*results)
         dr, de, tail, front, dw, dh = conv_backward(
             outg, inc, q, ds, dt, total, col_padded, e, rc, halo, dy, dx, dbc, hs, par, spread
         )
         if layer == 1:
             front, early[1] = tie(front, early[1])
-            early[1] = halve(early[1], 1)
+        else:
+            front, extra = tie(front, extra)
+            upper = halve(jnp.concatenate(extra, axis=0), 2)
         returned = lax.ppermute(front, everywhere, precede)
-        if layer == 0:
-            returned, pieces[1], upper = tie(returned, pieces[1], upper)
-            upper = halve(upper, 4) if size > 4 else upper
         dr = lax.dynamic_update_slice(dr, (tail + returned).astype(bf16), (rows - 8, 0))
         given = late_grads(u, dr)(1 - section).astype(bf16)
         given, dr, de = tie(given, dr, de)
         got = lax.ppermute(given, "section", SWAP)
         summed = (late_grads(u, dr)(section) + got.astype(f32)).astype(bf16)
         if layer == 0:
-            summed, early[0], grads[1] = tie(summed, early[0], grads[1])
+            summed, early[0], upper, pieces[1] = tie(summed, early[0], upper, pieces[1])
             early[0] = halve(early[0], 1)
+            upper = halve(upper, 4) if size > 4 else upper
+        summed, dr, de = tie(summed, dr, de)
         late[layer] = row_sum(summed)
         du = du + nn(dr, w_conv[layer]) + nn(de, w_step[layer])
         wide = hidden.astype(f32)
@@ -1039,10 +1149,9 @@
         grad_e = columns(de, u)[:H].reshape(H // 2, 2 * D)
         grad = (grad.astype(f32) + dhidden).astype(bf16)
         if layer == 1:
-            grad, acts = tie(grad, acts)
             holding = grad
         else:
-            grads[0] = to_holders(grad, 0)
+            grads = to_holders(grad, holding)
         pieces[layer] = (dw, dnorm, dgain, dh, grad_e)
 
     def table_of(dw, dnorm, dgain, dh, grad_e):
@@ -1061,26 +1170,34 @@
     small = [table_of(*pieces[layer]) for layer in range(2)]
     mine = pick(low, small[0], small[1]) + lax.ppermute(pick(low, small[1], small[0]), "section", SWAP)
     mine = exchange_sum(mine, steps[0])
-    late[0], early[0], mine, grads[0], upper = tie(late[0], early[0], mine, grads[0], upper)
+    late[0], early[0], mine, upper = tie(late[0], early[0], mine, upper)
     far = distances()
+    for distance in far[3:]:
+        upper = halve(upper, distance)
     late[0] = halve(late[0], 1)
     mine = exchange_sum(mine, steps[1])
-    late[0], mine = tie(late[0], mine)
-    for distance in far[3:]:
-        upper = halve(upper, distance)
     for distance in far[1:]:
+        early[0] = halve(early[0], distance)
+    for distance in reversed(far[1:]):
+        upper = rejoin(upper, distance)
+    for distance in far[1:2]:
         late[0] = halve(late[0], distance)
-        early[0] = halve(early[0], distance)
+    late[0], early[0], mine, grads, upper = tie(late[0], early[0], mine, grads, upper)
+    early[1], late[1] = rejoin(upper[:HALF], 1), rejoin(upper[HALF:], 1)
+    for distance in far[2:]:
+        late[0] = halve(late[0], distance)
     for step in steps[2:]:
         mine = exchange_sum(mine, step)
     for distance in reversed(far[1:]):
+        early[0] = rejoin(early[0], distance)
+    for distance in reversed(far[2:]):
         late[0] = rejoin(late[0], distance)
-        early[0] = rejoin(early[0], distance)
-        upper = rejoin(upper, distance)
+    late[0], early[0], mine, upper = tie(late[0], early[0], mine, (early[1], late[1]))
+    early[1], late[1] = upper
+    early[0] = rejoin(early[0], 1)
+    for distance in far[1:2]:
+        late[0] = rejoin(late[0], distance)
     late[0] = rejoin(late[0], 1)
-    early[0] = rejoin(early[0], 1)
-    split_at = early[0].shape[0] // 2
-    early[1], late[1] = rejoin(upper[:split_at], 1), rejoin(upper[split_at:], 1)
     early_got = lax.ppermute(pick(low, early[1], early[0]), "section", SWAP)
     late_got = lax.ppermute(pick(low, late[1], late[0]), "section", SWAP)
     early_own, late_own = pick(low, early[0], early[1]), pick(low, late[0], late[1])

time: 591 us -> 545 us (0.922)
  starting transfers between devices: 137 us -> 98.2 us
  Pallas kernels: 140 us -> 131 us
    ppermute x24 -> x14, starting transfers between devices: 48.2 us -> 13.9 us  [the longest x2 4.84 us: move_rows(): lax.ppermute(shard, 'fsdp', [(i, (i + shift) % parts) for i in range(part...]
    ppermute x10, waiting for transfers between devices: 41.9 us -> 23.3 us  [rejoin(): got = lax.ppermute(array, 'seq', [(i, i ^ distance) for i in range(size)])]
    ppermute x24 -> x14, waiting for transfers between devices: 13.6 us -> 27.5 us  [the longest x2 23.1 us: move_rows(): lax.ppermute(shard, 'fsdp', [(i, (i + shift) % parts) for i in range(part...]
    ppermute x4, waiting for transfers between devices: 13.1 us -> 2.15 us  [row_sum(): got = lax.ppermute(given, 'fsdp', SWAP)]
    ppermute x4, starting transfers between devices: 3.85 us -> 12 us  [chain_scan(): got = lax.ppermute(given, 'section', SWAP)]
    ppermute x2, waiting for transfers between devices: 0.01 us -> 7.36 us  [to_chain(): return pick(aligned, own, lax.ppermute(given, everywhere, exchange))]
    select_n x29 -> x30, other arithmetic: 16.9 us -> 21.8 us  [pick(): return jnp.where(first, a, b)]
    unnamed x317 -> x356, local copies, waits for them, and re-layouts: 26.8 us -> 28.7 us
  transfers between devices with their start and end apart: 78 -> 68, of which waited for: 27 -> 34; matrix products, arithmetic and copies ran while one was open for 18% -> 19% of each run, Pallas kernels for 20% -> 18%
where the time goes in v3:
time: 545 us; the launch traced here: 535 us
  waiting for transfers between devices  146 us (27%)
  Pallas kernels  131 us (24%)
  starting transfers between devices  98.2 us (18%)
  other arithmetic  66 us (12%)
  local copies, waits for them, and re-layouts  51.5 us (9%)
  matrix products  38.3 us (7%)
    ppermute x10, waiting for transfers between devices, halve(): got = lax.ppermute(given, 'seq', [(i, i ^ distance) for i in range(size)])  38.5 us
    pallas_call x2, Pallas kernels, conv_backward(): pl.pallas_call(conv_back_kernel, grid=(2 * count,), in_specs=[whole(outg)...  30.2 us
    pallas_call x2, Pallas kernels, intra_backward(): pl.pallas_call(intra_back_kernel, grid=(rows // Q,), in_specs=[by_row(CON...  29.8 us
    unnamed x356, local copies, waits for them, and re-layouts  28.7 us
    ppermute x8, starting transfers between devices, chain_scan(): arrived = lax.ppermute(sent, 'seq', route)  25.7 us
    ppermute x8, waiting for transfers between devices, chain_scan(): arrived = lax.ppermute(sent, 'seq', route)  23.5 us
    ppermute x10, waiting for transfers between devices, rejoin(): got = lax.ppermute(array, 'seq', [(i, i ^ distance) for i in range(size)])  23.3 us
    ppermute x2, waiting for transfers between devices, move_rows(): lax.ppermute(shard, 'fsdp', [(i, (i + shift) % parts) for i in range(part...  23.1 us
  transfers between devices with their start and end apart: 68, of which 34 were waited for; matrix products, arithmetic and copies ran while one was open for 19% of the time, Pallas kernels for 18%

profile of v3, /device:TPU:0, one launch (start us, length us, event | category | flops | bytes accessed | tf_op | source)
XLA Modules:
  0.0 535.0 jit_solution(1203701939204715643)
XLA Ops:
  2.3 3.0 collective-permute-start
  7.5 4.3 collective-permute-start.1
  22.0 7.1 %collective-permute-done.2 = bf16[512,768]{1,0:T(8,128)(2,1)} collective-permute-done((bf16[512,768]{1,0:T(8,128)(2,1)}, bf16[512,768]{1,0:T(8,128)(2,1)}, u32[]{:S(2)}, u32[]{:S(2)}) %collective-permute-start.2) | collective-permute-done | bytes 786464 | tf_op jit(solution)/shard_map/ppermute | solution.py:951
  30.1 6.0 %collective-permute-done = bf16[1824,384]{1,0:T(8,128)(2,1)} collective-permute-done((bf16[1824,384]{1,0:T(8,128)(2,1)S(1)}, bf16[1824,384]{1,0:T(8,128)(2,1)}, u32[]{:S(2)}, u32[]{:S(2)}) %collective-permute-start) | collective-permute-done | bytes 1400864 | tf_op jit(solution)/shard_map/ppermute | solution.py:792
  42.1 3.2 broadcast_select_fusion.12
  49.6 8.8 %shard_map.213 = (f32[512,1792]{1,0:T(8,128)}, bf16[512,1792]{1,0:T(8,128)(2,1)S(1)}, f32[512,128]{1,0:T(8,128)S(1)}, f32[512,128]{1,0:T(8,128)S(1)}, f32[512,12...) custom-call(s32[1]{0:T(128)} %bitcast.section_ref, ...), custom_call_target="tpu_custom_call" | custom-call | tf_op jit(solution)/shard_map/pallas_call | solution.py:514
  62.5 4.5 collective-permute-start.8
  67.0 7.7 %shard_map.214.y0_ref = f32[512,1536]{1,0:T(8,128)S(1)} custom-call(f32[512,1792]{1,0:T(8,128)} %get-tuple-element.327.q_ref.c_ref, f32[512,128]{1,0:T(8,128)S(1)} %get-tuple-element.328.dt_ref, f32[512,128]{1,0:T(8,128)S(1)} %get-tuple-element.329.cum_ref, f32[512,128]{1,0:T(8,128)S(1)} %get-tuple-element.331.col_ref, ...), custom_call_target="tpu_custom_call" | custom-call | flops 805306368 | bytes 10240000 | tf_op jit(solution)/shard_map/pallas_call | solution.py:549
  76.3 17.0 %collective-permute-done.9 = bf16[3072,384]{1,0:T(8,128)(2,1)} collective-permute-done((bf16[3072,384]{1,0:T(8,128)(2,1)}, bf16[3072,384]{1,0:T(8,128)(2,1)}, u32[]{:S(2)}, u32[]{:S(2)}) %collective-permute-start.9) | collective-permute-done | bytes 2359328 | tf_op jit(solution)/shard_map/ppermute | solution.py:792
  93.9 4.9 collective-permute-start.10
  101.4 4.1 broadcast_select_fusion.5
  106.0 3.0 fusion.34.z_ref
  111.2 7.5 %shard_map.215 = (f32[512,1536]{1,0:T(8,128)}, bf16[512,1536]{1,0:T(8,128)(2,1)S(1)}, bf16[512,768]{1,0:T(8,128)(2,1)S(1)}) custom-call(f32[512,1536]{1,0:T(8,128)} %copy-done.3, f32[512,1536]{1,0:T(8,128)} %fusion.34.z_ref, f32[512,1792]{1,0:T(8,128)} %get-tuple-element.327.q_ref.c_ref, f32[512,128]{1,0:T(8,128)S(1)} %get-tuple-element.330.all_ref, ...), custom_call_target="tpu_custom_call" | custom-call | tf_op jit(solution)/shard_map/pallas_call | solution.py:578
  124.2 8.8 %shard_map.216 = (f32[512,1792]{1,0:T(8,128)}, bf16[512,1792]{1,0:T(8,128)(2,1)S(1)}, f32[512,128]{1,0:T(8,128)S(1)}, f32[512,128]{1,0:T(8,128)S(1)}, f32[512,12...) custom-call(s32[1]{0:T(128)} %bitcast.section_ref, ...), custom_call_target="tpu_custom_call" | custom-call | tf_op jit(solution)/shard_map/pallas_call | solution.py:514
  133.0 9.1 %collective-permute-start.15 = (f32[136,768]{1,0:T(8,128)S(1)}, f32[136,768]{1,0:T(8,128)S(1)}, u32[]{:S(2)}, u32[]{:S(2)}) collective-permute-start(f32[136,768]{1,0:T(8,128)S(1)} %get-tuple-element.240.given_ref), channel_id=1, source_target_pairs={{0,16},{16,0},{1,17},{17,1},{2,18},{18,2},{3,19},{19,3},{4,20},{20... | collective-permute-start | bytes 1253384 | tf_op jit(solution)/shard_map/ppermute | solution.py:752
  144.8 5.3 collective-permute-start.16
  152.9 7.7 %shard_map.217.y0_ref = f32[512,1536]{1,0:T(8,128)S(1)} custom-call(f32[512,1792]{1,0:T(8,128)} %get-tuple-element.268.q_ref.c_ref, f32[512,128]{1,0:T(8,128)S(1)} %copy-done.34, f32[512,128]{1,0:T(8,128)S(1)} %copy-done.53, f32[512,128]{1,0:T(8,128)S(1)} %get-tuple-element.331.col_ref, f32[8,512]{1,0:T(8,128)S(1)} %get-tuple-element.332.lab_ref, ...), custom_call_target="tpu_custom_call" | custom-call | flops 805306368 | bytes 10240000 | tf_op jit(solution)/shard_map/pallas_call | solution.py:549
  162.8 4.7 collective-permute-start.17
  170.0 3.0 fusion.32.z_ref
  173.0 3.3 collective-permute-done.17
  180.1 7.6 %shard_map.218 = (f32[512,1536]{1,0:T(8,128)}, bf16[512,1536]{1,0:T(8,128)(2,1)S(1)}, bf16[512,768]{1,0:T(8,128)(2,1)S(1)}) custom-call(f32[512,1536]{1,0:T(8,128)} %copy-done.4, f32[512,1536]{1,0:T(8,128)} %fusion.32.z_ref, f32[512,1792]{1,0:T(8,128)} %get-tuple-element.268.q_ref.c_ref, f32[512,128]{1,0:T(8,128)S(1)} %copy-done.28, ...), custom_call_target="tpu_custom_call" | custom-call | tf_op jit(solution)/shard_map/pallas_call | solution.py:578
  188.6 9.2 %shard_map.219 = (bf16[512,1536]{1,0:T(8,128)(2,1)S(1)}, bf16[512,1536]{1,0:T(8,128)(2,1)}, f32[1,1536]{1,0:T(1,128)S(1)}, bf16[144,768]{1,0:T(8,128)(2,1)S(1)}, bf16[144,768]{1,0:T(8,128)(2,1)S(1)}) custom-call(s32[1]{0:T(128)} %bitcast.section_ref, bf16[512,768]{1,0:T(8,128)(2,1)S(1)} %copy-done.7, bf16[1536,768]{1,0:T(8,128)(2,1)} %maximum_maximum_fusion.1.w_ref, ...), custom_call_target="tpu_custom_call" | custom-call | tf_op jit(solution)/shard_map/pallas_call | solution.py:614
  213.3 15.0 %shard_map.220 = (f32[512,1536]{1,0:T(8,128)}, f32[512,256]{1,0:T(8,128)S(1)}, f32[512,256]{1,0:T(8,128)S(1)}) custom-call(f32[512,1792]{1,0:T(8,128)} %get-tuple-element.268.q_ref.c_ref, f32[512,128]{1,0:T(8,128)S(1)} %copy-done.35, f32[512,128]{1,0:T(8,128)S(1)} %copy-done.54, f32[512,128]{1,0:T(8,128)S(1)} %copy-done.29, ...), custom_call_target="tpu_custom_call" | custom-call | flops 3019898880 | bytes 15360000 | tf_op jit(solution)/shard_map/pallas_call | solution.py:645
  235.8 2.5 fusion.31
  238.3 13.5 %collective-permute-done.22 = bf16[144,768]{1,0:T(8,128)(2,1)S(1)} collective-permute-done((bf16[144,768]{1,0:T(8,128)(2,1)S(1)}, bf16[144,768]{1,0:T(8,128)(2,1)S(1)}, u32[]{:S(2)}, u32[]{:S(2)}) %collective-permute-start.22) | collective-permute-done | bytes 221216 | tf_op jit(solution)/shard_map/ppermute | solution.py:769
  267.0 15.1 %shard_map.221 = (bf16[512,1792]{1,0:T(8,128)(2,1)}, bf16[512,128]{1,0:T(8,128)(2,1)S(1)}, f32[8,1792]{1,0:T(8,128)S(1)}, f32[8,1792]{1,0:T(8,128)}, f32[8,1792]{1,0:T(8,128)S(1)}, /*index=5*/f32[8,128]{1,0:T(8,128)S(1)}) custom-call(bf16[128,1536]{1,0:T(8,128)(2,1)S(1)} %pad_maximum_fusion.27.outg_ref, f32[128,1536]{1,0:T(8,128)S(1)} %copy-done.2, ...), custom_call_target="tpu_custom_call" | custom-call | tf_op jit(solution)/shard_map/pallas_call | solution.py:693
  282.9 2.6 fusion.5
  295.1 2.6 broadcast_select_fusion.20
  310.2 8.7 %shard_map.222 = (bf16[512,1536]{1,0:T(8,128)(2,1)S(1)}, bf16[512,1536]{1,0:T(8,128)(2,1)}, f32[1,1536]{1,0:T(1,128)S(1)}, bf16[144,768]{1,0:T(8,128)(2,1)S(1)}, bf16[144,768]{1,0:T(8,128)(2,1)S(1)}) custom-call(s32[1]{0:T(128)} %bitcast.section_ref, bf16[512,768]{1,0:T(8,128)(2,1)S(1)} %fusion.27.g_ref, bf16[1536,768]{1,0:T(8,128)(2,1)} %maximum_maximum_fusion.w_ref, ...), custom_call_target="tpu_custom_call" | custom-call | tf_op jit(solution)/shard_map/pallas_call | solution.py:614
  340.1 14.9 %shard_map.223 = (f32[512,1536]{1,0:T(8,128)}, f32[512,256]{1,0:T(8,128)S(1)}, f32[512,256]{1,0:T(8,128)S(1)}) custom-call(f32[512,1792]{1,0:T(8,128)} %get-tuple-element.327.q_ref.c_ref, f32[512,128]{1,0:T(8,128)S(1)} %copy-done.32, f32[512,128]{1,0:T(8,128)S(1)} %copy-done.51, f32[512,128]{1,0:T(8,128)S(1)} %copy-done.26, ...), custom_call_target="tpu_custom_call" | custom-call | flops 3019898880 | bytes 15360000 | tf_op jit(solution)/shard_map/pallas_call | solution.py:645
  368.0 5.3 collective-permute-done.35
  378.2 15.1 %shard_map.224 = (bf16[512,1792]{1,0:T(8,128)(2,1)}, bf16[512,128]{1,0:T(8,128)(2,1)S(1)}, f32[8,1792]{1,0:T(8,128)S(1)}, f32[8,1792]{1,0:T(8,128)S(1)}, f32[8,1792]{1,0:T(8,128)S(1)}, /*index=5*/f32[8,128]{1,0:T(8,128)S(1)}) custom-call(bf16[128,1536]{1,0:T(8,128)(2,1)S(1)} %pad_maximum_fusion.28.outg_ref, f32[128,1536]{1,0:T(8,128)S(1)} %pad_maximum_fusion.17.inc_ref, ...), custom_call_target="tpu_custom_call" | custom-call | tf_op jit(solution)/shard_map/pallas_call | solution.py:693
  395.1 2.5 collective-permute-start.40
  402.3 7.0 %collective-permute-done.40 = bf16[608,384]{1,0:T(8,128)(2,1)S(1)} collective-permute-done((bf16[608,384]{1,0:T(8,128)(2,1)S(1)}, bf16[608,384]{1,0:T(8,128)(2,1)S(1)}, u32[]{:S(2)}, u32[]{:S(2)}) %collective-permute-start.40) | collective-permute-done | bytes 466976 | tf_op jit(solution)/shard_map/ppermute | solution.py:832
  422.9 2.9 collective-permute-start.52
  425.8 7.0 %collective-permute-done.45 = bf16[304,384]{1,0:T(8,128)(2,1)S(1)} collective-permute-done((bf16[304,384]{1,0:T(8,128)(2,1)S(1)}, bf16[304,384]{1,0:T(8,128)(2,1)S(1)}, u32[]{:S(2)}, u32[]{:S(2)}) %collective-permute-start.45) | collective-permute-done | bytes 233504 | tf_op jit(solution)/shard_map/ppermute | solution.py:832
  434.0 5.1 collective-permute-done.44
  444.0 7.7 %collective-permute-done.50 = f32[22,1792]{1,0:T(8,128)S(1)} collective-permute-done((f32[22,1792]{1,0:T(8,128)S(1)}, f32[22,1792]{1,0:T(8,128)S(1)}, u32[]{:S(2)}, u32[]{:S(2)}) %collective-permute-start.50) | collective-permute-done | bytes 157728 | tf_op jit(solution)/shard_map/ppermute | solution.py:862
  454.0 9.3 %collective-permute-done.48 = bf16[384,384]{1,0:T(8,128)(2,1)S(1)} collective-permute-done((bf16[384,384]{1,0:T(8,128)(2,1)S(1)}, bf16[384,384]{1,0:T(8,128)(2,1)S(1)}, u32[]{:S(2)}, u32[]{:S(2)}) %collective-permute-start.48) | collective-permute-done | bytes 294944 | tf_op jit(solution)/shard_map/ppermute | solution.py:832
  463.8 8.1 %collective-permute-done.49 = bf16[192,384]{1,0:T(8,128)(2,1)S(1)} collective-permute-done((bf16[192,384]{1,0:T(8,128)(2,1)S(1)}, bf16[192,384]{1,0:T(8,128)(2,1)S(1)}, u32[]{:S(2)}, u32[]{:S(2)}) %collective-permute-start.49) | collective-permute-done | bytes 147488 | tf_op jit(solution)/shard_map/ppermute | solution.py:832
  471.9 4.3 collective-permute-done.47
  486.4 4.5 collective-permute-done.57
  491.3 3.4 collective-permute-start.60
  494.8 4.9 collective-permute-done.60
  499.8 3.9 collective-permute-done.62
  509.6 3.1 collective-permute-done.65
  513.5 9.0 %collective-permute-done.63 = bf16[768,384]{1,0:T(8,128)(2,1)} collective-permute-done((bf16[768,384]{1,0:T(8,128)(2,1)}, bf16[768,384]{1,0:T(8,128)(2,1)}, u32[]{:S(2)}, u32[]{:S(2)}) %collective-permute-start.63) | collective-permute-done | bytes 589856 | tf_op jit(solution)/shard_map/ppermute | solution.py:838
  530.8 3.7 shard_map.225
  (695 shorter events, 209.3 us)
Async XLA Ops:
  2.3 33.8 %collective-permute-start = (bf16[1824,384]{1,0:T(8,128)(2,1)S(1)}, bf16[1824,384]{1,0:T(8,128)(2,1)}, u32[]{:S(2)}, u32[]{:S(2)}) collective-permute-start(bf16[1824,384]{1,0:T(8,128)(2,1)S(1)} %pad.60), channel_id=1, source_target_pairs={{0,1},{1,0},{2,3},{3,2},{4,5},{5,4},{6,7},{7,6},{8,9},{9,8},{10,11... | collective-permute-start | bytes 4202504 | tf_op jit(solution)/shard_map/ppermute | solution.py:792
  7.5 13.2 %collective-permute-start.1 = (bf16[512,768]{1,0:T(8,128)(2,1)}, bf16[512,768]{1,0:T(8,128)(2,1)}, u32[]{:S(2)}, u32[]{:S(2)}) collective-permute-start(bf16[512,768]{1,0:T(8,128)(2,1)} %dynamic-slice_bitcast_fusion.3), channel_id=1, source_target_pairs={{0,2},{18,16},{4,6},{22,20},{8,10},{26,24},{12,14},{30,28},{1,3},{... | collective-permute-start | bytes 2359304 | tf_op jit(solution)/shard_map/ppermute | solution.py:951
  12.7 16.4 %collective-permute-start.2 = (bf16[512,768]{1,0:T(8,128)(2,1)}, bf16[512,768]{1,0:T(8,128)(2,1)}, u32[]{:S(2)}, u32[]{:S(2)}) collective-permute-start(bf16[512,768]{1,0:T(8,128)(2,1)} %dynamic-slice_bitcast_fusion.2), channel_id=1, source_target_pairs={{0,2},{18,16},{4,6},{22,20},{8,10},{26,24},{12,14},{30,28},{1,3},{... | collective-permute-start | bytes 2359304 | tf_op jit(solution)/shard_map/ppermute | solution.py:951
  15.8 23.0 %collective-permute-start.3 = (f32[16,1792]{1,0:T(8,128)}, f32[16,1792]{1,0:T(8,128)}, u32[]{:S(2)}, u32[]{:S(2)}) collective-permute-start(f32[16,1792]{1,0:T(8,128)} %pad.66), channel_id=1, source_target_pairs={{0,16},{16,0},{1,17},{17,1},{2,18},{18,2},{3,19},{19,3},{4,20},{20... | collective-permute-start | bytes 344072 | tf_op jit(solution)/shard_map/ppermute | solution.py:986
  39.7 53.6 %collective-permute-start.9 = (bf16[3072,384]{1,0:T(8,128)(2,1)}, bf16[3072,384]{1,0:T(8,128)(2,1)}, u32[]{:S(2)}, u32[]{:S(2)}) collective-permute-start(bf16[3072,384]{1,0:T(8,128)(2,1)} %pad_maximum_fusion.2), channel_id=1, source_target_pairs={{0,1},{1,0},{2,3},{3,2},{4,5},{5,4},{6,7},{7,6},{8,9},{9,8},{10,11... | collective-permute-start | bytes 7077896 | tf_op jit(solution)/shard_map/ppermute | solution.py:792
  62.5 13.7 %collective-permute-start.8 = (f32[136,768]{1,0:T(8,128)S(1)}, f32[136,768]{1,0:T(8,128)S(1)}, u32[]{:S(2)}, u32[]{:S(2)}) collective-permute-start(f32[136,768]{1,0:T(8,128)S(1)} %pad_maximum_fusion.23), channel_id=1, source_target_pairs={{0,4},{2,6},{4,8},{6,10},{8,12},{10,14},{1,5},{3,7},{5,9},{7,11},{... | collective-permute-start | bytes 1253384 | tf_op jit(solution)/shard_map/ppermute | solution.py:769
  93.9 15.1 %collective-permute-start.10 = (f32[136,768]{1,0:T(8,128)S(1)}, f32[136,768]{1,0:T(8,128)S(1)}, u32[]{:S(2)}, u32[]{:S(2)}) collective-permute-start(f32[136,768]{1,0:T(8,128)S(1)} %pad_maximum_fusion.24), channel_id=1, source_target_pairs={{0,8},{2,10},{4,12},{6,14},{1,9},{3,11},{5,13},{7,15},{16,24},{18,... | collective-permute-start | bytes 1253384 | tf_op jit(solution)/shard_map/ppermute | solution.py:769
  133.0 10.5 %collective-permute-start.15 = (f32[136,768]{1,0:T(8,128)S(1)}, f32[136,768]{1,0:T(8,128)S(1)}, u32[]{:S(2)}, u32[]{:S(2)}) collective-permute-start(f32[136,768]{1,0:T(8,128)S(1)} %get-tuple-element.240.given_ref), channel_id=1, source_target_pairs={{0,16},{16,0},{1,17},{17,1},{2,18},{18,2},{3,19},{19,3},{4,20},{20... | collective-permute-start | bytes 1253384 | tf_op jit(solution)/shard_map/ppermute | solution.py:752
  144.8 15.8 %collective-permute-start.16 = (f32[136,768]{1,0:T(8,128)}, f32[136,768]{1,0:T(8,128)}, u32[]{:S(2)}, u32[]{:S(2)}) collective-permute-start(f32[136,768]{1,0:T(8,128)} %pad_maximum_fusion.25), channel_id=1, source_target_pairs={{0,4},{2,6},{4,8},{6,10},{8,12},{10,14},{1,5},{3,7},{5,9},{7,11},{... | collective-permute-start | bytes 1253384 | tf_op jit(solution)/shard_map/ppermute | solution.py:769
  162.8 13.4 %collective-permute-start.17 = (f32[136,768]{1,0:T(8,128)S(1)}, f32[136,768]{1,0:T(8,128)S(1)}, u32[]{:S(2)}, u32[]{:S(2)}) collective-permute-start(f32[136,768]{1,0:T(8,128)S(1)} %pad_maximum_fusion.26), channel_id=1, source_target_pairs={{0,8},{2,10},{4,12},{6,14},{1,9},{3,11},{5,13},{7,15},{16,24},{18,... | collective-permute-start | bytes 1253384 | tf_op jit(solution)/shard_map/ppermute | solution.py:769
  205.2 23.1 %collective-permute-start.21 = (bf16[2,1536,384]{2,1,0:T(8,128)(2,1)}, bf16[2,1536,384]{2,1,0:T(8,128)(2,1)}, u32[]{:S(2)}, u32[]{:S(2)}) collective-permute-start(bf16[2,1536,384]{2,1,0:T(8,128)(2,1)} %pad_maximum_fusion.5), channel_id=1, source_target_pairs={{0,16},{16,0},{1,17},{17,1},{2,18},{18,2},{3,19},{19,3},{4,20},{20... | collective-permute-start | bytes 7077896 | tf_op jit(solution)/shard_map/ppermute | solution.py:1101
  205.7 22.6 %collective-permute-start.20 = (bf16[144,768]{1,0:T(8,128)(2,1)}, bf16[144,768]{1,0:T(8,128)(2,1)S(1)}, u32[]{:S(2)}, u32[]{:S(2)}) collective-permute-start(bf16[144,768]{1,0:T(8,128)(2,1)} %pad_maximum_fusion.31), channel_id=1, source_target_pairs={{4,0},{6,2},{8,4},{10,6},{12,8},{14,10},{5,1},{7,3},{9,5},{11,7},{... | collective-permute-start | bytes 663560 | tf_op jit(solution)/shard_map/ppermute | solution.py:769
  228.7 23.2 %collective-permute-start.22 = (bf16[144,768]{1,0:T(8,128)(2,1)S(1)}, bf16[144,768]{1,0:T(8,128)(2,1)S(1)}, u32[]{:S(2)}, u32[]{:S(2)}) collective-permute-start(bf16[144,768]{1,0:T(8,128)(2,1)S(1)} %pad_maximum_fusion.32), channel_id=1, source_target_pairs={{8,0},{10,2},{12,4},{14,6},{9,1},{11,3},{13,5},{15,7},{24,16},{26,... | collective-permute-start | bytes 663560 | tf_op jit(solution)/shard_map/ppermute | solution.py:769
  255.6 27.3 %collective-permute-start.24 = (bf16[1536,384]{1,0:T(8,128)(2,1)}, bf16[1536,384]{1,0:T(8,128)(2,1)}, u32[]{:S(2)}, u32[]{:S(2)}) collective-permute-start(bf16[1536,384]{1,0:T(8,128)(2,1)} %dynamic-slice_bitcast_fusion.1), channel_id=1, source_target_pairs={{0,1},{1,0},{2,3},{3,2},{4,5},{5,4},{6,7},{7,6},{8,9},{9,8},{10,11... | collective-permute-start | bytes 3538952 | tf_op jit(solution)/shard_map/ppermute | solution.py:822
  294.1 8.3 %collective-permute-start.26 = (bf16[2,896,384]{2,1,0:T(8,128)(2,1)}, bf16[2,896,384]{2,1,0:T(8,128)(2,1)}, u32[]{:S(2)}, u32[]{:S(2)}) collective-permute-start(bf16[2,896,384]{2,1,0:T(8,128)(2,1)} %pad_maximum_fusion.11), channel_id=1, source_target_pairs={{0,16},{16,0},{1,17},{17,1},{2,18},{18,2},{3,19},{19,3},{4,20},{20... | collective-permute-start | bytes 4128776 | tf_op jit(solution)/shard_map/ppermute | solution.py:1135
  297.6 28.6 %collective-permute-start.28 = (bf16[512,768]{1,0:T(8,128)(2,1)}, bf16[512,768]{1,0:T(8,128)(2,1)S(1)}, u32[]{:S(2)}, u32[]{:S(2)}) collective-permute-start(bf16[512,768]{1,0:T(8,128)(2,1)} %get-tuple-element.489), channel_id=1, source_target_pairs={{0,0},{2,16},{16,2},{18,18},{4,4},{6,20},{20,6},{22,22},{8,8},{10,... | collective-permute-start | bytes 2359304 | tf_op jit(solution)/shard_map/ppermute | solution.py:1009
  299.6 26.7 %collective-permute-start.29 = (bf16[512,768]{1,0:T(8,128)(2,1)}, bf16[512,768]{1,0:T(8,128)(2,1)S(1)}, u32[]{:S(2)}, u32[]{:S(2)}) collective-permute-start(bf16[512,768]{1,0:T(8,128)(2,1)} %get-tuple-element.488), channel_id=1, source_target_pairs={{0,16},{2,0},{16,18},{18,2},{4,20},{6,4},{20,22},{22,6},{8,24},{10... | collective-permute-start | bytes 2359304 | tf_op jit(solution)/shard_map/ppermute | solution.py:1010
  307.7 17.4 %collective-permute-start.27 = (bf16[896,384]{1,0:T(8,128)(2,1)S(1)}, bf16[896,384]{1,0:T(8,128)(2,1)S(1)}, u32[]{:S(2)}, u32[]{:S(2)}) collective-permute-start(bf16[896,384]{1,0:T(8,128)(2,1)S(1)} %dynamic-slice_bitcast_fusion.5), channel_id=1, source_target_pairs={{0,1},{1,0},{2,3},{3,2},{4,5},{5,4},{6,7},{7,6},{8,9},{9,8},{10,11... | collective-permute-start | bytes 2064392 | tf_op jit(solution)/shard_map/ppermute | solution.py:822
  329.9 28.8 %collective-permute-start.34 = (bf16[2,1536,384]{2,1,0:T(8,128)(2,1)}, bf16[2,1536,384]{2,1,0:T(8,128)(2,1)}, u32[]{:S(2)}, u32[]{:S(2)}) collective-permute-start(bf16[2,1536,384]{2,1,0:T(8,128)(2,1)} %pad_maximum_fusion.6), channel_id=1, source_target_pairs={{0,16},{16,0},{1,17},{17,1},{2,18},{18,2},{3,19},{19,3},{4,20},{20... | collective-permute-start | bytes 7077896 | tf_op jit(solution)/shard_map/ppermute | solution.py:1101
  333.9 23.7 %collective-permute-start.32 = (bf16[768,384]{1,0:T(8,128)(2,1)S(1)}, bf16[768,384]{1,0:T(8,128)(2,1)S(1)}, u32[]{:S(2)}, u32[]{:S(2)}) collective-permute-start(bf16[768,384]{1,0:T(8,128)(2,1)S(1)} %dynamic-slice_bitcast_fusion.7), channel_id=1, source_target_pairs={{0,2},{2,0},{4,6},{6,4},{8,10},{10,8},{12,14},{14,12},{1,3},{3,1},... | collective-permute-start | bytes 1769480 | tf_op jit(solution)/shard_map/ppermute | solution.py:832
  335.6 21.2 %collective-permute-start.33 = (bf16[448,384]{1,0:T(8,128)(2,1)S(1)}, bf16[448,384]{1,0:T(8,128)(2,1)S(1)}, u32[]{:S(2)}, u32[]{:S(2)}) collective-permute-start(bf16[448,384]{1,0:T(8,128)(2,1)S(1)} %dynamic-slice_bitcast_fusion.10), channel_id=1, source_target_pairs={{0,2},{2,0},{4,6},{6,4},{8,10},{10,8},{12,14},{14,12},{1,3},{3,1},... | collective-permute-start | bytes 1032200 | tf_op jit(solution)/shard_map/ppermute | solution.py:832
  338.4 20.2 %collective-permute-start.31 = (bf16[144,768]{1,0:T(8,128)(2,1)S(1)}, bf16[144,768]{1,0:T(8,128)(2,1)S(1)}, u32[]{:S(2)}, u32[]{:S(2)}) collective-permute-start(bf16[144,768]{1,0:T(8,128)(2,1)S(1)} %copy-done.147), channel_id=1, source_target_pairs={{4,0},{6,2},{8,4},{10,6},{12,8},{14,10},{5,1},{7,3},{9,5},{11,7},{... | collective-permute-start | bytes 663560 | tf_op jit(solution)/shard_map/ppermute | solution.py:769
  358.9 14.4 %collective-permute-start.35 = (bf16[144,768]{1,0:T(8,128)(2,1)S(1)}, bf16[144,768]{1,0:T(8,128)(2,1)S(1)}, u32[]{:S(2)}, u32[]{:S(2)}) collective-permute-start(bf16[144,768]{1,0:T(8,128)(2,1)S(1)} %pad_maximum_fusion.34), channel_id=1, source_target_pairs={{8,0},{10,2},{12,4},{14,6},{9,1},{11,3},{13,5},{15,7},{24,16},{26,... | collective-permute-start | bytes 663560 | tf_op jit(solution)/shard_map/ppermute | solution.py:769
  376.8 32.6 %collective-permute-start.39 = (bf16[1536,384]{1,0:T(8,128)(2,1)}, bf16[1536,384]{1,0:T(8,128)(2,1)}, u32[]{:S(2)}, u32[]{:S(2)}) collective-permute-start(bf16[1536,384]{1,0:T(8,128)(2,1)} %dynamic-slice_bitcast_fusion), channel_id=1, source_target_pairs={{0,1},{1,0},{2,3},{3,2},{4,5},{5,4},{6,7},{7,6},{8,9},{9,8},{10,11... | collective-permute-start | bytes 3538952 | tf_op jit(solution)/shard_map/ppermute | solution.py:822
  395.1 14.2 %collective-permute-start.40 = (bf16[608,384]{1,0:T(8,128)(2,1)S(1)}, bf16[608,384]{1,0:T(8,128)(2,1)S(1)}, u32[]{:S(2)}, u32[]{:S(2)}) collective-permute-start(bf16[608,384]{1,0:T(8,128)(2,1)S(1)} %dynamic-slice_bitcast_fusion.8), channel_id=1, source_target_pairs={{0,4},{2,6},{4,0},{6,2},{8,12},{10,14},{12,8},{14,10},{1,5},{3,7},... | collective-permute-start | bytes 1400840 | tf_op jit(solution)/shard_map/ppermute | solution.py:832
  398.9 12.1 %collective-permute-start.38 = (bf16[2,896,384]{2,1,0:T(8,128)(2,1)S(1)}, bf16[2,896,384]{2,1,0:T(8,128)(2,1)S(1)}, u32[]{:S(2)}, u32[]{:S(2)}) collective-permute-start(bf16[2,896,384]{2,1,0:T(8,128)(2,1)S(1)} %pad_maximum_fusion.12), channel_id=1, source_target_pairs={{0,16},{16,0},{1,17},{17,1},{2,18},{18,2},{3,19},{19,3},{4,20},{20... | collective-permute-start | bytes 4128776 | tf_op jit(solution)/shard_map/ppermute | solution.py:1135
  412.4 28.1 %collective-permute-start.41 = (bf16[896,384]{1,0:T(8,128)(2,1)}, bf16[896,384]{1,0:T(8,128)(2,1)}, u32[]{:S(2)}, u32[]{:S(2)}) collective-permute-start(bf16[896,384]{1,0:T(8,128)(2,1)} %dynamic-slice_bitcast_fusion.4), channel_id=1, source_target_pairs={{0,1},{1,0},{2,3},{3,2},{4,5},{5,4},{6,7},{7,6},{8,9},{9,8},{10,11... | collective-permute-start | bytes 2064392 | tf_op jit(solution)/shard_map/ppermute | solution.py:822
  414.3 24.9 %collective-permute-start.42 = (bf16[768,384]{1,0:T(8,128)(2,1)}, bf16[768,384]{1,0:T(8,128)(2,1)}, u32[]{:S(2)}, u32[]{:S(2)}) collective-permute-start(bf16[768,384]{1,0:T(8,128)(2,1)} %dynamic-slice_bitcast_fusion.6), channel_id=1, source_target_pairs={{0,2},{2,0},{4,6},{6,4},{8,10},{10,8},{12,14},{14,12},{1,3},{3,1},... | collective-permute-start | bytes 1769480 | tf_op jit(solution)/shard_map/ppermute | solution.py:832
  419.6 13.2 %collective-permute-start.45 = (bf16[304,384]{1,0:T(8,128)(2,1)S(1)}, bf16[304,384]{1,0:T(8,128)(2,1)S(1)}, u32[]{:S(2)}, u32[]{:S(2)}) collective-permute-start(bf16[304,384]{1,0:T(8,128)(2,1)S(1)} %dynamic-slice_bitcast_fusion.12), channel_id=1, source_target_pairs={{0,8},{2,10},{4,12},{6,14},{8,0},{10,2},{12,4},{14,6},{1,9},{3,11}... | collective-permute-start | bytes 700424 | tf_op jit(solution)/shard_map/ppermute | solution.py:832
  421.7 54.9 %collective-permute-start.51 = (bf16[512,768]{1,0:T(8,128)(2,1)S(1)}, bf16[512,768]{1,0:T(8,128)(2,1)S(1)}, u32[]{:S(2)}, u32[]{:S(2)}) collective-permute-start(bf16[512,768]{1,0:T(8,128)(2,1)S(1)} %get-tuple-element.465), channel_id=1, source_target_pairs={{0,0},{2,16},{16,2},{18,18},{4,4},{6,20},{20,6},{22,22},{8,8},{10,... | collective-permute-start | bytes 2359304 | tf_op jit(solution)/shard_map/ppermute | solution.py:1009
  422.9 53.7 %collective-permute-start.52 = (bf16[512,768]{1,0:T(8,128)(2,1)S(1)}, bf16[512,768]{1,0:T(8,128)(2,1)S(1)}, u32[]{:S(2)}, u32[]{:S(2)}) collective-permute-start(bf16[512,768]{1,0:T(8,128)(2,1)S(1)} %get-tuple-element.464), channel_id=1, source_target_pairs={{0,16},{2,0},{16,18},{18,2},{4,20},{6,4},{20,22},{22,6},{8,24},{10... | collective-permute-start | bytes 2359304 | tf_op jit(solution)/shard_map/ppermute | solution.py:1010
  441.7 10.0 %collective-permute-start.50 = (f32[22,1792]{1,0:T(8,128)S(1)}, f32[22,1792]{1,0:T(8,128)S(1)}, u32[]{:S(2)}, u32[]{:S(2)}) collective-permute-start(f32[22,1792]{1,0:T(8,128)S(1)} %add.434), channel_id=1, source_target_pairs={{0,2},{2,0},{4,6},{6,4},{8,10},{10,8},{12,14},{14,12},{1,3},{3,1},... | collective-permute-start | bytes 473096 | tf_op jit(solution)/shard_map/ppermute | solution.py:862
  443.3 9.8 %collective-permute-start.53 = (bf16[304,384]{1,0:T(8,128)(2,1)S(1)}, bf16[304,384]{1,0:T(8,128)(2,1)S(1)}, u32[]{:S(2)}, u32[]{:S(2)}) collective-permute-start(bf16[304,384]{1,0:T(8,128)(2,1)S(1)} %fusion.55), channel_id=1, source_target_pairs={{0,8},{2,10},{4,12},{6,14},{8,0},{10,2},{12,4},{14,6},{1,9},{3,11}... | collective-permute-start | bytes 700424 | tf_op jit(solution)/shard_map/ppermute | solution.py:838
  443.4 20.2 %collective-permute-start.46 = (bf16[448,384]{1,0:T(8,128)(2,1)S(1)}, bf16[448,384]{1,0:T(8,128)(2,1)S(1)}, u32[]{:S(2)}, u32[]{:S(2)}) collective-permute-start(bf16[448,384]{1,0:T(8,128)(2,1)S(1)} %dynamic-slice_bitcast_fusion.9), channel_id=1, source_target_pairs={{0,2},{2,0},{4,6},{6,4},{8,10},{10,8},{12,14},{14,12},{1,3},{3,1},... | collective-permute-start | bytes 1032200 | tf_op jit(solution)/shard_map/ppermute | solution.py:832
  451.7 11.5 %collective-permute-start.48 = (bf16[384,384]{1,0:T(8,128)(2,1)S(1)}, bf16[384,384]{1,0:T(8,128)(2,1)S(1)}, u32[]{:S(2)}, u32[]{:S(2)}) collective-permute-start(bf16[384,384]{1,0:T(8,128)(2,1)S(1)} %dynamic-slice_bitcast_fusion.11), channel_id=1, source_target_pairs={{0,4},{2,6},{4,0},{6,2},{8,12},{10,14},{12,8},{14,10},{1,5},{3,7},... | collective-permute-start | bytes 884744 | tf_op jit(solution)/shard_map/ppermute | solution.py:832
  453.3 23.0 %collective-permute-start.54 = (bf16[608,384]{1,0:T(8,128)(2,1)S(1)}, bf16[608,384]{1,0:T(8,128)(2,1)S(1)}, u32[]{:S(2)}, u32[]{:S(2)}) collective-permute-start(bf16[608,384]{1,0:T(8,128)(2,1)S(1)} %pad_maximum_fusion.22), channel_id=1, source_target_pairs={{0,4},{2,6},{4,0},{6,2},{8,12},{10,14},{12,8},{14,10},{1,5},{3,7},... | collective-permute-start | bytes 1400840 | tf_op jit(solution)/shard_map/ppermute | solution.py:838
  463.4 8.5 %collective-permute-start.49 = (bf16[192,384]{1,0:T(8,128)(2,1)S(1)}, bf16[192,384]{1,0:T(8,128)(2,1)S(1)}, u32[]{:S(2)}, u32[]{:S(2)}) collective-permute-start(bf16[192,384]{1,0:T(8,128)(2,1)S(1)} %dynamic-slice_bitcast_fusion.14), channel_id=1, source_target_pairs={{0,8},{2,10},{4,12},{6,14},{8,0},{10,2},{12,4},{14,6},{1,9},{3,11}... | collective-permute-start | bytes 442376 | tf_op jit(solution)/shard_map/ppermute | solution.py:832
  463.7 12.5 %collective-permute-start.47 = (bf16[224,384]{1,0:T(8,128)(2,1)S(1)}, bf16[224,384]{1,0:T(8,128)(2,1)S(1)}, u32[]{:S(2)}, u32[]{:S(2)}) collective-permute-start(bf16[224,384]{1,0:T(8,128)(2,1)S(1)} %dynamic-slice_bitcast_fusion.13), channel_id=1, source_target_pairs={{0,4},{2,6},{4,0},{6,2},{8,12},{10,14},{12,8},{14,10},{1,5},{3,7},... | collective-permute-start | bytes 516104 | tf_op jit(solution)/shard_map/ppermute | solution.py:832
  476.7 8.7 %collective-permute-start.55 = (bf16[112,384]{1,0:T(8,128)(2,1)S(1)}, bf16[112,384]{1,0:T(8,128)(2,1)S(1)}, u32[]{:S(2)}, u32[]{:S(2)}) collective-permute-start(bf16[112,384]{1,0:T(8,128)(2,1)S(1)} %dynamic-slice_bitcast_fusion.15), channel_id=1, source_target_pairs={{0,8},{2,10},{4,12},{6,14},{8,0},{10,2},{12,4},{14,6},{1,9},{3,11}... | collective-permute-start | bytes 258056 | tf_op jit(solution)/shard_map/ppermute | solution.py:832
  479.1 11.9 %collective-permute-start.57 = (bf16[192,384]{1,0:T(8,128)(2,1)S(1)}, bf16[192,384]{1,0:T(8,128)(2,1)S(1)}, u32[]{:S(2)}, u32[]{:S(2)}) collective-permute-start(bf16[192,384]{1,0:T(8,128)(2,1)S(1)} %fusion.71), channel_id=1, source_target_pairs={{0,8},{2,10},{4,12},{6,14},{8,0},{10,2},{12,4},{14,6},{1,9},{3,11}... | collective-permute-start | bytes 442376 | tf_op jit(solution)/shard_map/ppermute | solution.py:838
  481.1 10.2 %collective-permute-start.59 = (f32[22,1792]{1,0:T(8,128)S(1)}, f32[22,1792]{1,0:T(8,128)S(1)}, u32[]{:S(2)}, u32[]{:S(2)}) collective-permute-start(f32[22,1792]{1,0:T(8,128)S(1)} %add.443), channel_id=1, source_target_pairs={{0,4},{2,6},{4,0},{6,2},{8,12},{10,14},{12,8},{14,10},{1,5},{3,7},... | collective-permute-start | bytes 473096 | tf_op jit(solution)/shard_map/ppermute | solution.py:862
  482.3 23.3 %collective-permute-start.61 = (bf16[768,384]{1,0:T(8,128)(2,1)S(1)}, bf16[768,384]{1,0:T(8,128)(2,1)S(1)}, u32[]{:S(2)}, u32[]{:S(2)}) collective-permute-start(bf16[768,384]{1,0:T(8,128)(2,1)S(1)} %slice.368), channel_id=1, source_target_pairs={{0,2},{2,0},{4,6},{6,4},{8,10},{10,8},{12,14},{14,12},{1,3},{3,1},... | collective-permute-start | bytes 1769480 | tf_op jit(solution)/shard_map/ppermute | solution.py:838
  482.8 20.8 %collective-permute-start.62 = (bf16[448,384]{1,0:T(8,128)(2,1)S(1)}, bf16[448,384]{1,0:T(8,128)(2,1)S(1)}, u32[]{:S(2)}, u32[]{:S(2)}) collective-permute-start(bf16[448,384]{1,0:T(8,128)(2,1)S(1)} %slice.369), channel_id=1, source_target_pairs={{0,2},{2,0},{4,6},{6,4},{8,10},{10,8},{12,14},{14,12},{1,3},{3,1},... | collective-permute-start | bytes 1032200 | tf_op jit(solution)/shard_map/ppermute | solution.py:838
  485.4 9.4 %collective-permute-start.56 = (bf16[112,384]{1,0:T(8,128)(2,1)S(1)}, bf16[112,384]{1,0:T(8,128)(2,1)S(1)}, u32[]{:S(2)}, u32[]{:S(2)}) collective-permute-start(bf16[112,384]{1,0:T(8,128)(2,1)S(1)} %fusion.74), channel_id=1, source_target_pairs={{0,8},{2,10},{4,12},{6,14},{8,0},{10,2},{12,4},{14,6},{1,9},{3,11}... | collective-permute-start | bytes 258056 | tf_op jit(solution)/shard_map/ppermute | solution.py:838
  491.0 13.7 %collective-permute-start.58 = (bf16[384,384]{1,0:T(8,128)(2,1)S(1)}, bf16[384,384]{1,0:T(8,128)(2,1)S(1)}, u32[]{:S(2)}, u32[]{:S(2)}) collective-permute-start(bf16[384,384]{1,0:T(8,128)(2,1)S(1)} %pad_maximum_fusion.30), channel_id=1, source_target_pairs={{0,4},{2,6},{4,0},{6,2},{8,12},{10,14},{12,8},{14,10},{1,5},{3,7},... | collective-permute-start | bytes 884744 | tf_op jit(solution)/shard_map/ppermute | solution.py:838
  491.3 8.4 %collective-permute-start.60 = (f32[22,1792]{1,0:T(8,128)S(1)}, f32[22,1792]{1,0:T(8,128)S(1)}, u32[]{:S(2)}, u32[]{:S(2)}) collective-permute-start(f32[22,1792]{1,0:T(8,128)S(1)} %add.446), channel_id=1, source_target_pairs={{0,8},{2,10},{4,12},{6,14},{8,0},{10,2},{12,4},{14,6},{1,9},{3,11}... | collective-permute-start | bytes 473096 | tf_op jit(solution)/shard_map/ppermute | solution.py:862
  505.9 16.6 %collective-permute-start.63 = (bf16[768,384]{1,0:T(8,128)(2,1)}, bf16[768,384]{1,0:T(8,128)(2,1)}, u32[]{:S(2)}, u32[]{:S(2)}) collective-permute-start(bf16[768,384]{1,0:T(8,128)(2,1)} %pad_maximum_fusion.21), channel_id=1, source_target_pairs={{0,2},{2,0},{4,6},{6,4},{8,10},{10,8},{12,14},{14,12},{1,3},{3,1},... | collective-permute-start | bytes 1769480 | tf_op jit(solution)/shard_map/ppermute | solution.py:838
  512.7 14.2 %collective-permute-start.66 = (bf16[448,384]{1,0:T(8,128)(2,1)S(1)}, bf16[448,384]{1,0:T(8,128)(2,1)S(1)}, u32[]{:S(2)}, u32[]{:S(2)}) collective-permute-start(bf16[448,384]{1,0:T(8,128)(2,1)S(1)} %pad_maximum_fusion.29), channel_id=1, source_target_pairs={{0,2},{2,0},{4,6},{6,4},{8,10},{10,8},{12,14},{14,12},{1,3},{3,1},... | collective-permute-start | bytes 1032200 | tf_op jit(solution)/shard_map/ppermute | solution.py:838
  (198 other events, 1544.0 us)

commit v4 on v3

--- a/solution.py
+++ b/solution.py
@@ -479,9 +479,9 @@
             back_ref[:, lanes] = early
 
 
-def params(steps):
+def params(steps, limit=48):
     return pltpu.CompilerParams(
-        dimension_semantics=("arbitrary",) * steps, vmem_limit_bytes=48 * 1024 * 1024
+        dimension_semantics=("arbitrary",) * steps, vmem_limit_bytes=limit * 1024 * 1024
     )
 
 
@@ -592,7 +592,7 @@
         ],
         out_specs=(by_row(DI), by_row(DI), by_row(D)),
         out_shape=(shape(rows, DI), shape(rows, DI, dtype=bf16), shape(rows, D, dtype=bf16)),
-        compiler_params=params(1),
+        compiler_params=params(1, 32),
     )(y0, z, q, total, col, inc, par, w_out, hidden, spread)
 
 
@@ -631,7 +631,7 @@
         out_specs=(by_row(DI), by_row(DI), whole(outs[2]), whole(outs[3]), whole(outs[4])),
         out_shape=outs,
         scratch_shapes=[pltpu.VMEM((STATE, DI), f32)],
-        compiler_params=params(1),
+        compiler_params=params(1, 32),
     )(section, grad, w_out, y, z, par, q, total, col, kept, given, spread)
 
 

time: 545 us -> 535 us (0.982)
  Pallas kernels: 131 us -> 116 us
  waiting for transfers between devices: 146 us -> 155 us
  matrix products: 38.3 us -> 32.1 us
  local copies, waits for them, and re-layouts: 51.5 us -> 57.1 us
    pallas_call x2, Pallas kernels: 17.8 us -> 9.43 us  [gate_backward(): pl.pallas_call(gate_back_kernel, grid=(rows // size,), in_specs=[pl.Block...]
    pallas_call x2, Pallas kernels: 15.1 us -> 8.29 us  [gate_forward(): pl.pallas_call(gate_kernel, grid=(rows // size,), in_specs=[by_row(DI), b...]
    unnamed x356 -> x388, local copies, waits for them, and re-layouts: 28.7 us -> 35.4 us
  transfers between devices with their start and end apart: 68 -> 68, of which waited for: 34 -> 38; matrix products, arithmetic and copies ran while one was open for 19% -> 17% of each run, Pallas kernels for 18% -> 17%
where the time goes in v4:
time: 535 us; the launch traced here: 525 us
  waiting for transfers between devices  155 us (29%)
  Pallas kernels  116 us (22%)
  starting transfers between devices  98.8 us (18%)
  other arithmetic  62.3 us (12%)
  local copies, waits for them, and re-layouts  57.1 us (11%)
  matrix products  32.1 us (6%)
    ppermute x10, waiting for transfers between devices, halve(): got = lax.ppermute(given, 'seq', [(i, i ^ distance) for i in range(size)])  38.1 us
    unnamed x388, local copies, waits for them, and re-layouts  35.4 us
    pallas_call x2, Pallas kernels, conv_backward(): pl.pallas_call(conv_back_kernel, grid=(2 * count,), in_specs=[whole(outg)...  30.2 us
    pallas_call x2, Pallas kernels, intra_backward(): pl.pallas_call(intra_back_kernel, grid=(rows // Q,), in_specs=[by_row(CON...  29.8 us
    ppermute x8, starting transfers between devices, chain_scan(): arrived = lax.ppermute(sent, 'seq', route)  25.7 us
    ppermute x8, waiting for transfers between devices, chain_scan(): arrived = lax.ppermute(sent, 'seq', route)  25.6 us
    ppermute x10, waiting for transfers between devices, rejoin(): got = lax.ppermute(array, 'seq', [(i, i ^ distance) for i in range(size)])  24 us
    ppermute x2, waiting for transfers between devices, move_rows(): lax.ppermute(shard, 'fsdp', [(i, (i + shift) % parts) for i in range(part...  22.9 us
  transfers between devices with their start and end apart: 68, of which 38 were waited for; matrix products, arithmetic and copies ran while one was open for 17% of the time, Pallas kernels for 17%

profile of v4, /device:TPU:0, one launch (start us, length us, event | category | flops | bytes accessed | tf_op | source)
XLA Modules:
  0.0 525.2 jit_solution(6064630133078891963)
XLA Ops:
  2.3 3.0 collective-permute-start
  7.5 4.3 collective-permute-start.1
  22.0 7.2 %collective-permute-done.2 = bf16[512,768]{1,0:T(8,128)(2,1)} collective-permute-done((bf16[512,768]{1,0:T(8,128)(2,1)}, bf16[512,768]{1,0:T(8,128)(2,1)}, u32[]{:S(2)}, u32[]{:S(2)}) %collective-permute-start.2) | collective-permute-done | bytes 786464 | tf_op jit(solution)/shard_map/ppermute | solution.py:951
  30.1 6.0 %collective-permute-done = bf16[1824,384]{1,0:T(8,128)(2,1)} collective-permute-done((bf16[1824,384]{1,0:T(8,128)(2,1)S(1)}, bf16[1824,384]{1,0:T(8,128)(2,1)}, u32[]{:S(2)}, u32[]{:S(2)}) %collective-permute-start) | collective-permute-done | bytes 1400864 | tf_op jit(solution)/shard_map/ppermute | solution.py:792
  41.7 3.0 broadcast_select_fusion.12
  49.3 8.8 %shard_map.213 = (f32[512,1792]{1,0:T(8,128)}, bf16[512,1792]{1,0:T(8,128)(2,1)S(1)}, f32[512,128]{1,0:T(8,128)S(1)}, f32[512,128]{1,0:T(8,128)S(1)}, f32[512,12...) custom-call(s32[1]{0:T(128)} %bitcast.section_ref, ...), custom_call_target="tpu_custom_call" | custom-call | tf_op jit(solution)/shard_map/pallas_call | solution.py:514
  62.0 4.5 collective-permute-start.8
  66.5 7.7 %shard_map.214.y0_ref = f32[512,1536]{1,0:T(8,128)S(1)} custom-call(f32[512,1792]{1,0:T(8,128)} %get-tuple-element.327.q_ref.c_ref, f32[512,128]{1,0:T(8,128)S(1)} %get-tuple-element.328.dt_ref, f32[512,128]{1,0:T(8,128)S(1)} %get-tuple-element.329.cum_ref, f32[512,128]{1,0:T(8,128)S(1)} %get-tuple-element.331.col_ref, ...), custom_call_target="tpu_custom_call" | custom-call | flops 805306368 | bytes 10240000 | tf_op jit(solution)/shard_map/pallas_call | solution.py:549
  75.8 16.9 %collective-permute-done.9 = bf16[3072,384]{1,0:T(8,128)(2,1)} collective-permute-done((bf16[3072,384]{1,0:T(8,128)(2,1)}, bf16[3072,384]{1,0:T(8,128)(2,1)}, u32[]{:S(2)}, u32[]{:S(2)}) %collective-permute-start.9) | collective-permute-done | bytes 2359328 | tf_op jit(solution)/shard_map/ppermute | solution.py:792
  93.3 4.9 collective-permute-start.10
  100.8 4.2 broadcast_select_fusion.5
  110.9 4.1 shard_map.215
  122.0 8.8 %shard_map.216 = (f32[512,1792]{1,0:T(8,128)}, bf16[512,1792]{1,0:T(8,128)(2,1)S(1)}, f32[512,128]{1,0:T(8,128)S(1)}, f32[512,128]{1,0:T(8,128)S(1)}, f32[512,12...) custom-call(s32[1]{0:T(128)} %bitcast.section_ref, ...), custom_call_target="tpu_custom_call" | custom-call | tf_op jit(solution)/shard_map/pallas_call | solution.py:514
  130.9 10.3 %collective-permute-start.15 = (f32[136,768]{1,0:T(8,128)S(1)}, f32[136,768]{1,0:T(8,128)S(1)}, u32[]{:S(2)}, u32[]{:S(2)}) collective-permute-start(f32[136,768]{1,0:T(8,128)S(1)} %get-tuple-element.240.given_ref), channel_id=1, source_target_pairs={{0,16},{16,0},{1,17},{17,1},{2,18},{18,2},{3,19},{19,3},{4,20},{20... | collective-permute-start | bytes 1253384 | tf_op jit(solution)/shard_map/ppermute | solution.py:752
  143.8 5.3 %collective-permute-start.16 = (f32[136,768]{1,0:T(8,128)}, f32[136,768]{1,0:T(8,128)}, u32[]{:S(2)}, u32[]{:S(2)}) collective-permute-start(f32[136,768]{1,0:T(8,128)} %pad_maximum_fusion.25), channel_id=1, source_target_pairs={{0,4},{2,6},{4,8},{6,10},{8,12},{10,14},{1,5},{3,7},{5,9},{7,11},{... | collective-permute-start | bytes 1253384 | tf_op jit(solution)/shard_map/ppermute | solution.py:769
  151.9 7.7 %shard_map.217.y0_ref = f32[512,1536]{1,0:T(8,128)S(1)} custom-call(f32[512,1792]{1,0:T(8,128)} %get-tuple-element.268.q_ref.c_ref, f32[512,128]{1,0:T(8,128)S(1)} %copy-done.44, f32[512,128]{1,0:T(8,128)S(1)} %copy-done.63, f32[512,128]{1,0:T(8,128)S(1)} %get-tuple-element.331.col_ref, f32[8,512]{1,0:T(8,128)S(1)} %get-tuple-element.332.lab_ref, ...), custom_call_target="tpu_custom_call" | custom-call | flops 805306368 | bytes 10240000 | tf_op jit(solution)/shard_map/pallas_call | solution.py:549
  161.8 4.7 collective-permute-start.17
  170.4 4.9 collective-permute-done.17
  180.5 4.1 shard_map.218
  185.6 4.7 shard_map.219
  204.7 15.0 %shard_map.220 = (f32[512,1536]{1,0:T(8,128)}, f32[512,256]{1,0:T(8,128)S(1)}, f32[512,256]{1,0:T(8,128)S(1)}) custom-call(f32[512,1792]{1,0:T(8,128)} %get-tuple-element.268.q_ref.c_ref, f32[512,128]{1,0:T(8,128)S(1)} %copy-done.45, f32[512,128]{1,0:T(8,128)S(1)} %copy-done.64, f32[512,128]{1,0:T(8,128)S(1)} %copy-done.39, ...), custom_call_target="tpu_custom_call" | custom-call | flops 3019898880 | bytes 15360000 | tf_op jit(solution)/shard_map/pallas_call | solution.py:645
  227.2 2.5 fusion.31
  229.7 13.8 %collective-permute-done.22 = bf16[144,768]{1,0:T(8,128)(2,1)S(1)} collective-permute-done((bf16[144,768]{1,0:T(8,128)(2,1)S(1)}, bf16[144,768]{1,0:T(8,128)(2,1)S(1)}, u32[]{:S(2)}, u32[]{:S(2)}) %collective-permute-start.22) | collective-permute-done | bytes 221216 | tf_op jit(solution)/shard_map/ppermute | solution.py:769
  258.6 15.1 %shard_map.221 = (bf16[512,1792]{1,0:T(8,128)(2,1)}, bf16[512,128]{1,0:T(8,128)(2,1)S(1)}, f32[8,1792]{1,0:T(8,128)S(1)}, f32[8,1792]{1,0:T(8,128)}, f32[8,1792]{1,0:T(8,128)S(1)}, /*index=5*/f32[8,128]{1,0:T(8,128)S(1)}) custom-call(bf16[128,1536]{1,0:T(8,128)(2,1)S(1)} %pad_maximum_fusion.27.outg_ref, f32[128,1536]{1,0:T(8,128)S(1)} %copy-done.7, ...), custom_call_target="tpu_custom_call" | custom-call | tf_op jit(solution)/shard_map/pallas_call | solution.py:693
  274.9 2.6 fusion.5
  289.4 2.8 collective-permute-start.29
  302.5 4.8 shard_map.222
  311.4 4.6 collective-permute-done.27
  331.0 14.9 %shard_map.223 = (f32[512,1536]{1,0:T(8,128)}, f32[512,256]{1,0:T(8,128)S(1)}, f32[512,256]{1,0:T(8,128)S(1)}) custom-call(f32[512,1792]{1,0:T(8,128)} %get-tuple-element.327.q_ref.c_ref, f32[512,128]{1,0:T(8,128)S(1)} %copy-done.42, f32[512,128]{1,0:T(8,128)S(1)} %copy-done.61, f32[512,128]{1,0:T(8,128)S(1)} %copy-done.36, ...), custom_call_target="tpu_custom_call" | custom-call | flops 3019898880 | bytes 15360000 | tf_op jit(solution)/shard_map/pallas_call | solution.py:645
  356.3 2.5 fusion.33
  358.9 5.3 %collective-permute-done.35 = bf16[144,768]{1,0:T(8,128)(2,1)S(1)} collective-permute-done((bf16[144,768]{1,0:T(8,128)(2,1)S(1)}, bf16[144,768]{1,0:T(8,128)(2,1)S(1)}, u32[]{:S(2)}, u32[]{:S(2)}) %collective-permute-start.35) | collective-permute-done | bytes 221216 | tf_op jit(solution)/shard_map/ppermute | solution.py:769
  368.6 15.1 %shard_map.224 = (bf16[512,1792]{1,0:T(8,128)(2,1)}, bf16[512,128]{1,0:T(8,128)(2,1)S(1)}, f32[8,1792]{1,0:T(8,128)S(1)}, f32[8,1792]{1,0:T(8,128)S(1)}, f32[8,1792]{1,0:T(8,128)S(1)}, /*index=5*/f32[8,128]{1,0:T(8,128)S(1)}) custom-call(bf16[128,1536]{1,0:T(8,128)(2,1)S(1)} %pad_maximum_fusion.28.outg_ref, f32[128,1536]{1,0:T(8,128)S(1)} %pad_maximum_fusion.17.inc_ref, ...), custom_call_target="tpu_custom_call" | custom-call | tf_op jit(solution)/shard_map/pallas_call | solution.py:693
  385.5 2.5 collective-permute-start.40
  392.7 7.0 %collective-permute-done.40 = bf16[608,384]{1,0:T(8,128)(2,1)S(1)} collective-permute-done((bf16[608,384]{1,0:T(8,128)(2,1)S(1)}, bf16[608,384]{1,0:T(8,128)(2,1)S(1)}, u32[]{:S(2)}, u32[]{:S(2)}) %collective-permute-start.40) | collective-permute-done | bytes 466976 | tf_op jit(solution)/shard_map/ppermute | solution.py:832
  413.3 2.8 collective-permute-start.52
  416.2 6.9 %collective-permute-done.45 = bf16[304,384]{1,0:T(8,128)(2,1)S(1)} collective-permute-done((bf16[304,384]{1,0:T(8,128)(2,1)S(1)}, bf16[304,384]{1,0:T(8,128)(2,1)S(1)}, u32[]{:S(2)}, u32[]{:S(2)}) %collective-permute-start.45) | collective-permute-done | bytes 233504 | tf_op jit(solution)/shard_map/ppermute | solution.py:832
  424.6 4.9 collective-permute-done.44
  434.3 7.7 %collective-permute-done.50 = f32[22,1792]{1,0:T(8,128)S(1)} collective-permute-done((f32[22,1792]{1,0:T(8,128)S(1)}, f32[22,1792]{1,0:T(8,128)S(1)}, u32[]{:S(2)}, u32[]{:S(2)}) %collective-permute-start.50) | collective-permute-done | bytes 157728 | tf_op jit(solution)/shard_map/ppermute | solution.py:862
  444.2 9.3 %collective-permute-done.48 = bf16[384,384]{1,0:T(8,128)(2,1)S(1)} collective-permute-done((bf16[384,384]{1,0:T(8,128)(2,1)S(1)}, bf16[384,384]{1,0:T(8,128)(2,1)S(1)}, u32[]{:S(2)}, u32[]{:S(2)}) %collective-permute-start.48) | collective-permute-done | bytes 294944 | tf_op jit(solution)/shard_map/ppermute | solution.py:832
  454.4 7.7 %collective-permute-done.49 = bf16[192,384]{1,0:T(8,128)(2,1)S(1)} collective-permute-done((bf16[192,384]{1,0:T(8,128)(2,1)S(1)}, bf16[192,384]{1,0:T(8,128)(2,1)S(1)}, u32[]{:S(2)}, u32[]{:S(2)}) %collective-permute-start.49) | collective-permute-done | bytes 147488 | tf_op jit(solution)/shard_map/ppermute | solution.py:832
  462.2 4.3 collective-permute-done.47
  476.7 5.5 %collective-permute-done.57 = bf16[192,384]{1,0:T(8,128)(2,1)S(1)} collective-permute-done((bf16[192,384]{1,0:T(8,128)(2,1)S(1)}, bf16[192,384]{1,0:T(8,128)(2,1)S(1)}, u32[]{:S(2)}, u32[]{:S(2)}) %collective-permute-start.57) | collective-permute-done | bytes 147488 | tf_op jit(solution)/shard_map/ppermute | solution.py:838
  484.9 5.1 collective-permute-done.60
  490.0 3.6 collective-permute-done.62
  500.1 2.8 collective-permute-done.65
  503.5 9.0 %collective-permute-done.63 = bf16[768,384]{1,0:T(8,128)(2,1)} collective-permute-done((bf16[768,384]{1,0:T(8,128)(2,1)}, bf16[768,384]{1,0:T(8,128)(2,1)}, u32[]{:S(2)}, u32[]{:S(2)}) %collective-permute-start.63) | collective-permute-done | bytes 589856 | tf_op jit(solution)/shard_map/ppermute | solution.py:838
  514.4 2.7 collective-permute-done.66
  521.0 3.7 shard_map.225
  (727 shorter events, 211.2 us)
Async XLA Ops:
  2.3 33.8 %collective-permute-start = (bf16[1824,384]{1,0:T(8,128)(2,1)S(1)}, bf16[1824,384]{1,0:T(8,128)(2,1)}, u32[]{:S(2)}, u32[]{:S(2)}) collective-permute-start(bf16[1824,384]{1,0:T(8,128)(2,1)S(1)} %pad.60), channel_id=1, source_target_pairs={{0,1},{1,0},{2,3},{3,2},{4,5},{5,4},{6,7},{7,6},{8,9},{9,8},{10,11... | collective-permute-start | bytes 4202504 | tf_op jit(solution)/shard_map/ppermute | solution.py:792
  7.5 13.2 %collective-permute-start.1 = (bf16[512,768]{1,0:T(8,128)(2,1)}, bf16[512,768]{1,0:T(8,128)(2,1)}, u32[]{:S(2)}, u32[]{:S(2)}) collective-permute-start(bf16[512,768]{1,0:T(8,128)(2,1)} %dynamic-slice_bitcast_fusion.3), channel_id=1, source_target_pairs={{0,2},{18,16},{4,6},{22,20},{8,10},{26,24},{12,14},{30,28},{1,3},{... | collective-permute-start | bytes 2359304 | tf_op jit(solution)/shard_map/ppermute | solution.py:951
  12.7 16.4 %collective-permute-start.2 = (bf16[512,768]{1,0:T(8,128)(2,1)}, bf16[512,768]{1,0:T(8,128)(2,1)}, u32[]{:S(2)}, u32[]{:S(2)}) collective-permute-start(bf16[512,768]{1,0:T(8,128)(2,1)} %dynamic-slice_bitcast_fusion.2), channel_id=1, source_target_pairs={{0,2},{18,16},{4,6},{22,20},{8,10},{26,24},{12,14},{30,28},{1,3},{... | collective-permute-start | bytes 2359304 | tf_op jit(solution)/shard_map/ppermute | solution.py:951
  15.8 22.3 %collective-permute-start.3 = (f32[16,1792]{1,0:T(8,128)}, f32[16,1792]{1,0:T(8,128)}, u32[]{:S(2)}, u32[]{:S(2)}) collective-permute-start(f32[16,1792]{1,0:T(8,128)} %pad.66), channel_id=1, source_target_pairs={{0,16},{16,0},{1,17},{17,1},{2,18},{18,2},{3,19},{19,3},{4,20},{20... | collective-permute-start | bytes 344072 | tf_op jit(solution)/shard_map/ppermute | solution.py:986
  39.1 53.6 %collective-permute-start.9 = (bf16[3072,384]{1,0:T(8,128)(2,1)}, bf16[3072,384]{1,0:T(8,128)(2,1)}, u32[]{:S(2)}, u32[]{:S(2)}) collective-permute-start(bf16[3072,384]{1,0:T(8,128)(2,1)} %pad_maximum_fusion.2), channel_id=1, source_target_pairs={{0,1},{1,0},{2,3},{3,2},{4,5},{5,4},{6,7},{7,6},{8,9},{9,8},{10,11... | collective-permute-start | bytes 7077896 | tf_op jit(solution)/shard_map/ppermute | solution.py:792
  62.0 13.7 %collective-permute-start.8 = (f32[136,768]{1,0:T(8,128)S(1)}, f32[136,768]{1,0:T(8,128)S(1)}, u32[]{:S(2)}, u32[]{:S(2)}) collective-permute-start(f32[136,768]{1,0:T(8,128)S(1)} %pad_maximum_fusion.23), channel_id=1, source_target_pairs={{0,4},{2,6},{4,8},{6,10},{8,12},{10,14},{1,5},{3,7},{5,9},{7,11},{... | collective-permute-start | bytes 1253384 | tf_op jit(solution)/shard_map/ppermute | solution.py:769
  92.7 7.9 %collective-permute-start.11 = (bf16[3072,384]{1,0:T(8,128)(2,1)S(1)}, bf16[3072,384]{1,0:T(8,128)(2,1)S(1)}, u32[]{:S(2)}, u32[]{:S(2)}) collective-permute-start(bf16[3072,384]{1,0:T(8,128)(2,1)S(1)} %copy-done.99), channel_id=1, source_target_pairs={{0,16},{16,0},{1,17},{17,1},{2,18},{18,2},{3,19},{19,3},{4,20},{20... | collective-permute-start | bytes 7077896 | tf_op jit(solution)/shard_map/ppermute | solution.py:799
  92.7 8.1 %collective-permute-start.12 = (bf16[3072,384]{1,0:T(8,128)(2,1)}, bf16[3072,384]{1,0:T(8,128)(2,1)S(1)}, u32[]{:S(2)}, u32[]{:S(2)}) collective-permute-start(bf16[3072,384]{1,0:T(8,128)(2,1)} %collective-permute-done.9), channel_id=1, source_target_pairs={{0,16},{16,0},{1,17},{17,1},{2,18},{18,2},{3,19},{19,3},{4,20},{20... | collective-permute-start | bytes 7077896 | tf_op jit(solution)/shard_map/ppermute | solution.py:799
  93.3 13.8 %collective-permute-start.10 = (f32[136,768]{1,0:T(8,128)S(1)}, f32[136,768]{1,0:T(8,128)S(1)}, u32[]{:S(2)}, u32[]{:S(2)}) collective-permute-start(f32[136,768]{1,0:T(8,128)S(1)} %pad_maximum_fusion.24), channel_id=1, source_target_pairs={{0,8},{2,10},{4,12},{6,14},{1,9},{3,11},{5,13},{7,15},{16,24},{18,... | collective-permute-start | bytes 1253384 | tf_op jit(solution)/shard_map/ppermute | solution.py:769
  130.9 11.7 %collective-permute-start.15 = (f32[136,768]{1,0:T(8,128)S(1)}, f32[136,768]{1,0:T(8,128)S(1)}, u32[]{:S(2)}, u32[]{:S(2)}) collective-permute-start(f32[136,768]{1,0:T(8,128)S(1)} %get-tuple-element.240.given_ref), channel_id=1, source_target_pairs={{0,16},{16,0},{1,17},{17,1},{2,18},{18,2},{3,19},{19,3},{4,20},{20... | collective-permute-start | bytes 1253384 | tf_op jit(solution)/shard_map/ppermute | solution.py:752
  143.8 15.8 %collective-permute-start.16 = (f32[136,768]{1,0:T(8,128)}, f32[136,768]{1,0:T(8,128)}, u32[]{:S(2)}, u32[]{:S(2)}) collective-permute-start(f32[136,768]{1,0:T(8,128)} %pad_maximum_fusion.25), channel_id=1, source_target_pairs={{0,4},{2,6},{4,8},{6,10},{8,12},{10,14},{1,5},{3,7},{5,9},{7,11},{... | collective-permute-start | bytes 1253384 | tf_op jit(solution)/shard_map/ppermute | solution.py:769
  161.8 13.5 %collective-permute-start.17 = (f32[136,768]{1,0:T(8,128)S(1)}, f32[136,768]{1,0:T(8,128)S(1)}, u32[]{:S(2)}, u32[]{:S(2)}) collective-permute-start(f32[136,768]{1,0:T(8,128)S(1)} %pad_maximum_fusion.26), channel_id=1, source_target_pairs={{0,8},{2,10},{4,12},{6,14},{1,9},{3,11},{5,13},{7,15},{16,24},{18,... | collective-permute-start | bytes 1253384 | tf_op jit(solution)/shard_map/ppermute | solution.py:769
  196.8 22.8 %collective-permute-start.21 = (bf16[2,1536,384]{2,1,0:T(8,128)(2,1)}, bf16[2,1536,384]{2,1,0:T(8,128)(2,1)}, u32[]{:S(2)}, u32[]{:S(2)}) collective-permute-start(bf16[2,1536,384]{2,1,0:T(8,128)(2,1)} %pad_maximum_fusion.5), channel_id=1, source_target_pairs={{0,16},{16,0},{1,17},{17,1},{2,18},{18,2},{3,19},{19,3},{4,20},{20... | collective-permute-start | bytes 7077896 | tf_op jit(solution)/shard_map/ppermute | solution.py:1101
  197.1 22.6 %collective-permute-start.20 = (bf16[144,768]{1,0:T(8,128)(2,1)}, bf16[144,768]{1,0:T(8,128)(2,1)S(1)}, u32[]{:S(2)}, u32[]{:S(2)}) collective-permute-start(bf16[144,768]{1,0:T(8,128)(2,1)} %pad_maximum_fusion.31), channel_id=1, source_target_pairs={{4,0},{6,2},{8,4},{10,6},{12,8},{14,10},{5,1},{7,3},{9,5},{11,7},{... | collective-permute-start | bytes 663560 | tf_op jit(solution)/shard_map/ppermute | solution.py:769
  220.0 23.5 %collective-permute-start.22 = (bf16[144,768]{1,0:T(8,128)(2,1)S(1)}, bf16[144,768]{1,0:T(8,128)(2,1)S(1)}, u32[]{:S(2)}, u32[]{:S(2)}) collective-permute-start(bf16[144,768]{1,0:T(8,128)(2,1)S(1)} %pad_maximum_fusion.32), channel_id=1, source_target_pairs={{8,0},{10,2},{12,4},{14,6},{9,1},{11,3},{13,5},{15,7},{24,16},{26,... | collective-permute-start | bytes 663560 | tf_op jit(solution)/shard_map/ppermute | solution.py:769
  247.2 27.7 %collective-permute-start.24 = (bf16[1536,384]{1,0:T(8,128)(2,1)}, bf16[1536,384]{1,0:T(8,128)(2,1)}, u32[]{:S(2)}, u32[]{:S(2)}) collective-permute-start(bf16[1536,384]{1,0:T(8,128)(2,1)} %dynamic-slice_bitcast_fusion.1), channel_id=1, source_target_pairs={{0,1},{1,0},{2,3},{3,2},{4,5},{5,4},{6,7},{7,6},{8,9},{9,8},{10,11... | collective-permute-start | bytes 3538952 | tf_op jit(solution)/shard_map/ppermute | solution.py:822
  288.5 28.6 %collective-permute-start.28 = (bf16[512,768]{1,0:T(8,128)(2,1)S(1)}, bf16[512,768]{1,0:T(8,128)(2,1)S(1)}, u32[]{:S(2)}, u32[]{:S(2)}) collective-permute-start(bf16[512,768]{1,0:T(8,128)(2,1)S(1)} %get-tuple-element.489), channel_id=1, source_target_pairs={{0,0},{2,16},{16,2},{18,18},{4,4},{6,20},{20,6},{22,22},{8,8},{10,... | collective-permute-start | bytes 2359304 | tf_op jit(solution)/shard_map/ppermute | solution.py:1009
  289.4 27.7 %collective-permute-start.29 = (bf16[512,768]{1,0:T(8,128)(2,1)S(1)}, bf16[512,768]{1,0:T(8,128)(2,1)S(1)}, u32[]{:S(2)}, u32[]{:S(2)}) collective-permute-start(bf16[512,768]{1,0:T(8,128)(2,1)S(1)} %get-tuple-element.488), channel_id=1, source_target_pairs={{0,16},{2,0},{16,18},{18,2},{4,20},{6,4},{20,22},{22,6},{8,24},{10... | collective-permute-start | bytes 2359304 | tf_op jit(solution)/shard_map/ppermute | solution.py:1010
  298.5 17.4 %collective-permute-start.27 = (bf16[896,384]{1,0:T(8,128)(2,1)S(1)}, bf16[896,384]{1,0:T(8,128)(2,1)S(1)}, u32[]{:S(2)}, u32[]{:S(2)}) collective-permute-start(bf16[896,384]{1,0:T(8,128)(2,1)S(1)} %dynamic-slice_bitcast_fusion.5), channel_id=1, source_target_pairs={{0,1},{1,0},{2,3},{3,2},{4,5},{5,4},{6,7},{7,6},{8,9},{9,8},{10,11... | collective-permute-start | bytes 2064392 | tf_op jit(solution)/shard_map/ppermute | solution.py:822
  320.7 28.7 %collective-permute-start.34 = (bf16[2,1536,384]{2,1,0:T(8,128)(2,1)}, bf16[2,1536,384]{2,1,0:T(8,128)(2,1)}, u32[]{:S(2)}, u32[]{:S(2)}) collective-permute-start(bf16[2,1536,384]{2,1,0:T(8,128)(2,1)} %pad_maximum_fusion.6), channel_id=1, source_target_pairs={{0,16},{16,0},{1,17},{17,1},{2,18},{18,2},{3,19},{19,3},{4,20},{20... | collective-permute-start | bytes 7077896 | tf_op jit(solution)/shard_map/ppermute | solution.py:1101
  324.8 23.7 %collective-permute-start.32 = (bf16[768,384]{1,0:T(8,128)(2,1)S(1)}, bf16[768,384]{1,0:T(8,128)(2,1)S(1)}, u32[]{:S(2)}, u32[]{:S(2)}) collective-permute-start(bf16[768,384]{1,0:T(8,128)(2,1)S(1)} %dynamic-slice_bitcast_fusion.7), channel_id=1, source_target_pairs={{0,2},{2,0},{4,6},{6,4},{8,10},{10,8},{12,14},{14,12},{1,3},{3,1},... | collective-permute-start | bytes 1769480 | tf_op jit(solution)/shard_map/ppermute | solution.py:832
  326.5 21.2 %collective-permute-start.33 = (bf16[448,384]{1,0:T(8,128)(2,1)S(1)}, bf16[448,384]{1,0:T(8,128)(2,1)S(1)}, u32[]{:S(2)}, u32[]{:S(2)}) collective-permute-start(bf16[448,384]{1,0:T(8,128)(2,1)S(1)} %dynamic-slice_bitcast_fusion.10), channel_id=1, source_target_pairs={{0,2},{2,0},{4,6},{6,4},{8,10},{10,8},{12,14},{14,12},{1,3},{3,1},... | collective-permute-start | bytes 1032200 | tf_op jit(solution)/shard_map/ppermute | solution.py:832
  329.3 20.2 %collective-permute-start.31 = (bf16[144,768]{1,0:T(8,128)(2,1)S(1)}, bf16[144,768]{1,0:T(8,128)(2,1)S(1)}, u32[]{:S(2)}, u32[]{:S(2)}) collective-permute-start(bf16[144,768]{1,0:T(8,128)(2,1)S(1)} %copy-done.163), channel_id=1, source_target_pairs={{4,0},{6,2},{8,4},{10,6},{12,8},{14,10},{5,1},{7,3},{9,5},{11,7},{... | collective-permute-start | bytes 663560 | tf_op jit(solution)/shard_map/ppermute | solution.py:769
  349.8 14.4 %collective-permute-start.35 = (bf16[144,768]{1,0:T(8,128)(2,1)S(1)}, bf16[144,768]{1,0:T(8,128)(2,1)S(1)}, u32[]{:S(2)}, u32[]{:S(2)}) collective-permute-start(bf16[144,768]{1,0:T(8,128)(2,1)S(1)} %pad_maximum_fusion.34), channel_id=1, source_target_pairs={{8,0},{10,2},{12,4},{14,6},{9,1},{11,3},{13,5},{15,7},{24,16},{26,... | collective-permute-start | bytes 663560 | tf_op jit(solution)/shard_map/ppermute | solution.py:769
  366.7 33.1 %collective-permute-start.39 = (bf16[1536,384]{1,0:T(8,128)(2,1)S(1)}, bf16[1536,384]{1,0:T(8,128)(2,1)}, u32[]{:S(2)}, u32[]{:S(2)}) collective-permute-start(bf16[1536,384]{1,0:T(8,128)(2,1)S(1)} %dynamic-slice_bitcast_fusion), channel_id=1, source_target_pairs={{0,1},{1,0},{2,3},{3,2},{4,5},{5,4},{6,7},{7,6},{8,9},{9,8},{10,11... | collective-permute-start | bytes 3538952 | tf_op jit(solution)/shard_map/ppermute | solution.py:822
  385.5 14.2 %collective-permute-start.40 = (bf16[608,384]{1,0:T(8,128)(2,1)S(1)}, bf16[608,384]{1,0:T(8,128)(2,1)S(1)}, u32[]{:S(2)}, u32[]{:S(2)}) collective-permute-start(bf16[608,384]{1,0:T(8,128)(2,1)S(1)} %dynamic-slice_bitcast_fusion.8), channel_id=1, source_target_pairs={{0,4},{2,6},{4,0},{6,2},{8,12},{10,14},{12,8},{14,10},{1,5},{3,7},... | collective-permute-start | bytes 1400840 | tf_op jit(solution)/shard_map/ppermute | solution.py:832
  389.3 12.2 %collective-permute-start.38 = (bf16[2,896,384]{2,1,0:T(8,128)(2,1)S(1)}, bf16[2,896,384]{2,1,0:T(8,128)(2,1)S(1)}, u32[]{:S(2)}, u32[]{:S(2)}) collective-permute-start(bf16[2,896,384]{2,1,0:T(8,128)(2,1)S(1)} %pad_maximum_fusion.12), channel_id=1, source_target_pairs={{0,16},{16,0},{1,17},{17,1},{2,18},{18,2},{3,19},{19,3},{4,20},{20... | collective-permute-start | bytes 4128776 | tf_op jit(solution)/shard_map/ppermute | solution.py:1135
  402.9 27.9 %collective-permute-start.41 = (bf16[896,384]{1,0:T(8,128)(2,1)}, bf16[896,384]{1,0:T(8,128)(2,1)}, u32[]{:S(2)}, u32[]{:S(2)}) collective-permute-start(bf16[896,384]{1,0:T(8,128)(2,1)} %dynamic-slice_bitcast_fusion.4), channel_id=1, source_target_pairs={{0,1},{1,0},{2,3},{3,2},{4,5},{5,4},{6,7},{7,6},{8,9},{9,8},{10,11... | collective-permute-start | bytes 2064392 | tf_op jit(solution)/shard_map/ppermute | solution.py:822
  404.6 24.9 %collective-permute-start.42 = (bf16[768,384]{1,0:T(8,128)(2,1)}, bf16[768,384]{1,0:T(8,128)(2,1)}, u32[]{:S(2)}, u32[]{:S(2)}) collective-permute-start(bf16[768,384]{1,0:T(8,128)(2,1)} %dynamic-slice_bitcast_fusion.6), channel_id=1, source_target_pairs={{0,2},{2,0},{4,6},{6,4},{8,10},{10,8},{12,14},{14,12},{1,3},{3,1},... | collective-permute-start | bytes 1769480 | tf_op jit(solution)/shard_map/ppermute | solution.py:832
  410.0 13.1 %collective-permute-start.45 = (bf16[304,384]{1,0:T(8,128)(2,1)S(1)}, bf16[304,384]{1,0:T(8,128)(2,1)S(1)}, u32[]{:S(2)}, u32[]{:S(2)}) collective-permute-start(bf16[304,384]{1,0:T(8,128)(2,1)S(1)} %dynamic-slice_bitcast_fusion.12), channel_id=1, source_target_pairs={{0,8},{2,10},{4,12},{6,14},{8,0},{10,2},{12,4},{14,6},{1,9},{3,11}... | collective-permute-start | bytes 700424 | tf_op jit(solution)/shard_map/ppermute | solution.py:832
  412.2 54.7 %collective-permute-start.51 = (bf16[512,768]{1,0:T(8,128)(2,1)S(1)}, bf16[512,768]{1,0:T(8,128)(2,1)S(1)}, u32[]{:S(2)}, u32[]{:S(2)}) collective-permute-start(bf16[512,768]{1,0:T(8,128)(2,1)S(1)} %get-tuple-element.465), channel_id=1, source_target_pairs={{0,0},{2,16},{16,2},{18,18},{4,4},{6,20},{20,6},{22,22},{8,8},{10,... | collective-permute-start | bytes 2359304 | tf_op jit(solution)/shard_map/ppermute | solution.py:1009
  413.3 53.6 %collective-permute-start.52 = (bf16[512,768]{1,0:T(8,128)(2,1)S(1)}, bf16[512,768]{1,0:T(8,128)(2,1)S(1)}, u32[]{:S(2)}, u32[]{:S(2)}) collective-permute-start(bf16[512,768]{1,0:T(8,128)(2,1)S(1)} %get-tuple-element.464), channel_id=1, source_target_pairs={{0,16},{2,0},{16,18},{18,2},{4,20},{6,4},{20,22},{22,6},{8,24},{10... | collective-permute-start | bytes 2359304 | tf_op jit(solution)/shard_map/ppermute | solution.py:1010
  432.0 9.9 %collective-permute-start.50 = (f32[22,1792]{1,0:T(8,128)S(1)}, f32[22,1792]{1,0:T(8,128)S(1)}, u32[]{:S(2)}, u32[]{:S(2)}) collective-permute-start(f32[22,1792]{1,0:T(8,128)S(1)} %add.434), channel_id=1, source_target_pairs={{0,2},{2,0},{4,6},{6,4},{8,10},{10,8},{12,14},{14,12},{1,3},{3,1},... | collective-permute-start | bytes 473096 | tf_op jit(solution)/shard_map/ppermute | solution.py:862
  433.6 9.8 %collective-permute-start.53 = (bf16[304,384]{1,0:T(8,128)(2,1)S(1)}, bf16[304,384]{1,0:T(8,128)(2,1)S(1)}, u32[]{:S(2)}, u32[]{:S(2)}) collective-permute-start(bf16[304,384]{1,0:T(8,128)(2,1)S(1)} %fusion.55), channel_id=1, source_target_pairs={{0,8},{2,10},{4,12},{6,14},{8,0},{10,2},{12,4},{14,6},{1,9},{3,11}... | collective-permute-start | bytes 700424 | tf_op jit(solution)/shard_map/ppermute | solution.py:838
  433.7 20.5 %collective-permute-start.46 = (bf16[448,384]{1,0:T(8,128)(2,1)S(1)}, bf16[448,384]{1,0:T(8,128)(2,1)S(1)}, u32[]{:S(2)}, u32[]{:S(2)}) collective-permute-start(bf16[448,384]{1,0:T(8,128)(2,1)S(1)} %dynamic-slice_bitcast_fusion.9), channel_id=1, source_target_pairs={{0,2},{2,0},{4,6},{6,4},{8,10},{10,8},{12,14},{14,12},{1,3},{3,1},... | collective-permute-start | bytes 1032200 | tf_op jit(solution)/shard_map/ppermute | solution.py:832
  441.9 11.5 %collective-permute-start.48 = (bf16[384,384]{1,0:T(8,128)(2,1)S(1)}, bf16[384,384]{1,0:T(8,128)(2,1)S(1)}, u32[]{:S(2)}, u32[]{:S(2)}) collective-permute-start(bf16[384,384]{1,0:T(8,128)(2,1)S(1)} %dynamic-slice_bitcast_fusion.11), channel_id=1, source_target_pairs={{0,4},{2,6},{4,0},{6,2},{8,12},{10,14},{12,8},{14,10},{1,5},{3,7},... | collective-permute-start | bytes 884744 | tf_op jit(solution)/shard_map/ppermute | solution.py:832
  443.6 23.0 %collective-permute-start.54 = (bf16[608,384]{1,0:T(8,128)(2,1)S(1)}, bf16[608,384]{1,0:T(8,128)(2,1)S(1)}, u32[]{:S(2)}, u32[]{:S(2)}) collective-permute-start(bf16[608,384]{1,0:T(8,128)(2,1)S(1)} %pad_maximum_fusion.22), channel_id=1, source_target_pairs={{0,4},{2,6},{4,0},{6,2},{8,12},{10,14},{12,8},{14,10},{1,5},{3,7},... | collective-permute-start | bytes 1400840 | tf_op jit(solution)/shard_map/ppermute | solution.py:838
  453.6 8.6 %collective-permute-start.49 = (bf16[192,384]{1,0:T(8,128)(2,1)S(1)}, bf16[192,384]{1,0:T(8,128)(2,1)S(1)}, u32[]{:S(2)}, u32[]{:S(2)}) collective-permute-start(bf16[192,384]{1,0:T(8,128)(2,1)S(1)} %dynamic-slice_bitcast_fusion.14), channel_id=1, source_target_pairs={{0,8},{2,10},{4,12},{6,14},{8,0},{10,2},{12,4},{14,6},{1,9},{3,11}... | collective-permute-start | bytes 442376 | tf_op jit(solution)/shard_map/ppermute | solution.py:832
  454.3 12.2 %collective-permute-start.47 = (bf16[224,384]{1,0:T(8,128)(2,1)S(1)}, bf16[224,384]{1,0:T(8,128)(2,1)S(1)}, u32[]{:S(2)}, u32[]{:S(2)}) collective-permute-start(bf16[224,384]{1,0:T(8,128)(2,1)S(1)} %dynamic-slice_bitcast_fusion.13), channel_id=1, source_target_pairs={{0,4},{2,6},{4,0},{6,2},{8,12},{10,14},{12,8},{14,10},{1,5},{3,7},... | collective-permute-start | bytes 516104 | tf_op jit(solution)/shard_map/ppermute | solution.py:832
  466.9 8.7 %collective-permute-start.55 = (bf16[112,384]{1,0:T(8,128)(2,1)S(1)}, bf16[112,384]{1,0:T(8,128)(2,1)S(1)}, u32[]{:S(2)}, u32[]{:S(2)}) collective-permute-start(bf16[112,384]{1,0:T(8,128)(2,1)S(1)} %dynamic-slice_bitcast_fusion.15), channel_id=1, source_target_pairs={{0,8},{2,10},{4,12},{6,14},{8,0},{10,2},{12,4},{14,6},{1,9},{3,11}... | collective-permute-start | bytes 258056 | tf_op jit(solution)/shard_map/ppermute | solution.py:832
  469.3 12.9 %collective-permute-start.57 = (bf16[192,384]{1,0:T(8,128)(2,1)S(1)}, bf16[192,384]{1,0:T(8,128)(2,1)S(1)}, u32[]{:S(2)}, u32[]{:S(2)}) collective-permute-start(bf16[192,384]{1,0:T(8,128)(2,1)S(1)} %fusion.71), channel_id=1, source_target_pairs={{0,8},{2,10},{4,12},{6,14},{8,0},{10,2},{12,4},{14,6},{1,9},{3,11}... | collective-permute-start | bytes 442376 | tf_op jit(solution)/shard_map/ppermute | solution.py:838
  471.4 11.0 %collective-permute-start.59 = (f32[22,1792]{1,0:T(8,128)S(1)}, f32[22,1792]{1,0:T(8,128)S(1)}, u32[]{:S(2)}, u32[]{:S(2)}) collective-permute-start(f32[22,1792]{1,0:T(8,128)S(1)} %add.443), channel_id=1, source_target_pairs={{0,4},{2,6},{4,0},{6,2},{8,12},{10,14},{12,8},{14,10},{1,5},{3,7},... | collective-permute-start | bytes 473096 | tf_op jit(solution)/shard_map/ppermute | solution.py:862
  472.6 23.0 %collective-permute-start.61 = (bf16[768,384]{1,0:T(8,128)(2,1)S(1)}, bf16[768,384]{1,0:T(8,128)(2,1)S(1)}, u32[]{:S(2)}, u32[]{:S(2)}) collective-permute-start(bf16[768,384]{1,0:T(8,128)(2,1)S(1)} %slice.368), channel_id=1, source_target_pairs={{0,2},{2,0},{4,6},{6,4},{8,10},{10,8},{12,14},{14,12},{1,3},{3,1},... | collective-permute-start | bytes 1769480 | tf_op jit(solution)/shard_map/ppermute | solution.py:838
  473.1 20.5 %collective-permute-start.62 = (bf16[448,384]{1,0:T(8,128)(2,1)S(1)}, bf16[448,384]{1,0:T(8,128)(2,1)S(1)}, u32[]{:S(2)}, u32[]{:S(2)}) collective-permute-start(bf16[448,384]{1,0:T(8,128)(2,1)S(1)} %slice.369), channel_id=1, source_target_pairs={{0,2},{2,0},{4,6},{6,4},{8,10},{10,8},{12,14},{14,12},{1,3},{3,1},... | collective-permute-start | bytes 1032200 | tf_op jit(solution)/shard_map/ppermute | solution.py:838
  475.7 9.2 %collective-permute-start.56 = (bf16[112,384]{1,0:T(8,128)(2,1)S(1)}, bf16[112,384]{1,0:T(8,128)(2,1)S(1)}, u32[]{:S(2)}, u32[]{:S(2)}) collective-permute-start(bf16[112,384]{1,0:T(8,128)(2,1)S(1)} %fusion.74), channel_id=1, source_target_pairs={{0,8},{2,10},{4,12},{6,14},{8,0},{10,2},{12,4},{14,6},{1,9},{3,11}... | collective-permute-start | bytes 258056 | tf_op jit(solution)/shard_map/ppermute | solution.py:838
  482.4 12.3 %collective-permute-start.58 = (bf16[384,384]{1,0:T(8,128)(2,1)S(1)}, bf16[384,384]{1,0:T(8,128)(2,1)S(1)}, u32[]{:S(2)}, u32[]{:S(2)}) collective-permute-start(bf16[384,384]{1,0:T(8,128)(2,1)S(1)} %pad_maximum_fusion.30), channel_id=1, source_target_pairs={{0,4},{2,6},{4,0},{6,2},{8,12},{10,14},{12,8},{14,10},{1,5},{3,7},... | collective-permute-start | bytes 884744 | tf_op jit(solution)/shard_map/ppermute | solution.py:838
  495.9 16.6 %collective-permute-start.63 = (bf16[768,384]{1,0:T(8,128)(2,1)}, bf16[768,384]{1,0:T(8,128)(2,1)}, u32[]{:S(2)}, u32[]{:S(2)}) collective-permute-start(bf16[768,384]{1,0:T(8,128)(2,1)} %pad_maximum_fusion.21), channel_id=1, source_target_pairs={{0,2},{2,0},{4,6},{6,4},{8,10},{10,8},{12,14},{14,12},{1,3},{3,1},... | collective-permute-start | bytes 1769480 | tf_op jit(solution)/shard_map/ppermute | solution.py:838
  503.0 14.1 %collective-permute-start.66 = (bf16[448,384]{1,0:T(8,128)(2,1)S(1)}, bf16[448,384]{1,0:T(8,128)(2,1)S(1)}, u32[]{:S(2)}, u32[]{:S(2)}) collective-permute-start(bf16[448,384]{1,0:T(8,128)(2,1)S(1)} %pad_maximum_fusion.29), channel_id=1, source_target_pairs={{0,2},{2,0},{4,6},{6,4},{8,10},{10,8},{12,14},{14,12},{1,3},{3,1},... | collective-permute-start | bytes 1032200 | tf_op jit(solution)/shard_map/ppermute | solution.py:838
  (214 other events, 1508.9 us)
